TPU v7x, 32 devices: a whole 2x2x4 slice. The times are simulated.
32 devices in a mesh: orbit: 8 (over z, y), space: 4 (over x, core).
Axes of the slice: x: 2, y: 2, z: 4, core: 2. Of those that a mesh axis runs over, the one named last changes fastest.
Arguments:
- latents: bfloat16 [32, 4, 16, 1024], P('orbit', 'space'), may hold values from -6 to 6
- conv_gain: float32 [1024], replicated, may hold values from 0.1 to 1.9
- spatial_weight: bfloat16 [3, 3, 1024, 1024], P(None, None, 'space'), may hold values from -0.0625 to 0.0625
- temporal_weight: bfloat16 [3, 1024, 1024], P(None, 'space'), may hold values from -0.109375 to 0.109375
- attn_gain: float32 [1024], replicated, may hold values from 0.1 to 1.9
- qkv_weight: bfloat16 [3, 1024, 1024], P(None, 'space'), may hold values from -0.1875 to 0.1875
- out_weight: bfloat16 [1024, 1024], P('space'), may hold values from -0.1875 to 0.1875
Outputs:
- restored: bfloat16 [32, 4, 16, 1024], P('orbit', 'space')
All inputs are finite; a program needn't handle non-finite values.
Results may differ from a plain program's by a relative error of at most 0.029.
Values may be sent and summed in bfloat16 or wider, within the bound.
No kernel may reach another device: no remote copies, remote signals or barrier semaphores. Data moves between devices by JAX's collectives and lax.ppermute only.
A program may use at most 64 MiB of HBM per device.

v0:
```python
import jax
import jax.numpy as jnp
from jax import lax
from jax.sharding import PartitionSpec as P

HD = 64


def from_behind(block, axis, distance):
    devices = range(lax.axis_size(axis))
    route = [((i - distance) % len(devices), i) for i in devices]
    return lax.ppermute(block, axis, route)


def rms_scale(values, gain):
    wide = values.astype(jnp.float32)
    return wide * lax.rsqrt(jnp.mean(wide * wide, axis=-1, keepdims=True) + 1e-06) * gain


def dot_trans(left, right):
    return lax.dot_general(
        left, right, (((1,), (1,)), ((), ())), preferred_element_type=jnp.float32
    )


def body(latents, conv_gain, spatial_weight, temporal_weight, attn_gain, qkv_weight, out_weight):
    views, own_rows, cols, chans = latents.shape
    gathered = lax.all_gather(latents, "space", axis=1, tiled=True)
    rows = gathered.shape[1]
    normed = rms_scale(gathered, conv_gain).astype(jnp.bfloat16)
    padded = jnp.pad(normed, ((0, 0), (1, 1), (1, 1), (0, 0)))
    slice_chans = spatial_weight.shape[2]
    total = jnp.zeros((views * rows * cols, slice_chans), jnp.float32)
    for i in range(3):
        for j in range(3):
            window = padded[:, i : i + rows, j : j + cols, :].reshape(-1, chans)
            total = total + dot_trans(window, spatial_weight[i, j])
    activated = jax.nn.silu(total).astype(jnp.bfloat16).reshape(views, rows, cols, slice_chans)
    edge = from_behind(activated[views - 1 :], "orbit", 1)
    previous = jnp.concatenate([edge, activated[: views - 1]], axis=0)
    before = previous[0::2].reshape(-1, slice_chans)
    even = activated[0::2].reshape(-1, slice_chans)
    odd = activated[1::2].reshape(-1, slice_chans)
    partial_value = jnp.dot(before, temporal_weight[0], preferred_element_type=jnp.float32)
    partial_value = partial_value + jnp.dot(
        even, temporal_weight[1], preferred_element_type=jnp.float32
    )
    partial_value = partial_value + jnp.dot(
        odd, temporal_weight[2], preferred_element_type=jnp.float32
    )
    half = views // 2
    partial_value = partial_value.reshape(half, rows, cols, chans)
    summed = lax.psum(partial_value.astype(jnp.bfloat16), "space")
    down_normed = rms_scale(summed, attn_gain).astype(jnp.bfloat16)
    start = lax.axis_index("space") * own_rows
    down_own = lax.dynamic_slice_in_dim(summed, start, own_rows, 1)
    flat = down_normed.reshape(-1, chans)
    head_count = slice_chans // HD
    shape5 = (half, rows, cols, head_count, HD)
    query = dot_trans(flat, qkv_weight[0]).astype(jnp.bfloat16).reshape(shape5)
    key_local = dot_trans(flat, qkv_weight[1]).astype(jnp.bfloat16).reshape(shape5)
    value_local = dot_trans(flat, qkv_weight[2]).astype(jnp.bfloat16).reshape(shape5)
    keys, values_all = (
        lax.all_gather(key_local, "orbit", axis=0, tiled=True),
        lax.all_gather(value_local, "orbit", axis=0, tiled=True),
    )
    scores = jnp.einsum(
        "thwnd,shwnd->hwnts", query, keys, preferred_element_type=jnp.float32
    ) / jnp.sqrt(jnp.float32(HD))
    probs = jax.nn.softmax(scores, axis=-1).astype(jnp.bfloat16)
    mixed = jnp.einsum(
        "hwnts,shwnd->thwnd", probs, values_all, preferred_element_type=jnp.float32
    ).astype(jnp.bfloat16)
    mixed = mixed.reshape(half, rows, cols, slice_chans)
    projected = jnp.dot(
        mixed.reshape(-1, slice_chans), out_weight, preferred_element_type=jnp.float32
    )
    projected = projected.reshape(half, rows, cols, chans)
    own_projected = lax.psum_scatter(
        projected.astype(jnp.bfloat16), "space", scatter_dimension=1, tiled=True
    ).astype(jnp.float32)
    bottom = (down_own.astype(jnp.float32) + own_projected).astype(jnp.bfloat16)
    grown = jnp.repeat(bottom, 2, axis=0)
    return (latents.astype(jnp.float32) + grown.astype(jnp.float32)).astype(jnp.bfloat16)


def solution(mesh):
    return jax.shard_map(
        body,
        mesh=mesh,
        in_specs=(
            P("orbit", "space", None, None),
            P(),
            P(None, None, "space", None),
            P(None, "space", None),
            P(),
            P(None, "space", None),
            P("space", None),
        ),
        out_specs=P("orbit", "space", None, None),
        check_vma=False,
    )
```

profile of v0, /device:TPU:0, one launch (start us, length us, event | category | flops | bytes accessed | tf_op | source)
XLA Modules:
  0.0 174.2 jit_solution(10860628888122835507)
XLA Ops:
  6.5 0.0 all-reduce.5.cloned.1.call-start
  6.5 8.9 %all_gather.9 = bf16[4,4,16,1024]{3,2,1,0:T(8,128)(2,1)S(1)} all-gather(bf16[4,1,16,1024]{3,2,1,0:T(8,128)(2,1)} %param.7), channel_id=1, replica_groups=mesh['orbit'=8,'space'=4] {'space'}, dimensions={1}, use_global_device_ids=true | all-gather | bytes 655360 | tf_op jit(solution)/shard_map/all_gather | solution.py:28
  15.5 0.2 fusion.5
  15.7 0.9 fusion.7
  16.6 0.0 copy-start.1
  16.6 0.6 pad_slice_fusion
  17.2 1.7 copy-done.1
  18.9 0.3 fusion.29
  19.3 0.3 convolution_add_fusion.9
  19.6 0.3 convolution_add_fusion.8
  20.0 0.3 convolution_add_fusion.7
  20.3 0.3 convolution_add_fusion.6
  20.6 0.3 convolution_add_fusion.5
  21.0 0.3 convolution_add_fusion.4
  21.3 0.3 convolution_add_fusion.3
  21.7 0.0 copy-start.2
  21.7 0.4 multiply_convert_fusion
  22.1 1.6 collective-permute-start
  23.7 0.2 fusion.18
  23.9 4.8 %collective-permute-done = bf16[1,4,16,256]{3,2,1,0:T(8,128)(2,1)S(1)} collective-permute-done((bf16[1,4,16,256]{3,2,1,0:T(8,128)(2,1)S(1)}, bf16[1,4,16,256]{3,2,1,0:T(8,128)(2,1)S(1)}, u32[]{:S(2)}, u32[]{:S(2)}) %collective-permute-start) | collective-permute-done | bytes 32800 | tf_op jit(solution)/shard_map/ppermute | solution.py:12
  28.8 0.0 copy-start.4
  28.8 0.2 convolution_add_fusion.1
  29.0 0.0 copy-start.5
  29.0 0.9 fusion.2
  30.0 0.0 all-reduce.5.cloned.1.call-update
  30.0 0.0 all-reduce.7.cloned.1.call-start
  30.1 30.2 %all-reduce.5.cloned.1.call-done = bf16[2,4,16,1024]{3,2,1,0:T(8,128)(2,1)} async-done(((bf16[2,4,16,1024]{3,2,1,0:T(8,128)(2,1)}), bf16[2,4,16,1024]{3,2,1,0:T(8,128)(2,1)}) %all-reduce.5.cloned.1.call-update) | async-done | bytes 262160 | tf_op jit(solution)/shard_map/psum | solution.py:53
  60.3 1.1 fusion.10
  61.4 0.0 copy-done.4
  61.4 1.1 fusion.12
  62.5 0.3 convolution_convert_fusion.2
  62.8 0.3 convolution_convert_fusion.3
  63.1 0.3 convolution_convert_fusion.4
  63.4 0.1 reshape.114
  63.6 33.7 %all_gather.11 = bf16[16,4,16,4,64]{4,2,3,1,0:T(8,128)(2,1)S(1)} all-gather(bf16[2,4,16,4,64]{4,2,3,1,0:T(8,128)(2,1)S(1)} %copy.16), channel_id=1, replica_groups=mesh['orbit'=8,'space'=4] {'orbit'}, dimensions={0}, use_global_device_ids=true | all-gather | bytes 589824 | tf_op jit(solution)/shard_map/all_gather | solution.py:64
  97.3 0.1 reshape.113
  97.4 0.1 reshape.112
  97.6 32.1 %all_gather.10 = bf16[16,4,16,4,64]{4,2,3,1,0:T(8,128)(2,1)S(1)} all-gather(bf16[2,4,16,4,64]{4,2,3,1,0:T(8,128)(2,1)S(1)} %copy.15), channel_id=1, replica_groups=mesh['orbit'=8,'space'=4] {'orbit'}, dimensions={0}, use_global_device_ids=true | all-gather | bytes 589824 | tf_op jit(solution)/shard_map/all_gather | solution.py:65
  129.6 1.2 fusion.53
  130.9 0.9 fusion.4
  131.7 0.0 copy-start.3
  131.8 0.1 dot_general.73
  132.0 0.9 convolution_convert_fusion
  132.9 0.0 all-reduce.7.cloned.1.call-update
  132.9 0.6 dynamic-slice
  133.5 31.6 %all-reduce.7.cloned.1.call-done = bf16[2,4,16,1024]{3,2,1,0:T(8,128)(2,1)} async-done(((bf16[2,4,16,1024]{3,2,1,0:T(8,128)(2,1)}), bf16[2,4,16,1024]{3,2,1,0:T(8,128)(2,1)}) %all-reduce.7.cloned.1.call-update) | async-done | bytes 262160
  165.1 1.5 fusion.51
  166.7 0.7 add_convert_fusion
  (18 shorter events, 0.2 us)
Async XLA Ops:
  6.5 125.4 %copy-start = (bf16[256,1024]{1,0:T(8,128)(2,1)S(1)}, bf16[256,1024]{1,0:T(8,128)(2,1)}, u32[]{:S(2)}) copy-start(bf16[256,1024]{1,0:T(8,128)(2,1)} %param.13) | copy-start | bytes 1572868
  6.5 53.8 %all-reduce.5.cloned.1.call-start = ((), (), s32[]{:S(2)}) async-start(), calls=%async_computation | async-start | bytes 524288 | tf_op jit(solution)/shard_map/psum | solution.py:53
  16.6 2.3 %copy-start.1 = (bf16[3,3,256,1024]{3,2,1,0:T(8,128)(2,1)S(1)}, bf16[3,3,256,1024]{3,2,1,0:T(8,128)(2,1)}, u32[]{:S(2)}) copy-start(bf16[3,3,256,1024]{3,2,1,0:T(8,128)(2,1)} %param.9) | copy-start | bytes 14155780
  21.7 2.0 %copy-start.2 = (bf16[3,256,1024]{2,1,0:T(8,128)(2,1)S(1)}, bf16[3,256,1024]{2,1,0:T(8,128)(2,1)}, u32[]{:S(2)}) copy-start(bf16[3,256,1024]{2,1,0:T(8,128)(2,1)} %param.10) | copy-start | bytes 4718596
  22.1 6.7 %collective-permute-start = (bf16[1,4,16,256]{3,2,1,0:T(8,128)(2,1)S(1)}, bf16[1,4,16,256]{3,2,1,0:T(8,128)(2,1)S(1)}, u32[]{:S(2)}, u32[]{:S(2)}) collective-permute-start(bf16[1,4,16,256]{3,2,1,0:T(8,128)(2,1)S(1)} %bitcast.119), channel_id=1, source_target_pairs={{28,0},{0,4},{4,8},{8,12},{12,16},{16,20},{20,24},{24,28},{29,1},{... | collective-permute-start | bytes 98312 | tf_op jit(solution)/shard_map/ppermute | solution.py:12
  28.8 32.6 %copy-start.4 = (f32[1024]{0:T(1024)S(1)}, f32[1024]{0:T(1024)}, u32[]{:S(2)}) copy-start(f32[1024]{0:T(1024)} %param.11) | copy-start | bytes 12292
  29.0 33.5 %copy-start.5 = (bf16[3,256,1024]{2,1,0:T(8,128)(2,1)S(1)}, bf16[3,256,1024]{2,1,0:T(8,128)(2,1)}, u32[]{:S(2)}) copy-start(bf16[3,256,1024]{2,1,0:T(8,128)(2,1)} %param.12) | copy-start | bytes 4718596
  30.0 135.1 %all-reduce.7.cloned.1.call-start = ((), (), s32[]{:S(2)}) async-start(), calls=%async_computation.1 | async-start | bytes 524288
  131.7 1.2 copy-start.6
  131.7 34.9 %copy-start.3 = (bf16[4,1,16,1024]{3,2,1,0:T(8,128)(2,1)S(1)}, bf16[4,1,16,1024]{3,2,1,0:T(8,128)(2,1)}, u32[]{:S(2)}) copy-start(bf16[4,1,16,1024]{3,2,1,0:T(8,128)(2,1)} %param.7) | copy-start | bytes 393220
Sparse Core Ops, SparseCore 0:
  30.1 30.1 all-reduce.4
  133.0 32.0 all-reduce.6
where the time goes:
time: 175 us; the launch traced here: 174 us
  blocking collectives  74.7 us (43%)
  waiting for transfers between devices  66.7 us (38%)
  between operations  13.7 us (8%)
  matrix products  8.44 us (5%)
  other arithmetic  5.49 us (3%)
  local copies, waits for them, and re-layouts  3.57 us (2%)
    all_gather x1, blocking collectives, body(): lax.all_gather(key_local, 'orbit', axis=0, tiled=True)  33.7 us
    all_gather x1, blocking collectives, body(): lax.all_gather(value_local, 'orbit', axis=0, tiled=True)  32.1 us
    unnamed x3, waiting for transfers between devices  31.6 us
    psum x1, waiting for transfers between devices, body(): summed = lax.psum(partial_value.astype(jnp.bfloat16), 'space')  30.2 us
    all_gather x1, blocking collectives, body(): gathered = lax.all_gather(latents, 'space', axis=1, tiled=True)  8.95 us
    ppermute x1, waiting for transfers between devices, from_behind(): return lax.ppermute(block, axis, route)  4.83 us
    dot_general x12, matrix products, dot_trans(): lax.dot_general(left, right, (((1,), (1,)), ((), ())), preferred_element_...  4 us
  transfers between devices with their start and end apart: 3, of which 3 were waited for; matrix products, arithmetic and copies ran while one was open for 0% of the time, Pallas kernels for 0%

commit v1 on v0

v1 whole, which is shorter than its diff:
```python
import functools

import jax
import jax.numpy as jnp
from jax import lax
from jax.experimental import pallas as pl
from jax.experimental.pallas import tpu as pltpu
from jax.sharding import PartitionSpec as P

HD = 64
CORES = 2
F32 = jnp.float32
BF16 = jnp.bfloat16


def dot(left, right):
    return jnp.dot(left, right, preferred_element_type=F32)


def dot_trans(left, right):
    return lax.dot_general(left, right, (((1,), (1,)), ((), ())), preferred_element_type=F32)


def rms_scale(wide, gain):
    return wide * lax.rsqrt(jnp.mean(wide * wide, axis=-1, keepdims=True) + 1e-06) * gain


def split_by(number, size):
    if size & (size - 1) == 0:
        quotient = number >> (size.bit_length() - 1)
    else:
        quotient = (number * (65536 // size + 1)) >> 16
    return quotient, number - quotient * size


def digits(count, sizes):
    number = lax.broadcasted_iota(jnp.int32, (count, 1), 0)
    found = []
    for size in reversed(sizes[1:]):
        number, digit = split_by(number, size)
        found.append(digit)
    return [number] + found[::-1]


def picks(source, width):
    columns = lax.broadcasted_iota(jnp.int32, (source.shape[0], width), 1)
    return columns == source


def as_weights(mask):
    return jnp.where(mask, 1.0, 0.0).astype(BF16)


class Plan:
    def __init__(self, orbit, space, cols, chans, slice_chans):
        self.orbit, self.space, self.cols, self.chans = orbit, space, cols, chans
        self.slice_chans = slice_chans
        self.x = space // CORES
        self.ncol = cols // orbit
        self.peers = orbit * self.x
        self.pixels = self.x * self.ncol
        self.views = 2 * orbit
        self.half_rows = self.views * self.pixels
        sets = 3 * self.pixels
        self.in_lanes = next(n for n in (1, 2, 4, 8) if sets * n % 8 == 0)
        self.in_rows, self.in_width = sets * self.in_lanes, chans // self.in_lanes
        back = 2 * self.ncol
        self.out_lanes = next(n for n in (1, 2, 4, 8) if back * n % 8 == 0)
        self.out_rows, self.out_width = back * self.out_lanes, chans // self.out_lanes


def conv_kernel(plan, x_ref, gain_ref, weight_ref, temporal_ref, send_ref, keep_ref, normed):
    rows, per_row = x_ref.shape[0], x_ref.shape[1]
    cols, depth = plan.cols, plan.slice_chans
    gain = gain_ref[...]
    for r in range(rows):
        normed[r * per_row : (r + 1) * per_row] = rms_scale(x_ref[r].astype(F32), gain).astype(BF16)
    count = rows * per_row
    column = split_by(lax.broadcasted_iota(jnp.int32, (count, 1), 0), cols)[1]
    total = None
    for j in (1, 0, 2):
        part = dot_trans(normed[...], weight_ref[1, j])
        above = dot_trans(normed[: count - per_row], weight_ref[0, j])
        below = dot_trans(normed[per_row:], weight_ref[2, j])
        edge = jnp.zeros((per_row, depth), F32)
        part = part + jnp.concatenate([edge, above]) + jnp.concatenate([below, edge])
        if j == 0:
            part = jnp.where(column == 0, 0.0, pltpu.roll(part, 1, 0))
        if j == 2:
            part = jnp.where(column == cols - 1, 0.0, pltpu.roll(part, count - 1, 0))
        total = part if total is None else total + part
    activated = (total / (1.0 + jnp.exp(-total))).astype(BF16)
    activated = activated.reshape(rows, per_row // cols, cols, depth)
    pixels = rows * cols
    even = [activated[:, f].reshape(pixels, depth) for f in (0, 2)]
    odd = [activated[:, f].reshape(pixels, depth) for f in (1, 3)]
    even, odd = jnp.concatenate(even), jnp.concatenate(odd)
    first, second, third = dot(odd, temporal_ref[0]), dot(even, temporal_ref[1]), dot(odd, temporal_ref[2])
    own = second + third
    sets = jnp.concatenate([own[:pixels], own[pixels:] + first[:pixels], first[pixels:]]).astype(BF16)
    width = plan.in_width
    stacked = jnp.concatenate([sets[:, k * width : (k + 1) * width] for k in range(plan.in_lanes)])
    core = lax.rem(lax.axis_index("space"), CORES)
    count = plan.orbit * plan.in_rows
    o, lane, which, r, c = digits(count, (plan.orbit, plan.in_lanes, 3, plan.x, plan.ncol))
    source = lane * (3 * pixels) + which * pixels + r * (CORES * cols) + o * plan.ncol + c
    for ref, parity in ((send_ref, 1 - core), (keep_ref, core)):
        ref[...] = dot(as_weights(picks(source + parity * cols, stacked.shape[0])), stacked).astype(BF16)


def norm_kernel(plan, got_ref, gain_ref, down_ref, normed_ref):
    o, t, r, c = digits(plan.half_rows, (plan.orbit, 2, plan.x, plan.ncol))
    width = plan.peers * plan.in_rows
    peer, lane, which, pixel = None, None, None, None
    number = lax.broadcasted_iota(jnp.int32, (1, width), 1)
    number, pixel = split_by(number, plan.pixels)
    number, which = split_by(number, 3)
    number, lane = split_by(number, plan.in_lanes)
    sender, _ = split_by(number, plan.x)
    before = jnp.where(o == 0, plan.orbit - 1, o - 1)
    same = (which == t) & (sender == o)
    edge = (which == 2) & (sender == before) & (t == 0)
    wanted = (pixel == r * plan.ncol + c) & (same | edge)
    got = got_ref[...]
    down = [dot(as_weights(wanted & (lane == k)), got) for k in range(plan.in_lanes)]
    down = jnp.concatenate(down, axis=1).astype(BF16)
    down_ref[...] = down
    normed_ref[...] = rms_scale(down.astype(F32), gain_ref[...]).astype(BF16)


def attend_kernel(plan, own_ref, other_ref, down_ref, qkv_ref, out_ref, send_ref, keep_ref):
    half, depth = plan.half_rows, plan.slice_chans
    heads = depth // HD
    flat = jnp.concatenate([own_ref[...], other_ref[...]])
    query, key, value = [dot_trans(flat, qkv_ref[k]).astype(BF16) for k in range(3)]
    lane_head = lax.broadcasted_iota(jnp.int32, (1, depth), 1) >> (HD.bit_length() - 1)
    count = 2 * half
    wide = query.astype(F32)
    query = jnp.concatenate([jnp.where(lane_head == h, wide, 0.0) for h in range(heads)]).astype(BF16)
    scores = dot_trans(query, key) * (HD**-0.5)
    row = lax.broadcasted_iota(jnp.int32, (heads * count, 1), 0) & (count - 1)
    column = lax.broadcasted_iota(jnp.int32, (1, count), 1)
    low, shift = plan.pixels - 1, half.bit_length() - 1
    same = ((row & low) == (column & low)) & ((row >> shift) == (column >> shift))
    top = jnp.max(jnp.where(same, scores, -jnp.inf), axis=-1, keepdims=True)
    weights = jnp.where(same, jnp.exp(scores - top), 0.0)
    probs = (weights / jnp.sum(weights, axis=-1, keepdims=True)).astype(BF16)
    found = dot(probs, value)
    mixed = jnp.zeros((count, depth), F32)
    for h in range(heads):
        mixed = jnp.where(lane_head == h, found[h * count : (h + 1) * count], mixed)
    projected = dot(mixed.astype(BF16), out_ref[...])
    first = lax.axis_index("space") < CORES
    kept = projected[:half] + jnp.where(first, 1.0, 0.0) * down_ref[...].astype(F32)
    rows = plan.peers * plan.out_rows
    o, r, lane, t, c = digits(rows, (plan.orbit, plan.x, plan.out_lanes, 2, plan.ncol))
    source = lane * half + ((o * 2 + t) * plan.x + r) * plan.ncol + c
    order = as_weights(picks(source, plan.out_lanes * half))
    width = plan.out_width
    for ref, block in ((send_ref, projected[half:]), (keep_ref, kept)):
        block = block.astype(BF16)
        block = jnp.concatenate([block[:, k * width : (k + 1) * width] for k in range(plan.out_lanes)])
        ref[...] = dot(order, block).astype(BF16)


def end_kernel(plan, got_ref, latents_ref, out_ref):
    rows = 2 * plan.cols
    t, o, c = digits(rows, (2, plan.orbit, plan.ncol))
    number = lax.broadcasted_iota(jnp.int32, (1, got_ref.shape[0]), 1)
    number, column = split_by(number, plan.ncol)
    number, view = split_by(number, 2)
    number, lane = split_by(number, plan.out_lanes)
    sender, _ = split_by(number, plan.x)
    wanted = (sender == o) & (column == c) & (view == t)
    got = got_ref[...]
    bottom = [dot(as_weights(wanted & (lane == k)), got) for k in range(plan.out_lanes)]
    bottom = jnp.concatenate(bottom, axis=1).astype(BF16).astype(F32)
    for f in range(4):
        block = bottom[(f // 2) * plan.cols : (f // 2 + 1) * plan.cols]
        out_ref[f] = (latents_ref[f].astype(F32) + block).astype(BF16)


def call(kernel, name, shapes, args, scratch=(), flops=0):
    whole = pl.BlockSpec(memory_space=pltpu.VMEM)
    outs = [jax.ShapeDtypeStruct(shape, BF16) for shape in shapes]
    moved = sum(a.size * a.dtype.itemsize for a in (*args, *outs))
    return pl.pallas_call(
        kernel,
        out_shape=outs,
        in_specs=[whole] * len(args),
        out_specs=[whole] * len(outs),
        scratch_shapes=list(scratch),
        compiler_params=pltpu.CompilerParams(vmem_limit_bytes=40 * 2**20),
        cost_estimate=pl.CostEstimate(flops=flops, bytes_accessed=moved, transcendentals=0),
        name=name,
    )(*args)


def body(latents, conv_gain, spatial_weight, temporal_weight, attn_gain, qkv_weight, out_weight):
    views, _, cols, chans = latents.shape
    orbit, space = lax.axis_size("orbit"), lax.axis_size("space")
    plan = Plan(orbit, space, cols, chans, spatial_weight.shape[2])
    both = ("orbit", "space")
    groups = [
        [(o * plan.x + x) * CORES + core for o in range(orbit) for x in range(plan.x)]
        for core in range(CORES)
    ]
    chip = [(s, s ^ 1) for s in range(space)]

    own = latents.reshape(views * cols, chans)
    gathered = lax.all_gather(own, "space", axis=0)
    shape = (orbit * plan.in_rows, plan.in_width)
    send, keep = call(
        functools.partial(conv_kernel, plan),
        "conv",
        [shape, shape],
        (gathered, conv_gain.reshape(1, chans), spatial_weight, temporal_weight),
        [pltpu.VMEM((space * views * cols, chans), BF16)],
        flops=2 * 9 * space * views * cols * chans * plan.slice_chans,
    )
    partial_sum = keep.astype(F32) + lax.ppermute(send, "space", chip).astype(F32)
    partial_sum = partial_sum.astype(BF16).reshape(orbit, 1, plan.in_rows, plan.in_width)
    spread = jnp.broadcast_to(partial_sum, (orbit, plan.x, plan.in_rows, plan.in_width))
    spread = spread.reshape(plan.peers, plan.in_rows, plan.in_width)
    got = lax.all_to_all(spread, both, 0, 0, tiled=True, axis_index_groups=groups)
    shape = (plan.half_rows, chans)
    down, normed = call(
        functools.partial(norm_kernel, plan),
        "down_norm",
        [shape, shape],
        (got.reshape(plan.peers * plan.in_rows, plan.in_width), attn_gain.reshape(1, chans)),
    )
    other = lax.ppermute(normed, "space", chip)
    shape = (plan.peers * plan.out_rows, plan.out_width)
    send, keep = call(
        functools.partial(attend_kernel, plan),
        "attend",
        [shape, shape],
        (normed, other, down, qkv_weight, out_weight),
        flops=2 * 4 * 2 * plan.half_rows * chans * plan.slice_chans,
    )
    partial_sum = keep.astype(F32) + lax.ppermute(send, "space", chip).astype(F32)
    partial_sum = partial_sum.astype(BF16).reshape(plan.peers, plan.out_rows, plan.out_width)
    got = lax.all_to_all(partial_sum, both, 0, 0, tiled=True, axis_index_groups=groups)
    (restored,) = call(
        functools.partial(end_kernel, plan),
        "restore",
        [(views, cols, chans)],
        (got.reshape(shape), latents.reshape(views, cols, chans)),
    )
    return restored.reshape(latents.shape)


def solution(mesh):
    return jax.shard_map(
        body,
        mesh=mesh,
        in_specs=(
            P("orbit", "space", None, None),
            P(),
            P(None, None, "space", None),
            P(None, "space", None),
            P(),
            P(None, "space", None),
            P("space", None),
        ),
        out_specs=P("orbit", "space", None, None),
        check_vma=False,
    )
```

time: 175 us -> 54.4 us (0.31)
  waiting for transfers between devices: 66.7 us -> 3.63 us
  blocking collectives: 74.7 us -> 39.4 us
  between operations: 13.7 us -> 0.07 us
  matrix products: 8.44 us -> 0 us
  Pallas kernels: 0 us -> 5.77 us
  other arithmetic: 5.49 us -> 0.08 us
    all_gather x3 -> x1, blocking collectives: 74.7 us -> 8.82 us  [body(): gathered = lax.all_gather(own, 'space', axis=0)]
    unnamed x3 -> x0, waiting for transfers between devices: 31.6 us -> none
    all_to_all x0 -> x2, blocking collectives: none -> 30.6 us  [the longest x1 19.4 us: body(): lax.all_to_all(spread, both, 0, 0, tiled=True, axis_index_groups=groups)]
    psum x1 -> x0, waiting for transfers between devices: 30.2 us -> none  [body(): summed = lax.psum(partial_value.astype(jnp.bfloat16), 'space')]
    dot_general x17 -> x0, matrix products: 7.21 us -> none  [the longest x12 4 us: dot_trans(): lax.dot_general(left, right, (((1,), (1,)), ((), ())), preferred_element_...]
    pallas_call x0 -> x4, Pallas kernels: none -> 5.77 us  [call(): pl.pallas_call(kernel, out_shape=outs, in_specs=[whole] * len(args), out_...]
    convert_element_type x4 -> x1, other arithmetic: 4.19 us -> 0.05 us  [body(): partial_sum.astype(BF16).reshape(orbit, 1, plan.in_rows, plan.in_width)]
    unnamed x15 -> x14, local copies, waits for them, and re-layouts: 2.29 us -> 4.45 us
where the time goes in v1:
time: 54.4 us; the launch traced here: 54.2 us
  blocking collectives  39.4 us (72%)
  Pallas kernels  5.77 us (11%)
  local copies, waits for them, and re-layouts  4.48 us (8%)
  waiting for transfers between devices  3.63 us (7%)
  starting transfers between devices  0.7 us (1%)
    all_to_all x1, blocking collectives, body(): lax.all_to_all(spread, both, 0, 0, tiled=True, axis_index_groups=groups)  19.4 us
    all_to_all x1, blocking collectives, body(): lax.all_to_all(partial_sum, both, 0, 0, tiled=True, axis_index_groups=gro...  11.2 us
    all_gather x1, blocking collectives, body(): gathered = lax.all_gather(own, 'space', axis=0)  8.82 us
    pallas_call x4, Pallas kernels, call(): pl.pallas_call(kernel, out_shape=outs, in_specs=[whole] * len(args), out_...  5.77 us
    unnamed x14, local copies, waits for them, and re-layouts  4.45 us
    ppermute x2, waiting for transfers between devices, body(): lax.ppermute(send, 'space', chip).astype(F32)  2.29 us
    ppermute x1, waiting for transfers between devices, body(): other = lax.ppermute(normed, 'space', chip)  1.33 us
  transfers between devices with their start and end apart: 3, of which 3 were waited for; matrix products, arithmetic and copies ran while one was open for 0% of the time, Pallas kernels for 0%

profile of v1, /device:TPU:0, one launch (start us, length us, event | category | flops | bytes accessed | tf_op | source)
XLA Modules:
  0.0 54.2 jit_solution(15940114895321345938)
XLA Ops:
  0.0 8.8 %all_gather.3.x_ref = bf16[4,64,1024]{2,1,0:T(8,128)(2,1)S(1)} all-gather(bf16[1,64,1024]{2,1,0:T(8,128)(2,1)} %bitcast.14), channel_id=1, replica_groups=mesh['orbit'=8,'space'=4] {'space'}, dimensions={0}, use_global_device_ids=true | all-gather | bytes 655360 | tf_op jit(solution)/shard_map/all_gather | solution.py:211
  8.8 0.0 copy-start
  8.8 2.3 %copy-done = bf16[3,3,256,1024]{3,2,1,0:T(8,128)(2,1)S(1)} copy-done((bf16[3,3,256,1024]{3,2,1,0:T(8,128)(2,1)S(1)}, bf16[3,3,256,1024]{3,2,1,0:T(8,128)(2,1)}, u32[]{:S(2)}) %copy-start) | copy-done | bytes 4718616
  11.2 0.0 copy-start.2
  11.2 1.4 %copy-done.2 = bf16[3,256,1024]{2,1,0:T(8,128)(2,1)S(1)} copy-done((bf16[3,256,1024]{2,1,0:T(8,128)(2,1)S(1)}, bf16[3,256,1024]{2,1,0:T(8,128)(2,1)}, u32[]{:S(2)}) %copy-start.2) | copy-done | bytes 1572888
  12.6 0.0 copy-start.5
  12.6 0.7 %copy-done.5 = f32[1024]{0:T(1024)S(1)} copy-done((f32[1024]{0:T(1024)S(1)}, f32[1024]{0:T(1024)}, u32[]{:S(2)}) %copy-start.5) | copy-done | bytes 4120
  13.2 0.0 copy-start.6
  13.3 3.1 %conv.1 = (bf16[192,512]{1,0:T(8,128)(2,1)S(1)}, bf16[192,512]{1,0:T(8,128)(2,1)S(1)}) custom-call(bf16[4,64,1024]{2,1,0:T(8,128)(2,1)S(1)} %all_gather.3.x_ref, f32[1,1024]{1,0:T(1,128)S(1)} %bitcast.17, bf16[3,3,256,1024]{3,2,1,0:T(8,128)(2,1)S(1)} %copy-done, bf16[3,256,1024]{2,1,0:T(8,128)(2,1)S(1)} %copy-done.2), custom_call_target="tpu_custom_call" | custom-call | flops 1207959552 | bytes 7213056 | tf_op jit(solution)/shard_map/conv/pallas_call | solution.py:187
  16.3 0.0 copy-start.1
  16.3 0.0 copy-start.3
  16.4 0.4 collective-permute-start
  16.8 1.1 %collective-permute-done = bf16[192,512]{1,0:T(8,128)(2,1)S(1)} collective-permute-done((bf16[192,512]{1,0:T(8,128)(2,1)S(1)}, bf16[192,512]{1,0:T(8,128)(2,1)S(1)}, u32[]{:S(2)}, u32[]{:S(2)}) %collective-permute-start) | collective-permute-done | bytes 196640 | tf_op jit(solution)/shard_map/ppermute | solution.py:221
  17.9 0.1 add_convert_fusion
  18.0 19.4 %all_to_all.10 = bf16[16,24,512]{2,1,0:T(8,128)(2,1)S(1)} all-to-all(bf16[16,24,512]{2,1,0:T(8,128)(2,1)S(1)} %bitcast.19), channel_id=1, replica_groups={{0,2,4,6,8,10,12,14,16,18,20,22,24,26,28,30},{1,3,5,7,9,11,13,15,17,19,..., dimensions={0} | all-to-all | bytes 786432 | tf_op jit(solution)/shard_map/all_to_all | solution.py:225
  37.3 0.0 copy-done.6
  37.3 0.4 down_norm.1
  37.7 0.1 collective-permute-start.1
  37.8 1.3 %collective-permute-done.1.other_ref = bf16[64,1024]{1,0:T(8,128)(2,1)S(1)} collective-permute-done((bf16[64,1024]{1,0:T(8,128)(2,1)S(1)}, bf16[64,1024]{1,0:T(8,128)(2,1)S(1)}, u32[]{:S(2)}, u32[]{:S(2)}) %collective-permute-start.1) | collective-permute-done | bytes 131104 | tf_op jit(solution)/shard_map/ppermute | solution.py:233
  39.1 0.0 copy-done.1
  39.1 0.0 copy-done.3
  39.1 0.0 copy-start.4
  39.1 1.5 %attend.1 = (bf16[128,512]{1,0:T(8,128)(2,1)S(1)}, bf16[128,512]{1,0:T(8,128)(2,1)S(1)}) custom-call(bf16[64,1024]{1,0:T(8,128)(2,1)S(1)} %get-tuple-element.13.own_ref, bf16[64,1024]{1,0:T(8,128)(2,1)S(1)} %collective-permute-done.1.other_ref, bf16[64,1024]{1,0:T(8,128)(2,1)S(1)} %get-tuple-element.14.down_ref, bf16[3,256,1024]{2,1,0:T(8,128)(2,1)S(1)} %copy-done.1, ...), custom_call_target="tpu_custom_call" | custom-call | flops 268435456 | bytes 2752512 | tf_op jit(solution)/shard_map/attend/pallas_call | solution.py:187
  40.6 0.2 collective-permute-start.2
  40.9 1.2 %collective-permute-done.2 = bf16[128,512]{1,0:T(8,128)(2,1)S(1)} collective-permute-done((bf16[128,512]{1,0:T(8,128)(2,1)S(1)}, bf16[128,512]{1,0:T(8,128)(2,1)S(1)}, u32[]{:S(2)}, u32[]{:S(2)}) %collective-permute-start.2) | collective-permute-done | bytes 131104 | tf_op jit(solution)/shard_map/ppermute | solution.py:242
  42.1 11.2 %all_to_all.11 = bf16[16,8,512]{2,1,0:T(8,128)(2,1)S(1)} all-to-all(bf16[16,8,512]{2,1,0:T(8,128)(2,1)S(1)} %fusion), channel_id=1, replica_groups={{0,2,4,6,8,10,12,14,16,18,20,22,24,26,28,30},{1,3,5,7,9,11,13,15,17,19,..., dimensions={0} | all-to-all | bytes 262144 | tf_op jit(solution)/shard_map/all_to_all | solution.py:244
  53.3 0.0 copy-done.4
  53.3 0.8 %restore.1 = bf16[4,16,1024]{2,1,0:T(8,128)(2,1)} custom-call(bf16[128,512]{1,0:T(8,128)(2,1)S(1)} %bitcast.16, bf16[4,16,1024]{2,1,0:T(8,128)(2,1)S(1)} %bitcast.15), custom_call_target="tpu_custom_call" | custom-call | bytes 393216 | tf_op jit(solution)/shard_map/restore/pallas_call | solution.py:187
  (2 shorter events, 0.1 us)
Async XLA Ops:
  8.8 2.3 %copy-start = (bf16[3,3,256,1024]{3,2,1,0:T(8,128)(2,1)S(1)}, bf16[3,3,256,1024]{3,2,1,0:T(8,128)(2,1)}, u32[]{:S(2)}) copy-start(bf16[3,3,256,1024]{3,2,1,0:T(8,128)(2,1)} %weight_ref.1) | copy-start | bytes 14155780
  11.2 1.4 %copy-start.2 = (bf16[3,256,1024]{2,1,0:T(8,128)(2,1)S(1)}, bf16[3,256,1024]{2,1,0:T(8,128)(2,1)}, u32[]{:S(2)}) copy-start(bf16[3,256,1024]{2,1,0:T(8,128)(2,1)} %temporal_ref.1) | copy-start | bytes 4718596
  12.6 0.7 %copy-start.5 = (f32[1024]{0:T(1024)S(1)}, f32[1024]{0:T(1024)}, u32[]{:S(2)}) copy-start(f32[1024]{0:T(1024)} %param.8) | copy-start | bytes 12292
  13.2 24.1 %copy-start.6 = (f32[1024]{0:T(1024)S(1)}, f32[1024]{0:T(1024)}, u32[]{:S(2)}) copy-start(f32[1024]{0:T(1024)} %param.11) | copy-start | bytes 12292
  16.3 22.8 %copy-start.1 = (bf16[3,256,1024]{2,1,0:T(8,128)(2,1)S(1)}, bf16[3,256,1024]{2,1,0:T(8,128)(2,1)}, u32[]{:S(2)}) copy-start(bf16[3,256,1024]{2,1,0:T(8,128)(2,1)} %qkv_ref.1) | copy-start | bytes 4718596
  16.3 22.8 %copy-start.3 = (bf16[256,1024]{1,0:T(8,128)(2,1)S(1)}, bf16[256,1024]{1,0:T(8,128)(2,1)}, u32[]{:S(2)}) copy-start(bf16[256,1024]{1,0:T(8,128)(2,1)} %out_ref.1) | copy-start | bytes 1572868
  16.4 1.5 %collective-permute-start = (bf16[192,512]{1,0:T(8,128)(2,1)S(1)}, bf16[192,512]{1,0:T(8,128)(2,1)S(1)}, u32[]{:S(2)}, u32[]{:S(2)}) collective-permute-start(bf16[192,512]{1,0:T(8,128)(2,1)S(1)} %get-tuple-element.12), channel_id=1, source_target_pairs={{0,1},{1,0},{2,3},{3,2},{4,5},{5,4},{6,7},{7,6},{8,9},{9,8},{10,11... | collective-permute-start | bytes 589832 | tf_op jit(solution)/shard_map/ppermute | solution.py:221
  37.7 1.4 %collective-permute-start.1 = (bf16[64,1024]{1,0:T(8,128)(2,1)S(1)}, bf16[64,1024]{1,0:T(8,128)(2,1)S(1)}, u32[]{:S(2)}, u32[]{:S(2)}) collective-permute-start(bf16[64,1024]{1,0:T(8,128)(2,1)S(1)} %get-tuple-element.13.own_ref), channel_id=1, source_target_pairs={{0,1},{1,0},{2,3},{3,2},{4,5},{5,4},{6,7},{7,6},{8,9},{9,8},{10,11... | collective-permute-start | bytes 393224 | tf_op jit(solution)/shard_map/ppermute | solution.py:233
  39.1 14.2 %copy-start.4 = (bf16[4,1,16,1024]{3,2,1,0:T(8,128)(2,1)S(1)}, bf16[4,1,16,1024]{3,2,1,0:T(8,128)(2,1)}, u32[]{:S(2)}) copy-start(bf16[4,1,16,1024]{3,2,1,0:T(8,128)(2,1)} %param.7) | copy-start | bytes 393220
  40.6 1.4 %collective-permute-start.2 = (bf16[128,512]{1,0:T(8,128)(2,1)S(1)}, bf16[128,512]{1,0:T(8,128)(2,1)S(1)}, u32[]{:S(2)}, u32[]{:S(2)}) collective-permute-start(bf16[128,512]{1,0:T(8,128)(2,1)S(1)} %get-tuple-element.16), channel_id=1, source_target_pairs={{0,1},{1,0},{2,3},{3,2},{4,5},{5,4},{6,7},{7,6},{8,9},{9,8},{10,11... | collective-permute-start | bytes 393224 | tf_op jit(solution)/shard_map/ppermute | solution.py:242

commit v2 on v0

v2 whole, which is shorter than its diff:
```python
import functools

import jax
import jax.numpy as jnp
import numpy as np
from jax import lax
from jax.experimental import pallas as pl
from jax.experimental.pallas import tpu as pltpu
from jax.sharding import PartitionSpec as P

HD = 64
CORES = 2
F32 = jnp.float32
BF16 = jnp.bfloat16


def dot(left, right):
    return jnp.dot(left, right, preferred_element_type=F32)


def dot_trans(left, right):
    return lax.dot_general(left, right, (((1,), (1,)), ((), ())), preferred_element_type=F32)


def rms_scale(wide, gain):
    return wide * lax.rsqrt(jnp.mean(wide * wide, axis=-1, keepdims=True) + 1e-06) * gain


def picks(source, width):
    return jnp.asarray(np.asarray(source).reshape(-1, 1) == np.arange(width), BF16)


class Plan:
    def __init__(self, orbit, space, views, cols, chans, slice_chans):
        self.orbit, self.space, self.views = orbit, space, views
        self.cols, self.chans, self.slice_chans = cols, chans, slice_chans
        self.x = space // CORES
        self.ncol = cols // orbit
        self.pixels = self.x * self.ncol
        self.down_views = views // 2 * orbit
        self.down_rows = self.down_views * self.pixels
        self.send_rows = views * self.pixels
        back = views // 2 * self.ncol
        self.lanes = next(n for n in (1, 2, 4, 8) if back * n % 8 == 0)
        self.back_rows, self.back_width = back * self.lanes, chans // self.lanes

    def send_order(self):
        o, core, odd, pair, r, c = np.indices((self.orbit, CORES, 2, self.views // 2, self.x, self.ncol))
        row, view, col = r * CORES + core, 2 * pair + odd, o * self.ncol + c
        return picks((row * self.views + view) * self.cols + col, self.space * self.views * self.cols)

    def back_order(self):
        o, r, lane, t, c = np.indices((self.orbit, self.x, self.lanes, self.views // 2, self.ncol))
        view = o * (self.views // 2) + t
        source = lane * self.down_rows + (view * self.x + r) * self.ncol + c
        return picks(source, self.lanes * self.down_rows)

    def end_order(self):
        sender, _, lane, view, c = np.indices((self.orbit, self.x, self.lanes, self.views // 2, self.ncol))
        target = view * self.cols + sender * self.ncol + c
        parts = []
        for k in range(self.lanes):
            wanted = np.where(lane == k, target, -1).reshape(1, -1)
            parts.append(wanted == np.arange(self.views // 2 * self.cols).reshape(-1, 1))
        return jnp.asarray(np.stack(parts), BF16)


def norm_kernel(gain_ref, *refs):
    count = len(refs) // 2
    for x_ref, out_ref in zip(refs[:count], refs[count:]):
        out_ref[...] = rms_scale(x_ref[...].astype(F32), gain_ref[...]).astype(BF16)


def conv_kernel(plan, gain_ref, weight_ref, order_ref, *refs):
    x_refs, (out_ref, normed) = refs[:-2], refs[-2:]
    per_row, cols, depth = plan.views * plan.cols, plan.cols, plan.slice_chans
    gain = gain_ref[...]
    space = lax.axis_index("space")
    ready = plan.x + 1
    for k, x_ref in enumerate(x_refs):
        block = x_ref[...]
        if k >= ready:
            block = rms_scale(block.astype(F32), gain).astype(BF16)
        index = k if k < 2 else (k - 1) * CORES if k < ready else (k - ready + 1) * CORES + 1
        normed[space ^ index] = block
    count = plan.space * per_row
    rows = normed[...].reshape(count, plan.chans)
    column = lax.broadcasted_iota(jnp.int32, (count, 1), 0) & (cols - 1)
    total = None
    for j in (1, 0, 2):
        part = dot_trans(rows, weight_ref[1, j])
        above = dot_trans(rows[: count - per_row], weight_ref[0, j])
        below = dot_trans(rows[per_row:], weight_ref[2, j])
        edge = jnp.zeros((per_row, depth), F32)
        part = part + jnp.concatenate([edge, above]) + jnp.concatenate([below, edge])
        if j == 0:
            part = jnp.where(column == 0, 0.0, pltpu.roll(part, 1, 0))
        if j == 2:
            part = jnp.where(column == cols - 1, 0.0, pltpu.roll(part, count - 1, 0))
        total = part if total is None else total + part
    activated = (total / (1.0 + jnp.exp(-total))).astype(BF16)
    out_ref[...] = dot(order_ref[...], activated).astype(BF16)


def temporal_kernel(plan, got_ref, own_ref, other_ref, out_ref):
    core = lax.rem(lax.axis_index("space"), CORES)
    half, depth = plan.send_rows // 2, plan.slice_chans
    total = None
    for index, weight_ref in ((core, own_ref), (1 - core, other_ref)):
        block = got_ref[:, index].astype(F32)
        even = block[:, :half].reshape(plan.down_rows, depth)
        odd = block[:, half:].reshape(plan.down_rows, depth)
        before = pltpu.roll(odd, plan.pixels, 0)
        for k, rows in enumerate((before, even, odd)):
            part = dot(rows.astype(BF16), weight_ref[k])
            total = part if total is None else total + part
    out_ref[...] = total.astype(BF16)


def attend_kernel(plan, gain_ref, order_ref, own_qkv, other_qkv, own_out, other_out, *refs):
    down_refs, out_ref = refs[:-1], refs[-1]
    rows, depth = plan.down_rows, plan.slice_chans
    heads = depth // HD
    down = down_refs[0][...].astype(F32)
    for ref in down_refs[1:]:
        down = down + ref[...].astype(F32)
    down = down.astype(BF16).astype(F32)
    normed = rms_scale(down, gain_ref[...]).astype(BF16)
    lane_head = lax.broadcasted_iota(jnp.int32, (1, depth), 1) >> (HD.bit_length() - 1)
    low = plan.pixels - 1
    row = lax.broadcasted_iota(jnp.int32, (heads * rows, 1), 0) & low
    column = lax.broadcasted_iota(jnp.int32, (1, rows), 1) & low
    same = row == column
    first = lax.axis_index("space") < CORES
    projected = jnp.where(first, 1.0, 0.0) * down
    for qkv_ref, weight_ref in ((own_qkv, own_out), (other_qkv, other_out)):
        query, key, value = [dot_trans(normed, qkv_ref[k]).astype(BF16) for k in range(3)]
        wide = query.astype(F32)
        query = jnp.concatenate([jnp.where(lane_head == h, wide, 0.0) for h in range(heads)]).astype(BF16)
        scores = dot_trans(query, key) * (HD**-0.5)
        top = jnp.max(jnp.where(same, scores, -jnp.inf), axis=-1, keepdims=True)
        weights = jnp.where(same, jnp.exp(scores - top), 0.0)
        probs = (weights / jnp.sum(weights, axis=-1, keepdims=True)).astype(BF16)
        found = dot(probs, value)
        mixed = found[:rows]
        for h in range(1, heads):
            mixed = jnp.where(lane_head == h, found[h * rows : (h + 1) * rows], mixed)
        projected = projected + dot(mixed.astype(BF16), weight_ref[...])
    projected = projected.astype(BF16)
    width = plan.back_width
    stacked = jnp.concatenate([projected[:, k * width : (k + 1) * width] for k in range(plan.lanes)])
    out_ref[...] = dot(order_ref[...], stacked).astype(BF16)


def end_kernel(plan, got_ref, order_ref, latents_ref, out_ref):
    got = got_ref[...]
    bottom = [dot(order_ref[k], got) for k in range(plan.lanes)]
    bottom = jnp.concatenate(bottom, axis=1).astype(BF16).astype(F32)
    for f in range(plan.views):
        block = bottom[(f // 2) * plan.cols : (f // 2 + 1) * plan.cols]
        out_ref[f] = (latents_ref[f].astype(F32) + block).astype(BF16)


def call(kernel, name, shapes, args, scratch=(), flops=0, space=pltpu.VMEM):
    outs = [s if isinstance(s, jax.ShapeDtypeStruct) else jax.ShapeDtypeStruct(s, BF16) for s in shapes]
    moved = sum(a.size * a.dtype.itemsize for a in (*args, *outs))
    return pl.pallas_call(
        kernel,
        out_shape=outs,
        in_specs=[pl.BlockSpec(memory_space=space)] * len(args),
        out_specs=[pl.BlockSpec(memory_space=pltpu.VMEM)] * len(outs),
        scratch_shapes=list(scratch),
        compiler_params=pltpu.CompilerParams(vmem_limit_bytes=40 * 2**20),
        cost_estimate=pl.CostEstimate(flops=flops, bytes_accessed=moved, transcendentals=0),
        name=name,
    )(*args)


def body(latents, conv_gain, spatial_weight, temporal_weight, attn_gain, qkv_weight, out_weight):
    views, _, cols, chans = latents.shape
    orbit, space = lax.axis_size("orbit"), lax.axis_size("space")
    plan = Plan(orbit, space, views, cols, chans, spatial_weight.shape[2])
    conv_gain, attn_gain = conv_gain.reshape(1, chans), attn_gain.reshape(1, chans)

    def swap(block, distance):
        return lax.ppermute(block, "space", [(s, s ^ distance) for s in range(space)])

    def exchange(blocks, groups):
        return lax.all_to_all(blocks, ("orbit", "space"), 0, 0, tiled=True, axis_index_groups=groups)

    by_core = [[o * space + x * CORES + c for o in range(orbit) for c in range(CORES)] for x in range(plan.x)]
    by_x = [[o * space + x * CORES + c for o in range(orbit) for x in range(plan.x)] for c in range(CORES)]

    own = latents.reshape(views * cols, chans)
    far = [swap(own, x * CORES) for x in range(1, plan.x)]
    near = swap(own, 1)
    (normed,) = call(norm_kernel, "norm_own", [own.shape], (conv_gain, own), flops=6 * 10**9)
    normed, near, far = lax.optimization_barrier((normed, near, far))
    other_temporal = swap(temporal_weight, 1)
    across = [swap(block, 1) for block in far]
    ready = call(norm_kernel, "norm", [own.shape] * plan.x, (conv_gain, near, *far), flops=6 * 10**9)

    count = space * views * cols
    (activated,) = call(
        functools.partial(conv_kernel, plan),
        "conv",
        [(count, plan.slice_chans)],
        (conv_gain, spatial_weight, plan.send_order(), normed, *ready, *across),
        [pltpu.VMEM((space, views * cols, chans), BF16)],
        flops=2 * 9 * count * chans * plan.slice_chans,
    )
    activated, qkv, out = lax.optimization_barrier((activated, qkv_weight, out_weight))
    other_qkv, other_out = swap(qkv, 1), swap(out, 1)
    got = exchange(activated.reshape(orbit * CORES, plan.send_rows, plan.slice_chans), by_core)
    (down,) = call(
        functools.partial(temporal_kernel, plan),
        "temporal",
        [(plan.down_rows, chans)],
        (got.reshape(orbit, CORES, plan.send_rows, plan.slice_chans), temporal_weight, other_temporal),
        flops=2 * 6 * plan.down_rows * chans * plan.slice_chans,
    )
    downs = [down] + [swap(down, x * CORES) for x in range(1, plan.x)]
    peers = orbit * plan.x
    (back,) = call(
        functools.partial(attend_kernel, plan),
        "attend",
        [(peers * plan.back_rows, plan.back_width)],
        (attn_gain, plan.back_order(), qkv_weight, other_qkv, out_weight, other_out, *downs),
        flops=2 * 8 * plan.down_rows * chans * plan.slice_chans,
    )
    got = exchange(back.reshape(peers, plan.back_rows, plan.back_width), by_x)
    (restored,) = call(
        functools.partial(end_kernel, plan),
        "restore",
        [(views, cols, chans)],
        (got.reshape(peers * plan.back_rows, plan.back_width), plan.end_order(), latents.reshape(views, cols, chans)),
    )
    return restored.reshape(latents.shape)


def solution(mesh):
    return jax.shard_map(
        body,
        mesh=mesh,
        in_specs=(
            P("orbit", "space", None, None),
            P(),
            P(None, None, "space", None),
            P(None, "space", None),
            P(),
            P(None, "space", None),
            P("space", None),
        ),
        out_specs=P("orbit", "space", None, None),
        check_vma=False,
    )
```

time: 175 us -> 46 us (0.26)
  waiting for transfers between devices: 66.7 us -> 7.06 us
  blocking collectives: 74.7 us -> 25.3 us
  between operations: 13.7 us -> 0.14 us
  matrix products: 8.44 us -> 0 us
  Pallas kernels: 0 us -> 6.3 us
  other arithmetic: 5.49 us -> 0.01 us
  starting transfers between devices: 1.62 us -> 5.3 us
  local copies, waits for them, and re-layouts: 3.57 us -> 1.65 us
    all_gather x3 -> x0, blocking collectives: 74.7 us -> none  [the longest x1 33.7 us: body(): lax.all_gather(key_local, 'orbit', axis=0, tiled=True)]
    unnamed x3 -> x0, waiting for transfers between devices: 31.6 us -> none
    psum x1 -> x0, waiting for transfers between devices: 30.2 us -> none  [body(): summed = lax.psum(partial_value.astype(jnp.bfloat16), 'space')]
    all_to_all x0 -> x2, blocking collectives: none -> 25.3 us  [exchange(): lax.all_to_all(blocks, ('orbit', 'space'), 0, 0, tiled=True, axis_index_g...]
    dot_general x17 -> x0, matrix products: 7.21 us -> none  [the longest x12 4 us: dot_trans(): lax.dot_general(left, right, (((1,), (1,)), ((), ())), preferred_element_...]
    pallas_call x0 -> x6, Pallas kernels: none -> 6.3 us  [call(): pl.pallas_call(kernel, out_shape=outs, in_specs=[pl.BlockSpec(memory_spac...]
    convert_element_type x4 -> x0, other arithmetic: 4.19 us -> none  [the longest x1 1.54 us: body(): grown.astype(jnp.float32)]
    ppermute x1 -> x7, starting transfers between devices: 1.58 us -> 5.3 us  [swap(): lax.ppermute(block, 'space', [(s, s ^ distance) for s in range(space)])]
  transfers between devices with their start and end apart: 3 -> 7, of which waited for: 3 -> 3; matrix products, arithmetic and copies ran while one was open for 0% -> 0% of each run, Pallas kernels for 0% -> 6%
where the time goes in v2:
time: 46 us; the launch traced here: 45.8 us
  blocking collectives  25.3 us (55%)
  waiting for transfers between devices  7.06 us (15%)
  Pallas kernels  6.3 us (14%)
  starting transfers between devices  5.3 us (12%)
  local copies, waits for them, and re-layouts  1.65 us (4%)
    all_to_all x2, blocking collectives, exchange(): lax.all_to_all(blocks, ('orbit', 'space'), 0, 0, tiled=True, axis_index_g...  25.3 us
    ppermute x7, waiting for transfers between devices, swap(): lax.ppermute(block, 'space', [(s, s ^ distance) for s in range(space)])  7.06 us
    pallas_call x6, Pallas kernels, call(): pl.pallas_call(kernel, out_shape=outs, in_specs=[pl.BlockSpec(memory_spac...  6.3 us
    ppermute x7, starting transfers between devices, swap(): lax.ppermute(block, 'space', [(s, s ^ distance) for s in range(space)])  5.3 us
    unnamed x24, local copies, waits for them, and re-layouts  1.65 us
  transfers between devices with their start and end apart: 7, of which 3 were waited for; matrix products, arithmetic and copies ran while one was open for 0% of the time, Pallas kernels for 6%

profile of v2, /device:TPU:0, one launch (start us, length us, event | category | flops | bytes accessed | tf_op | source)
XLA Modules:
  0.0 45.8 jit_solution(3336834661017105603)
XLA Ops:
  0.0 0.5 collective-permute-start
  0.5 2.5 %collective-permute-start.1 = (bf16[64,1024]{1,0:T(8,128)(2,1)}, bf16[64,1024]{1,0:T(8,128)(2,1)S(1)}, u32[]{:S(2)}, u32[]{:S(2)}) collective-permute-start(bf16[64,1024]{1,0:T(8,128)(2,1)} %bitcast.18), channel_id=1, source_target_pairs={{0,2},{1,3},{2,0},{3,1},{4,6},{5,7},{6,4},{7,5},{8,10},{9,11},{10,... | collective-permute-start | bytes 393224 | tf_op jit(solution)/shard_map/ppermute | solution.py:186
  2.9 0.2 collective-permute-start.5
  3.2 0.0 copy-start.3
  3.2 0.9 %copy-done.3 = bf16[4,1,16,1024]{3,2,1,0:T(8,128)(2,1)S(1)} copy-done((bf16[4,1,16,1024]{3,2,1,0:T(8,128)(2,1)S(1)}, bf16[4,1,16,1024]{3,2,1,0:T(8,128)(2,1)}, u32[]{:S(2)}) %copy-start.3) | copy-done | bytes 131096
  4.1 0.0 copy-start.8
  4.1 0.7 %copy-done.8 = f32[1024]{0:T(1024)S(1)} copy-done((f32[1024]{0:T(1024)S(1)}, f32[1024]{0:T(1024)}, u32[]{:S(2)}) %copy-start.8) | copy-done | bytes 4120
  4.8 0.0 slice-start
  4.8 0.1 norm_own.1.refs_0_
  4.9 0.0 slice-start.1
  4.9 0.0 copy-start.5
  4.9 0.0 collective-permute-done.refs_0_
  4.9 2.4 %collective-permute-done.1.refs_1_ = bf16[64,1024]{1,0:T(8,128)(2,1)S(1)} collective-permute-done((bf16[64,1024]{1,0:T(8,128)(2,1)}, bf16[64,1024]{1,0:T(8,128)(2,1)S(1)}, u32[]{:S(2)}, u32[]{:S(2)}) %collective-permute-start.1) | collective-permute-done | bytes 131104 | tf_op jit(solution)/shard_map/ppermute | solution.py:186
  7.3 0.0 collective-permute-start.2
  7.3 0.2 norm.1
  7.5 1.2 %collective-permute-done.2.refs_3_ = bf16[64,1024]{1,0:T(8,128)(2,1)S(1)} collective-permute-done((bf16[64,1024]{1,0:T(8,128)(2,1)S(1)}, bf16[64,1024]{1,0:T(8,128)(2,1)S(1)}, u32[]{:S(2)}, u32[]{:S(2)}) %collective-permute-start.2) | collective-permute-done | bytes 131104 | tf_op jit(solution)/shard_map/ppermute | solution.py:186
  8.7 0.0 slice-done
  8.7 0.0 slice-done.1
  8.7 0.0 copy-done.5
  8.7 0.0 copy-start.1
  8.7 0.0 copy-start.2
  8.7 0.0 copy-start
  8.7 1.9 %conv.1 = bf16[256,256]{1,0:T(8,128)(2,1)S(1)} custom-call(f32[1,1024]{1,0:T(1,128)S(1)} %bitcast.23, bf16[3,3,256,1024]{3,2,1,0:T(8,128)(2,1)S(1)} %bitcast.12, bf16[256,256]{1,0:T(8,128)(2,1)S(1)} %copy-done.5, bf16[64,1024]{1,0:T(8,128)(2,1)S(1)} %norm_own.1.refs_0_, bf16[64,1024]{1,0:T(8,128)(2,1)S(1)} %get-tuple-element.16.refs_1_, ...), custom_call_target="tpu_custom_call" | custom-call | flops 1207959552 | bytes 5509120 | tf_op jit(solution)/shard_map/conv/pallas_call | solution.py:167
  10.7 0.0 copy-done.1
  10.7 0.2 collective-permute-start.3
  10.9 0.0 copy-done.2
  10.9 0.4 collective-permute-start.4
  11.2 13.9 %all_to_all.10 = bf16[16,16,256]{2,1,0:T(8,128)(2,1)S(1)} all-to-all(bf16[16,16,256]{2,1,0:T(8,128)(2,1)S(1)} %bitcast.13), channel_id=1, replica_groups={{0,1,4,5,8,9,12,13,16,17,20,21,24,25,28,29},{2,3,6,7,10,11,14,15,18,19,..., dimensions={0} | all-to-all | bytes 262144 | tf_op jit(solution)/shard_map/all_to_all | solution.py:189
  25.2 0.0 collective-permute-done.5.other_ref
  25.2 0.0 copy-done
  25.2 0.0 copy-start.6
  25.2 0.0 copy-start.9
  25.2 0.7 %temporal.1.refs_0_ = bf16[64,1024]{1,0:T(8,128)(2,1)S(1)} custom-call(bf16[8,2,16,256]{3,2,1,0:T(8,128)(2,1)S(1)} %bitcast.15, bf16[3,256,1024]{2,1,0:T(8,128)(2,1)S(1)} %copy-done, bf16[3,256,1024]{2,1,0:T(8,128)(2,1)S(1)} %collective-permute-done.5.other_ref), custom_call_target="tpu_custom_call" | custom-call | flops 201326592 | bytes 3407872 | tf_op jit(solution)/shard_map/temporal/pallas_call | solution.py:167
  25.9 1.6 %collective-permute-start.6 = (bf16[64,1024]{1,0:T(8,128)(2,1)S(1)}, bf16[64,1024]{1,0:T(8,128)(2,1)S(1)}, u32[]{:S(2)}, u32[]{:S(2)}) collective-permute-start(bf16[64,1024]{1,0:T(8,128)(2,1)S(1)} %temporal.1.refs_0_), channel_id=1, source_target_pairs={{0,2},{1,3},{2,0},{3,1},{4,6},{5,7},{6,4},{7,5},{8,10},{9,11},{10,... | collective-permute-start | bytes 393224 | tf_op jit(solution)/shard_map/ppermute | solution.py:186
  27.4 0.0 collective-permute-done.4.other_out
  27.4 3.5 %collective-permute-done.6.refs_1_ = bf16[64,1024]{1,0:T(8,128)(2,1)S(1)} collective-permute-done((bf16[64,1024]{1,0:T(8,128)(2,1)S(1)}, bf16[64,1024]{1,0:T(8,128)(2,1)S(1)}, u32[]{:S(2)}, u32[]{:S(2)}) %collective-permute-start.6) | collective-permute-done | bytes 131104 | tf_op jit(solution)/shard_map/ppermute | solution.py:186
  30.9 0.0 collective-permute-done.3.other_qkv
  30.9 0.0 copy-done.6
  30.9 0.0 copy-done.9
  30.9 0.0 copy-start.4
  30.9 0.0 copy-start.7
  30.9 2.6 %attend.1 = bf16[128,512]{1,0:T(8,128)(2,1)S(1)} custom-call(f32[1,1024]{1,0:T(1,128)S(1)} %bitcast.24, bf16[128,128]{1,0:T(8,128)(2,1)S(1)} %copy-done.6, bf16[3,256,1024]{2,1,0:T(8,128)(2,1)S(1)} %copy-done.1, bf16[3,256,1024]{2,1,0:T(8,128)(2,1)S(1)} %collective-permute-done.3.other_qkv, bf16[256,1024]{1,0:T(8,128)(2,1)S(1)} %copy-done.2, ...), custom_call_target="tpu_custom_call" | custom-call | flops 268435456 | bytes 4624384 | tf_op jit(solution)/shard_map/attend/pallas_call | solution.py:167
  33.5 11.4 %all_to_all.11 = bf16[16,8,512]{2,1,0:T(8,128)(2,1)S(1)} all-to-all(bf16[16,8,512]{2,1,0:T(8,128)(2,1)S(1)} %bitcast.16), channel_id=1, replica_groups={{0,2,4,6,8,10,12,14,16,18,20,22,24,26,28,30},{1,3,5,7,9,11,13,15,17,19,..., dimensions={0} | all-to-all | bytes 262144 | tf_op jit(solution)/shard_map/all_to_all | solution.py:189
  45.0 0.0 copy-done.4
  45.0 0.0 copy-done.7
  45.0 0.8 %restore.1 = bf16[4,16,1024]{2,1,0:T(8,128)(2,1)} custom-call(bf16[128,512]{1,0:T(8,128)(2,1)S(1)} %bitcast.14, bf16[2,32,128]{2,1,0:T(8,128)(2,1)S(1)} %copy-done.7, bf16[4,16,1024]{2,1,0:T(8,128)(2,1)S(1)} %bitcast.20), custom_call_target="tpu_custom_call" | custom-call | bytes 409600 | tf_op jit(solution)/shard_map/restore/pallas_call | solution.py:167
  (1 shorter events, 0.0 us)
Async XLA Ops:
  0.0 4.9 %collective-permute-start = (bf16[64,1024]{1,0:T(8,128)(2,1)}, bf16[64,1024]{1,0:T(8,128)(2,1)S(1)}, u32[]{:S(2)}, u32[]{:S(2)}) collective-permute-start(bf16[64,1024]{1,0:T(8,128)(2,1)} %bitcast.17), channel_id=1, source_target_pairs={{0,1},{1,0},{2,3},{3,2},{4,5},{5,4},{6,7},{7,6},{8,9},{9,8},{10,11... | collective-permute-start | bytes 393224 | tf_op jit(solution)/shard_map/ppermute | solution.py:186
  0.5 6.9 %collective-permute-start.1 = (bf16[64,1024]{1,0:T(8,128)(2,1)}, bf16[64,1024]{1,0:T(8,128)(2,1)S(1)}, u32[]{:S(2)}, u32[]{:S(2)}) collective-permute-start(bf16[64,1024]{1,0:T(8,128)(2,1)} %bitcast.18), channel_id=1, source_target_pairs={{0,2},{1,3},{2,0},{3,1},{4,6},{5,7},{6,4},{7,5},{8,10},{9,11},{10,... | collective-permute-start | bytes 393224 | tf_op jit(solution)/shard_map/ppermute | solution.py:186
  2.9 22.2 %collective-permute-start.5 = (bf16[3,256,1024]{2,1,0:T(8,128)(2,1)}, bf16[3,256,1024]{2,1,0:T(8,128)(2,1)S(1)}, u32[]{:S(2)}, u32[]{:S(2)}) collective-permute-start(bf16[3,256,1024]{2,1,0:T(8,128)(2,1)} %own_ref.1), channel_id=1, source_target_pairs={{0,1},{1,0},{2,3},{3,2},{4,5},{5,4},{6,7},{7,6},{8,9},{9,8},{10,11... | collective-permute-start | bytes 4718600 | tf_op jit(solution)/shard_map/ppermute | solution.py:186
  3.2 0.9 %copy-start.3 = (bf16[4,1,16,1024]{3,2,1,0:T(8,128)(2,1)S(1)}, bf16[4,1,16,1024]{3,2,1,0:T(8,128)(2,1)}, u32[]{:S(2)}) copy-start(bf16[4,1,16,1024]{3,2,1,0:T(8,128)(2,1)} %param.10) | copy-start | bytes 393220
  4.1 0.7 %copy-start.8 = (f32[1024]{0:T(1024)S(1)}, f32[1024]{0:T(1024)}, u32[]{:S(2)}) copy-start(f32[1024]{0:T(1024)} %param.11) | copy-start | bytes 12292
  4.8 3.9 %slice-start = ((s8[4718592]{0:T(1024)(128)(4,1)}), s8[4194304]{0:T(1024)(128)(4,1)S(1)}, s32[]{:S(2)}) async-start(s8[4718592]{0:T(1024)(128)(4,1)} %bitcast.11), calls=%async_computation.2 | async-start | bytes 8388608
  4.9 3.8 %slice-start.1 = ((s8[4718592]{0:T(1024)(128)(4,1)}), s8[524288]{0:T(1024)(128)(4,1)S(1)}, s32[]{:S(2)}) async-start(s8[4718592]{0:T(1024)(128)(4,1)} %bitcast.11), calls=%async_computation.3 | async-start | bytes 1048576
  4.9 3.8 %copy-start.5 = (bf16[256,256]{1,0:T(8,128)(2,1)S(1)}, bf16[256,256]{1,0:T(8,128)(2,1)}, u32[]{:S(2)}) copy-start(bf16[256,256]{1,0:T(8,128)(2,1)} %constant.6.clone.order_ref) | copy-start | bytes 393220
  7.3 1.3 %collective-permute-start.2 = (bf16[64,1024]{1,0:T(8,128)(2,1)S(1)}, bf16[64,1024]{1,0:T(8,128)(2,1)S(1)}, u32[]{:S(2)}, u32[]{:S(2)}) collective-permute-start(bf16[64,1024]{1,0:T(8,128)(2,1)S(1)} %collective-permute-done.1.refs_1_), channel_id=1, source_target_pairs={{0,1},{1,0},{2,3},{3,2},{4,5},{5,4},{6,7},{7,6},{8,9},{9,8},{10,11... | collective-permute-start | bytes 393224 | tf_op jit(solution)/shard_map/ppermute | solution.py:186
  8.7 2.0 %copy-start.1 = (bf16[3,256,1024]{2,1,0:T(8,128)(2,1)S(1)}, bf16[3,256,1024]{2,1,0:T(8,128)(2,1)}, u32[]{:S(2)}) copy-start(bf16[3,256,1024]{2,1,0:T(8,128)(2,1)} %own_qkv.1) | copy-start | bytes 4718596
  8.7 2.2 %copy-start.2 = (bf16[256,1024]{1,0:T(8,128)(2,1)S(1)}, bf16[256,1024]{1,0:T(8,128)(2,1)}, u32[]{:S(2)}) copy-start(bf16[256,1024]{1,0:T(8,128)(2,1)} %own_out.1) | copy-start | bytes 1572868
  8.7 16.5 %copy-start = (bf16[3,256,1024]{2,1,0:T(8,128)(2,1)S(1)}, bf16[3,256,1024]{2,1,0:T(8,128)(2,1)}, u32[]{:S(2)}) copy-start(bf16[3,256,1024]{2,1,0:T(8,128)(2,1)} %own_ref.1) | copy-start | bytes 4718596
  10.7 20.2 %collective-permute-start.3 = (bf16[3,256,1024]{2,1,0:T(8,128)(2,1)S(1)}, bf16[3,256,1024]{2,1,0:T(8,128)(2,1)S(1)}, u32[]{:S(2)}, u32[]{:S(2)}) collective-permute-start(bf16[3,256,1024]{2,1,0:T(8,128)(2,1)S(1)} %copy-done.1), channel_id=1, source_target_pairs={{0,1},{1,0},{2,3},{3,2},{4,5},{5,4},{6,7},{7,6},{8,9},{9,8},{10,11... | collective-permute-start | bytes 4718600 | tf_op jit(solution)/shard_map/ppermute | solution.py:186
  10.9 16.5 %collective-permute-start.4 = (bf16[256,1024]{1,0:T(8,128)(2,1)S(1)}, bf16[256,1024]{1,0:T(8,128)(2,1)S(1)}, u32[]{:S(2)}, u32[]{:S(2)}) collective-permute-start(bf16[256,1024]{1,0:T(8,128)(2,1)S(1)} %copy-done.2), channel_id=1, source_target_pairs={{0,1},{1,0},{2,3},{3,2},{4,5},{5,4},{6,7},{7,6},{8,9},{9,8},{10,11... | collective-permute-start | bytes 1572872 | tf_op jit(solution)/shard_map/ppermute | solution.py:186
  25.2 5.7 %copy-start.6 = (bf16[128,128]{1,0:T(8,128)(2,1)S(1)}, bf16[128,128]{1,0:T(8,128)(2,1)}, u32[]{:S(2)}) copy-start(bf16[128,128]{1,0:T(8,128)(2,1)} %constant.7.clone.order_ref) | copy-start | bytes 98308
  25.2 5.7 %copy-start.9 = (f32[1024]{0:T(1024)S(1)}, f32[1024]{0:T(1024)}, u32[]{:S(2)}) copy-start(f32[1024]{0:T(1024)} %param.14) | copy-start | bytes 12292
  25.9 5.0 %collective-permute-start.6 = (bf16[64,1024]{1,0:T(8,128)(2,1)S(1)}, bf16[64,1024]{1,0:T(8,128)(2,1)S(1)}, u32[]{:S(2)}, u32[]{:S(2)}) collective-permute-start(bf16[64,1024]{1,0:T(8,128)(2,1)S(1)} %temporal.1.refs_0_), channel_id=1, source_target_pairs={{0,2},{1,3},{2,0},{3,1},{4,6},{5,7},{6,4},{7,5},{8,10},{9,11},{10,... | collective-permute-start | bytes 393224 | tf_op jit(solution)/shard_map/ppermute | solution.py:186
  30.9 14.1 %copy-start.4 = (bf16[4,1,16,1024]{3,2,1,0:T(8,128)(2,1)S(1)}, bf16[4,1,16,1024]{3,2,1,0:T(8,128)(2,1)}, u32[]{:S(2)}) copy-start(bf16[4,1,16,1024]{3,2,1,0:T(8,128)(2,1)} %param.10) | copy-start | bytes 393220
  30.9 14.1 %copy-start.7 = (bf16[2,32,128]{2,1,0:T(8,128)(2,1)S(1)}, bf16[2,32,128]{2,1,0:T(8,128)(2,1)}, u32[]{:S(2)}) copy-start(bf16[2,32,128]{2,1,0:T(8,128)(2,1)} %constant.8.clone.order_ref) | copy-start | bytes 49156

commit v3 on v2

--- a/solution.py
+++ b/solution.py
@@ -40,20 +40,15 @@
         self.down_views = views // 2 * orbit
         self.down_rows = self.down_views * self.pixels
         self.send_rows = views * self.pixels
-        back = views // 2 * self.ncol
-        self.lanes = next(n for n in (1, 2, 4, 8) if back * n % 8 == 0)
-        self.back_rows, self.back_width = back * self.lanes, chans // self.lanes
+        self.peers = orbit * self.x
+        self.back = views // 2 * self.ncol
+        self.lanes = next(n for n in (1, 2, 4, 8) if self.back * n % 8 == 0)
+        self.back_rows, self.back_width = self.back * self.lanes, chans // self.lanes
 
     def send_order(self):
-        o, core, odd, pair, r, c = np.indices((self.orbit, CORES, 2, self.views // 2, self.x, self.ncol))
+        o, core, odd, r, pair, c = np.indices((self.orbit, CORES, 2, self.x, self.views // 2, self.ncol))
         row, view, col = r * CORES + core, 2 * pair + odd, o * self.ncol + c
         return picks((row * self.views + view) * self.cols + col, self.space * self.views * self.cols)
-
-    def back_order(self):
-        o, r, lane, t, c = np.indices((self.orbit, self.x, self.lanes, self.views // 2, self.ncol))
-        view = o * (self.views // 2) + t
-        source = lane * self.down_rows + (view * self.x + r) * self.ncol + c
-        return picks(source, self.lanes * self.down_rows)
 
     def end_order(self):
         sender, _, lane, view, c = np.indices((self.orbit, self.x, self.lanes, self.views // 2, self.ncol))
@@ -105,19 +100,27 @@
 def temporal_kernel(plan, got_ref, own_ref, other_ref, out_ref):
     core = lax.rem(lax.axis_index("space"), CORES)
     half, depth = plan.send_rows // 2, plan.slice_chans
+    row = lax.broadcasted_iota(jnp.int32, (plan.down_rows, 1), 0)
+    first = (row & (plan.back - 1)) < plan.ncol
     total = None
     for index, weight_ref in ((core, own_ref), (1 - core, other_ref)):
         block = got_ref[:, index].astype(F32)
         even = block[:, :half].reshape(plan.down_rows, depth)
         odd = block[:, half:].reshape(plan.down_rows, depth)
-        before = pltpu.roll(odd, plan.pixels, 0)
+        before = jnp.where(first, pltpu.roll(odd, half - plan.back + plan.ncol, 0), pltpu.roll(odd, plan.ncol, 0))
         for k, rows in enumerate((before, even, odd)):
             part = dot(rows.astype(BF16), weight_ref[k])
             total = part if total is None else total + part
     out_ref[...] = total.astype(BF16)
 
 
-def attend_kernel(plan, gain_ref, order_ref, own_qkv, other_qkv, own_out, other_out, *refs):
+def turn_kernel(own_ref, other_ref, out_ref):
+    kinds, depth, chans = own_ref.shape
+    for k, ref in enumerate((own_ref, other_ref)):
+        out_ref[k] = ref[...].reshape(kinds * depth, chans).T
+
+
+def attend_kernel(plan, gain_ref, qkv_ref, own_out, other_out, *refs):
     down_refs, out_ref = refs[:-1], refs[-1]
     rows, depth = plan.down_rows, plan.slice_chans
     heads = depth // HD
@@ -126,30 +129,42 @@
         down = down + ref[...].astype(F32)
     down = down.astype(BF16).astype(F32)
     normed = rms_scale(down, gain_ref[...]).astype(BF16)
-    lane_head = lax.broadcasted_iota(jnp.int32, (1, depth), 1) >> (HD.bit_length() - 1)
-    low = plan.pixels - 1
-    row = lax.broadcasted_iota(jnp.int32, (heads * rows, 1), 0) & low
-    column = lax.broadcasted_iota(jnp.int32, (1, rows), 1) & low
-    same = row == column
+    channel_head = lax.broadcasted_iota(jnp.int32, (1, depth), 1) >> (HD.bit_length() - 1)
+    key_head = lax.broadcasted_iota(jnp.int32, (1, heads * rows), 1) >> (rows.bit_length() - 1)
+    key_row_head = lax.broadcasted_iota(jnp.int32, (heads * rows, 1), 0) >> (rows.bit_length() - 1)
+    spread = jnp.where(key_row_head == channel_head, 1.0, 0.0).astype(BF16)
+
+    def by_head(block):
+        wide = block.astype(F32)
+        return jnp.concatenate([jnp.where(channel_head == h, wide, 0.0) for h in range(heads)]).astype(BF16)
+
+    def pixel(number):
+        return (number & (plan.ncol - 1)) + ((number >> (plan.back.bit_length() - 1)) & (plan.x - 1)) * plan.ncol
+
+    query_pixel = pixel(lax.broadcasted_iota(jnp.int32, (rows, 1), 0))
+    key_pixel = pixel(lax.broadcasted_iota(jnp.int32, (1, heads * rows), 1) & (rows - 1))
+    same = query_pixel == key_pixel
     first = lax.axis_index("space") < CORES
     projected = jnp.where(first, 1.0, 0.0) * down
-    for qkv_ref, weight_ref in ((own_qkv, own_out), (other_qkv, other_out)):
-        query, key, value = [dot_trans(normed, qkv_ref[k]).astype(BF16) for k in range(3)]
-        wide = query.astype(F32)
-        query = jnp.concatenate([jnp.where(lane_head == h, wide, 0.0) for h in range(heads)]).astype(BF16)
-        scores = dot_trans(query, key) * (HD**-0.5)
-        top = jnp.max(jnp.where(same, scores, -jnp.inf), axis=-1, keepdims=True)
-        weights = jnp.where(same, jnp.exp(scores - top), 0.0)
-        probs = (weights / jnp.sum(weights, axis=-1, keepdims=True)).astype(BF16)
-        found = dot(probs, value)
-        mixed = found[:rows]
-        for h in range(1, heads):
-            mixed = jnp.where(lane_head == h, found[h * rows : (h + 1) * rows], mixed)
-        projected = projected + dot(mixed.astype(BF16), weight_ref[...])
-    projected = projected.astype(BF16)
+    both = range(CORES)
+    qkv = [dot(normed, qkv_ref[k]).astype(BF16) for k in both]
+    keys = [by_head(qkv[k][:, depth : 2 * depth]) for k in both]
+    values = [by_head(qkv[k][:, 2 * depth :]) for k in both]
+    scores = [dot_trans(qkv[k][:, :depth], keys[k]) * (HD**-0.5) for k in both]
+    weights = []
+    for score in scores:
+        score = jnp.where(same, score, -jnp.inf)
+        top = None
+        for h in range(heads):
+            peak = jnp.max(jnp.where(key_head == h, score, -jnp.inf), axis=-1, keepdims=True)
+            top = peak if h == 0 else jnp.where(key_head >= h, peak, top)
+        weights.append(jnp.exp(score - top).astype(BF16))
+    mixed = [(dot(w, v) / dot(w, spread)).astype(BF16) for w, v in zip(weights, values)]
+    projected = projected + dot(mixed[0], own_out[...]) + dot(mixed[1], other_out[...])
     width = plan.back_width
-    stacked = jnp.concatenate([projected[:, k * width : (k + 1) * width] for k in range(plan.lanes)])
-    out_ref[...] = dot(order_ref[...], stacked).astype(BF16)
+    parts = [projected[:, k * width : (k + 1) * width] for k in range(plan.lanes)]
+    parts = [part.reshape(plan.peers, plan.back, width) for part in parts]
+    out_ref[...] = jnp.concatenate(parts, axis=1).reshape(plan.peers * plan.back_rows, width).astype(BF16)
 
 
 def end_kernel(plan, got_ref, order_ref, latents_ref, out_ref):
@@ -170,7 +185,7 @@
         in_specs=[pl.BlockSpec(memory_space=space)] * len(args),
         out_specs=[pl.BlockSpec(memory_space=pltpu.VMEM)] * len(outs),
         scratch_shapes=list(scratch),
-        compiler_params=pltpu.CompilerParams(vmem_limit_bytes=40 * 2**20),
+        compiler_params=pltpu.CompilerParams(vmem_limit_bytes=16 * 2**20),
         cost_estimate=pl.CostEstimate(flops=flops, bytes_accessed=moved, transcendentals=0),
         name=name,
     )(*args)
@@ -194,9 +209,9 @@
     own = latents.reshape(views * cols, chans)
     far = [swap(own, x * CORES) for x in range(1, plan.x)]
     near = swap(own, 1)
-    (normed,) = call(norm_kernel, "norm_own", [own.shape], (conv_gain, own), flops=6 * 10**9)
-    normed, near, far = lax.optimization_barrier((normed, near, far))
-    other_temporal = swap(temporal_weight, 1)
+    (normed,) = call(norm_kernel, "norm_own", [own.shape], (conv_gain, own), flops=60 * 10**9)
+    far, near, normed = lax.optimization_barrier((far, near, normed))
+    other_temporal, other_qkv, other_out = [swap(w, 1) for w in (temporal_weight, qkv_weight, out_weight)]
     across = [swap(block, 1) for block in far]
     ready = call(norm_kernel, "norm", [own.shape] * plan.x, (conv_gain, near, *far), flops=6 * 10**9)
 
@@ -209,8 +224,8 @@
         [pltpu.VMEM((space, views * cols, chans), BF16)],
         flops=2 * 9 * count * chans * plan.slice_chans,
     )
-    activated, qkv, out = lax.optimization_barrier((activated, qkv_weight, out_weight))
-    other_qkv, other_out = swap(qkv, 1), swap(out, 1)
+    swapped = (other_temporal, other_qkv, other_out)
+    activated, (other_temporal, other_qkv, other_out) = lax.optimization_barrier((activated, swapped))
     got = exchange(activated.reshape(orbit * CORES, plan.send_rows, plan.slice_chans), by_core)
     (down,) = call(
         functools.partial(temporal_kernel, plan),
@@ -219,13 +234,21 @@
         (got.reshape(orbit, CORES, plan.send_rows, plan.slice_chans), temporal_weight, other_temporal),
         flops=2 * 6 * plan.down_rows * chans * plan.slice_chans,
     )
+    down, own_qkv, other_qkv = lax.optimization_barrier((down, qkv_weight, other_qkv))
     downs = [down] + [swap(down, x * CORES) for x in range(1, plan.x)]
-    peers = orbit * plan.x
+    (qkv,) = call(
+        turn_kernel,
+        "turn",
+        [(2, chans, 3 * plan.slice_chans)],
+        (own_qkv, other_qkv),
+        flops=6 * 10**9,
+    )
+    peers = plan.peers
     (back,) = call(
         functools.partial(attend_kernel, plan),
         "attend",
         [(peers * plan.back_rows, plan.back_width)],
-        (attn_gain, plan.back_order(), qkv_weight, other_qkv, out_weight, other_out, *downs),
+        (attn_gain, qkv, out_weight, other_out, *downs),
         flops=2 * 8 * plan.down_rows * chans * plan.slice_chans,
     )
     got = exchange(back.reshape(peers, plan.back_rows, plan.back_width), by_x)

time: 46 us -> 44 us (0.957)
  waiting for transfers between devices: 7.06 us -> 5.89 us
  blocking collectives: 25.3 us -> 24.7 us
    ppermute x7, waiting for transfers between devices: 7.06 us -> 5.89 us  [swap(): lax.ppermute(block, 'space', [(s, s ^ distance) for s in range(space)])]
    all_to_all x2, blocking collectives: 25.3 us -> 24.7 us  [exchange(): lax.all_to_all(blocks, ('orbit', 'space'), 0, 0, tiled=True, axis_index_g...]
    unnamed x24 -> x22, local copies, waits for them, and re-layouts: 1.65 us -> 2.04 us
    pallas_call x6 -> x7, Pallas kernels: 6.3 us -> 5.91 us  [call(): pl.pallas_call(kernel, out_shape=outs, in_specs=[pl.BlockSpec(memory_spac...]
  transfers between devices with their start and end apart: 7 -> 7, of which waited for: 3 -> 3; matrix products, arithmetic and copies ran while one was open for 0% -> 0% of each run, Pallas kernels for 6% -> 7%
where the time goes in v3:
time: 44 us; the launch traced here: 43.8 us
  blocking collectives  24.7 us (56%)
  Pallas kernels  5.91 us (13%)
  waiting for transfers between devices  5.89 us (13%)
  starting transfers between devices  5.13 us (12%)
  local copies, waits for them, and re-layouts  2.04 us (5%)
    all_to_all x2, blocking collectives, exchange(): lax.all_to_all(blocks, ('orbit', 'space'), 0, 0, tiled=True, axis_index_g...  24.7 us
    pallas_call x7, Pallas kernels, call(): pl.pallas_call(kernel, out_shape=outs, in_specs=[pl.BlockSpec(memory_spac...  5.91 us
    ppermute x7, waiting for transfers between devices, swap(): lax.ppermute(block, 'space', [(s, s ^ distance) for s in range(space)])  5.89 us
    ppermute x7, starting transfers between devices, swap(): lax.ppermute(block, 'space', [(s, s ^ distance) for s in range(space)])  5.13 us
    unnamed x22, local copies, waits for them, and re-layouts  2.04 us
  transfers between devices with their start and end apart: 7, of which 3 were waited for; matrix products, arithmetic and copies ran while one was open for 0% of the time, Pallas kernels for 7%

profile of v3, /device:TPU:0, one launch (start us, length us, event | category | flops | bytes accessed | tf_op | source)
XLA Modules:
  0.0 43.8 jit_solution(832105736674116927)
XLA Ops:
  0.0 2.9 %collective-permute-start = (bf16[64,1024]{1,0:T(8,128)(2,1)}, bf16[64,1024]{1,0:T(8,128)(2,1)S(1)}, u32[]{:S(2)}, u32[]{:S(2)}) collective-permute-start(bf16[64,1024]{1,0:T(8,128)(2,1)} %bitcast.17), channel_id=1, source_target_pairs={{0,2},{1,3},{2,0},{3,1},{4,6},{5,7},{6,4},{7,5},{8,10},{9,11},{10,... | collective-permute-start | bytes 393224 | tf_op jit(solution)/shard_map/ppermute | solution.py:201
  2.9 0.0 collective-permute-start.1
  2.9 0.5 %collective-permute-start.3 = (bf16[3,256,1024]{2,1,0:T(8,128)(2,1)}, bf16[3,256,1024]{2,1,0:T(8,128)(2,1)S(1)}, u32[]{:S(2)}, u32[]{:S(2)}) collective-permute-start(bf16[3,256,1024]{2,1,0:T(8,128)(2,1)} %own_ref.1), channel_id=1, source_target_pairs={{0,1},{1,0},{2,3},{3,2},{4,5},{5,4},{6,7},{7,6},{8,9},{9,8},{10,11... | collective-permute-start | bytes 4718600 | tf_op jit(solution)/shard_map/ppermute | solution.py:201
  3.5 0.0 collective-permute-start.4
  3.5 0.5 %collective-permute-start.5 = (bf16[256,1024]{1,0:T(8,128)(2,1)}, bf16[256,1024]{1,0:T(8,128)(2,1)S(1)}, u32[]{:S(2)}, u32[]{:S(2)}) collective-permute-start(bf16[256,1024]{1,0:T(8,128)(2,1)} %own_out.1), channel_id=1, source_target_pairs={{0,1},{1,0},{2,3},{3,2},{4,5},{5,4},{6,7},{7,6},{8,9},{9,8},{10,11... | collective-permute-start | bytes 1572872 | tf_op jit(solution)/shard_map/ppermute | solution.py:201
  4.0 0.0 slice-start
  4.0 0.0 copy-start.2
  4.0 1.1 %copy-done.2 = bf16[4,1,16,1024]{3,2,1,0:T(8,128)(2,1)S(1)} copy-done((bf16[4,1,16,1024]{3,2,1,0:T(8,128)(2,1)S(1)}, bf16[4,1,16,1024]{3,2,1,0:T(8,128)(2,1)}, u32[]{:S(2)}) %copy-start.2) | copy-done | bytes 131096
  5.0 0.0 copy-start.6
  5.0 0.9 %copy-done.6 = f32[1024]{0:T(1024)S(1)} copy-done((f32[1024]{0:T(1024)S(1)}, f32[1024]{0:T(1024)}, u32[]{:S(2)}) %copy-start.6) | copy-done | bytes 4120
  6.0 0.0 slice-start.1
  6.0 0.1 norm_own.1.refs_0_
  6.1 0.0 copy-start.4
  6.1 0.5 %collective-permute-done.refs_1_ = bf16[64,1024]{1,0:T(8,128)(2,1)S(1)} collective-permute-done((bf16[64,1024]{1,0:T(8,128)(2,1)}, bf16[64,1024]{1,0:T(8,128)(2,1)S(1)}, u32[]{:S(2)}, u32[]{:S(2)}) %collective-permute-start) | collective-permute-done | bytes 131104 | tf_op jit(solution)/shard_map/ppermute | solution.py:201
  6.6 0.0 collective-permute-done.1.refs_0_
  6.6 0.0 collective-permute-start.2
  6.7 0.2 norm.1
  6.8 2.4 %collective-permute-done.2.refs_3_ = bf16[64,1024]{1,0:T(8,128)(2,1)S(1)} collective-permute-done((bf16[64,1024]{1,0:T(8,128)(2,1)S(1)}, bf16[64,1024]{1,0:T(8,128)(2,1)S(1)}, u32[]{:S(2)}, u32[]{:S(2)}) %collective-permute-start.2) | collective-permute-done | bytes 131104 | tf_op jit(solution)/shard_map/ppermute | solution.py:201
  9.2 0.0 slice-done
  9.2 0.0 slice-done.1
  9.2 0.0 copy-done.4
  9.2 0.0 copy-start
  9.2 1.9 %conv.1 = bf16[256,256]{1,0:T(8,128)(2,1)S(1)} custom-call(f32[1,1024]{1,0:T(1,128)S(1)} %bitcast.23, bf16[3,3,256,1024]{3,2,1,0:T(8,128)(2,1)S(1)} %bitcast.12, bf16[256,256]{1,0:T(8,128)(2,1)S(1)} %copy-done.4, bf16[64,1024]{1,0:T(8,128)(2,1)S(1)} %norm_own.1.refs_0_, bf16[64,1024]{1,0:T(8,128)(2,1)S(1)} %get-tuple-element.20.refs_1_, ...), custom_call_target="tpu_custom_call" | custom-call | flops 1207959552 | bytes 5509120 | tf_op jit(solution)/shard_map/conv/pallas_call | solution.py:182
  11.1 0.0 collective-permute-done.5.other_out
  11.1 0.0 collective-permute-done.3.other_ref
  11.2 0.0 collective-permute-done.4.other_ref
  11.2 13.7 %all_to_all.10 = bf16[16,16,256]{2,1,0:T(8,128)(2,1)S(1)} all-to-all(bf16[16,16,256]{2,1,0:T(8,128)(2,1)S(1)} %bitcast.13), channel_id=1, replica_groups={{0,1,4,5,8,9,12,13,16,17,20,21,24,25,28,29},{2,3,6,7,10,11,14,15,18,19,..., dimensions={0} | all-to-all | bytes 262144 | tf_op jit(solution)/shard_map/all_to_all | solution.py:204
  24.8 0.0 copy-done
  24.8 0.0 copy-start.8
  24.8 0.7 %temporal.1.refs_0_ = bf16[64,1024]{1,0:T(8,128)(2,1)S(1)} custom-call(bf16[8,2,16,256]{3,2,1,0:T(8,128)(2,1)S(1)} %bitcast.15, bf16[3,256,1024]{2,1,0:T(8,128)(2,1)S(1)} %copy-done, bf16[3,256,1024]{2,1,0:T(8,128)(2,1)S(1)} %collective-permute-done.3.other_ref), custom_call_target="tpu_custom_call" | custom-call | flops 201326592 | bytes 3407872 | tf_op jit(solution)/shard_map/temporal/pallas_call | solution.py:182
  25.5 0.0 copy-start.1
  25.5 0.0 copy-start.7
  25.5 1.2 %collective-permute-start.6 = (bf16[64,1024]{1,0:T(8,128)(2,1)S(1)}, bf16[64,1024]{1,0:T(8,128)(2,1)S(1)}, u32[]{:S(2)}, u32[]{:S(2)}) collective-permute-start(bf16[64,1024]{1,0:T(8,128)(2,1)S(1)} %temporal.1.refs_0_), channel_id=1, source_target_pairs={{0,2},{1,3},{2,0},{3,1},{4,6},{5,7},{6,4},{7,5},{8,10},{9,11},{10,... | collective-permute-start | bytes 393224 | tf_op jit(solution)/shard_map/ppermute | solution.py:201
  26.7 0.0 copy-done.8
  26.7 0.9 %turn.1.qkv_ref = bf16[2,1024,768]{2,1,0:T(8,128)(2,1)S(1)} custom-call(bf16[3,256,1024]{2,1,0:T(8,128)(2,1)S(1)} %copy-done.8, bf16[3,256,1024]{2,1,0:T(8,128)(2,1)S(1)} %collective-permute-done.4.other_ref), custom_call_target="tpu_custom_call" | custom-call | flops 6000000000 | bytes 6291456 | tf_op jit(solution)/shard_map/turn/pallas_call | solution.py:182
  27.6 3.0 %collective-permute-done.6.refs_1_ = bf16[64,1024]{1,0:T(8,128)(2,1)S(1)} collective-permute-done((bf16[64,1024]{1,0:T(8,128)(2,1)S(1)}, bf16[64,1024]{1,0:T(8,128)(2,1)S(1)}, u32[]{:S(2)}, u32[]{:S(2)}) %collective-permute-start.6) | collective-permute-done | bytes 131104 | tf_op jit(solution)/shard_map/ppermute | solution.py:201
  30.6 0.0 copy-done.1
  30.6 0.0 copy-done.7
  30.6 0.0 copy-start.3
  30.6 0.0 copy-start.5
  30.6 1.4 %attend.1 = bf16[128,512]{1,0:T(8,128)(2,1)S(1)} custom-call(f32[1,1024]{1,0:T(1,128)S(1)} %bitcast.24, bf16[2,1024,768]{2,1,0:T(8,128)(2,1)S(1)} %turn.1.qkv_ref, bf16[256,1024]{1,0:T(8,128)(2,1)S(1)} %copy-done.1, bf16[256,1024]{1,0:T(8,128)(2,1)S(1)} %collective-permute-done.5.other_out, bf16[64,1024]{1,0:T(8,128)(2,1)S(1)} %temporal.1.refs_0_, ...), custom_call_target="tpu_custom_call" | custom-call | flops 268435456 | bytes 4591616 | tf_op jit(solution)/shard_map/attend/pallas_call | solution.py:182
  31.9 11.0 %all_to_all.11 = bf16[16,8,512]{2,1,0:T(8,128)(2,1)S(1)} all-to-all(bf16[16,8,512]{2,1,0:T(8,128)(2,1)S(1)} %bitcast.16), channel_id=1, replica_groups={{0,2,4,6,8,10,12,14,16,18,20,22,24,26,28,30},{1,3,5,7,9,11,13,15,17,19,..., dimensions={0} | all-to-all | bytes 262144 | tf_op jit(solution)/shard_map/all_to_all | solution.py:204
  43.0 0.0 copy-done.3
  43.0 0.0 copy-done.5
  43.0 0.8 %restore.1 = bf16[4,16,1024]{2,1,0:T(8,128)(2,1)} custom-call(bf16[128,512]{1,0:T(8,128)(2,1)S(1)} %bitcast.14, bf16[2,32,128]{2,1,0:T(8,128)(2,1)S(1)} %copy-done.5, bf16[4,16,1024]{2,1,0:T(8,128)(2,1)S(1)} %bitcast.20), custom_call_target="tpu_custom_call" | custom-call | bytes 409600 | tf_op jit(solution)/shard_map/restore/pallas_call | solution.py:182
  (1 shorter events, 0.0 us)
Async XLA Ops:
  0.0 6.6 %collective-permute-start = (bf16[64,1024]{1,0:T(8,128)(2,1)}, bf16[64,1024]{1,0:T(8,128)(2,1)S(1)}, u32[]{:S(2)}, u32[]{:S(2)}) collective-permute-start(bf16[64,1024]{1,0:T(8,128)(2,1)} %bitcast.17), channel_id=1, source_target_pairs={{0,2},{1,3},{2,0},{3,1},{4,6},{5,7},{6,4},{7,5},{8,10},{9,11},{10,... | collective-permute-start | bytes 393224 | tf_op jit(solution)/shard_map/ppermute | solution.py:201
  2.9 3.7 %collective-permute-start.1 = (bf16[64,1024]{1,0:T(8,128)(2,1)}, bf16[64,1024]{1,0:T(8,128)(2,1)S(1)}, u32[]{:S(2)}, u32[]{:S(2)}) collective-permute-start(bf16[64,1024]{1,0:T(8,128)(2,1)} %bitcast.18), channel_id=1, source_target_pairs={{0,1},{1,0},{2,3},{3,2},{4,5},{5,4},{6,7},{7,6},{8,9},{9,8},{10,11... | collective-permute-start | bytes 393224 | tf_op jit(solution)/shard_map/ppermute | solution.py:201
  2.9 8.2 %collective-permute-start.3 = (bf16[3,256,1024]{2,1,0:T(8,128)(2,1)}, bf16[3,256,1024]{2,1,0:T(8,128)(2,1)S(1)}, u32[]{:S(2)}, u32[]{:S(2)}) collective-permute-start(bf16[3,256,1024]{2,1,0:T(8,128)(2,1)} %own_ref.1), channel_id=1, source_target_pairs={{0,1},{1,0},{2,3},{3,2},{4,5},{5,4},{6,7},{7,6},{8,9},{9,8},{10,11... | collective-permute-start | bytes 4718600 | tf_op jit(solution)/shard_map/ppermute | solution.py:201
  3.5 7.7 %collective-permute-start.4 = (bf16[3,256,1024]{2,1,0:T(8,128)(2,1)}, bf16[3,256,1024]{2,1,0:T(8,128)(2,1)S(1)}, u32[]{:S(2)}, u32[]{:S(2)}) collective-permute-start(bf16[3,256,1024]{2,1,0:T(8,128)(2,1)} %own_ref.2), channel_id=1, source_target_pairs={{0,1},{1,0},{2,3},{3,2},{4,5},{5,4},{6,7},{7,6},{8,9},{9,8},{10,11... | collective-permute-start | bytes 4718600 | tf_op jit(solution)/shard_map/ppermute | solution.py:201
  3.5 7.7 %collective-permute-start.5 = (bf16[256,1024]{1,0:T(8,128)(2,1)}, bf16[256,1024]{1,0:T(8,128)(2,1)S(1)}, u32[]{:S(2)}, u32[]{:S(2)}) collective-permute-start(bf16[256,1024]{1,0:T(8,128)(2,1)} %own_out.1), channel_id=1, source_target_pairs={{0,1},{1,0},{2,3},{3,2},{4,5},{5,4},{6,7},{7,6},{8,9},{9,8},{10,11... | collective-permute-start | bytes 1572872 | tf_op jit(solution)/shard_map/ppermute | solution.py:201
  4.0 5.2 %slice-start = ((s8[4718592]{0:T(1024)(128)(4,1)}), s8[4194304]{0:T(1024)(128)(4,1)S(1)}, s32[]{:S(2)}) async-start(s8[4718592]{0:T(1024)(128)(4,1)} %bitcast.11), calls=%async_computation.2 | async-start | bytes 8388608
  4.0 1.1 %copy-start.2 = (bf16[4,1,16,1024]{3,2,1,0:T(8,128)(2,1)S(1)}, bf16[4,1,16,1024]{3,2,1,0:T(8,128)(2,1)}, u32[]{:S(2)}) copy-start(bf16[4,1,16,1024]{3,2,1,0:T(8,128)(2,1)} %param.9) | copy-start | bytes 393220
  5.0 0.9 %copy-start.6 = (f32[1024]{0:T(1024)S(1)}, f32[1024]{0:T(1024)}, u32[]{:S(2)}) copy-start(f32[1024]{0:T(1024)} %param.10) | copy-start | bytes 12292
  6.0 3.2 %slice-start.1 = ((s8[4718592]{0:T(1024)(128)(4,1)}), s8[524288]{0:T(1024)(128)(4,1)S(1)}, s32[]{:S(2)}) async-start(s8[4718592]{0:T(1024)(128)(4,1)} %bitcast.11), calls=%async_computation.3 | async-start | bytes 1048576
  6.1 3.1 %copy-start.4 = (bf16[256,256]{1,0:T(8,128)(2,1)S(1)}, bf16[256,256]{1,0:T(8,128)(2,1)}, u32[]{:S(2)}) copy-start(bf16[256,256]{1,0:T(8,128)(2,1)} %constant.4.clone.order_ref) | copy-start | bytes 393220
  6.6 2.5 %collective-permute-start.2 = (bf16[64,1024]{1,0:T(8,128)(2,1)S(1)}, bf16[64,1024]{1,0:T(8,128)(2,1)S(1)}, u32[]{:S(2)}, u32[]{:S(2)}) collective-permute-start(bf16[64,1024]{1,0:T(8,128)(2,1)S(1)} %collective-permute-done.refs_1_), channel_id=1, source_target_pairs={{0,1},{1,0},{2,3},{3,2},{4,5},{5,4},{6,7},{7,6},{8,9},{9,8},{10,11... | collective-permute-start | bytes 393224 | tf_op jit(solution)/shard_map/ppermute | solution.py:201
  9.2 15.7 %copy-start = (bf16[3,256,1024]{2,1,0:T(8,128)(2,1)S(1)}, bf16[3,256,1024]{2,1,0:T(8,128)(2,1)}, u32[]{:S(2)}) copy-start(bf16[3,256,1024]{2,1,0:T(8,128)(2,1)} %own_ref.1) | copy-start | bytes 4718596
  24.8 1.9 %copy-start.8 = (bf16[3,256,1024]{2,1,0:T(8,128)(2,1)S(1)}, bf16[3,256,1024]{2,1,0:T(8,128)(2,1)}, u32[]{:S(2)}) copy-start(bf16[3,256,1024]{2,1,0:T(8,128)(2,1)} %own_ref.2) | copy-start | bytes 4718596
  25.5 5.1 %copy-start.1 = (bf16[256,1024]{1,0:T(8,128)(2,1)S(1)}, bf16[256,1024]{1,0:T(8,128)(2,1)}, u32[]{:S(2)}) copy-start(bf16[256,1024]{1,0:T(8,128)(2,1)} %own_out.1) | copy-start | bytes 1572868
  25.5 5.1 %copy-start.7 = (f32[1024]{0:T(1024)S(1)}, f32[1024]{0:T(1024)}, u32[]{:S(2)}) copy-start(f32[1024]{0:T(1024)} %param.13) | copy-start | bytes 12292
  25.5 5.0 %collective-permute-start.6 = (bf16[64,1024]{1,0:T(8,128)(2,1)S(1)}, bf16[64,1024]{1,0:T(8,128)(2,1)S(1)}, u32[]{:S(2)}, u32[]{:S(2)}) collective-permute-start(bf16[64,1024]{1,0:T(8,128)(2,1)S(1)} %temporal.1.refs_0_), channel_id=1, source_target_pairs={{0,2},{1,3},{2,0},{3,1},{4,6},{5,7},{6,4},{7,5},{8,10},{9,11},{10,... | collective-permute-start | bytes 393224 | tf_op jit(solution)/shard_map/ppermute | solution.py:201
  30.6 12.4 %copy-start.3 = (bf16[4,1,16,1024]{3,2,1,0:T(8,128)(2,1)S(1)}, bf16[4,1,16,1024]{3,2,1,0:T(8,128)(2,1)}, u32[]{:S(2)}) copy-start(bf16[4,1,16,1024]{3,2,1,0:T(8,128)(2,1)} %param.9) | copy-start | bytes 393220
  30.6 12.4 %copy-start.5 = (bf16[2,32,128]{2,1,0:T(8,128)(2,1)S(1)}, bf16[2,32,128]{2,1,0:T(8,128)(2,1)}, u32[]{:S(2)}) copy-start(bf16[2,32,128]{2,1,0:T(8,128)(2,1)} %constant.5.clone.order_ref) | copy-start | bytes 49156

commit v4 on v3

--- a/solution.py
+++ b/solution.py
@@ -35,29 +35,33 @@
         self.orbit, self.space, self.views = orbit, space, views
         self.cols, self.chans, self.slice_chans = cols, chans, slice_chans
         self.x = space // CORES
-        self.ncol = cols // orbit
-        self.pixels = self.x * self.ncol
-        self.down_views = views // 2 * orbit
-        self.down_rows = self.down_views * self.pixels
+        share = cols // orbit
+        self.by_column = share % CORES == 0
+        self.ncol = share // CORES if self.by_column else share
+        self.rows = space if self.by_column else self.x
+        self.pixels = self.rows * self.ncol
+        self.pairs = views // 2
+        self.down_rows = self.pairs * orbit * self.pixels
         self.send_rows = views * self.pixels
-        self.peers = orbit * self.x
-        self.back = views // 2 * self.ncol
+        self.peers = orbit * self.rows
+        self.back = self.pairs * self.ncol
         self.lanes = next(n for n in (1, 2, 4, 8) if self.back * n % 8 == 0)
         self.back_rows, self.back_width = self.back * self.lanes, chans // self.lanes
 
+    def column(self, o, core, c):
+        return (o * CORES + core) * self.ncol + c if self.by_column else o * self.ncol + c
+
     def send_order(self):
-        o, core, odd, r, pair, c = np.indices((self.orbit, CORES, 2, self.x, self.views // 2, self.ncol))
-        row, view, col = r * CORES + core, 2 * pair + odd, o * self.ncol + c
-        return picks((row * self.views + view) * self.cols + col, self.space * self.views * self.cols)
+        o, core, odd, r, pair, c = np.indices((self.orbit, CORES, 2, self.rows, self.pairs, self.ncol))
+        row = r if self.by_column else r * CORES + core
+        source = (row * self.views + 2 * pair + odd) * self.cols + self.column(o, core, c)
+        return picks(source, self.space * self.views * self.cols)
 
     def end_order(self):
-        sender, _, lane, view, c = np.indices((self.orbit, self.x, self.lanes, self.views // 2, self.ncol))
-        target = view * self.cols + sender * self.ncol + c
-        parts = []
-        for k in range(self.lanes):
-            wanted = np.where(lane == k, target, -1).reshape(1, -1)
-            parts.append(wanted == np.arange(self.views // 2 * self.cols).reshape(-1, 1))
-        return jnp.asarray(np.stack(parts), BF16)
+        o, s, lane, view, c = np.indices((self.orbit, self.rows, self.lanes, self.pairs, self.ncol))
+        target = (lane * self.pairs + view) * self.cols + self.column(o, s % CORES, c)
+        count = self.lanes * self.pairs * self.cols
+        return jnp.asarray(target.reshape(1, -1) == np.arange(count).reshape(-1, 1), BF16)
 
 
 def norm_kernel(gain_ref, *refs):
@@ -139,7 +143,7 @@
         return jnp.concatenate([jnp.where(channel_head == h, wide, 0.0) for h in range(heads)]).astype(BF16)
 
     def pixel(number):
-        return (number & (plan.ncol - 1)) + ((number >> (plan.back.bit_length() - 1)) & (plan.x - 1)) * plan.ncol
+        return (number & (plan.ncol - 1)) + ((number >> (plan.back.bit_length() - 1)) & (plan.rows - 1)) * plan.ncol
 
     query_pixel = pixel(lax.broadcasted_iota(jnp.int32, (rows, 1), 0))
     key_pixel = pixel(lax.broadcasted_iota(jnp.int32, (1, heads * rows), 1) & (rows - 1))
@@ -168,9 +172,10 @@
 
 
 def end_kernel(plan, got_ref, order_ref, latents_ref, out_ref):
-    got = got_ref[...]
-    bottom = [dot(order_ref[k], got) for k in range(plan.lanes)]
-    bottom = jnp.concatenate(bottom, axis=1).astype(BF16).astype(F32)
+    rows = plan.pairs * plan.cols
+    bottom = dot(order_ref[...], got_ref[...])
+    bottom = jnp.concatenate([bottom[k * rows : (k + 1) * rows] for k in range(plan.lanes)], axis=1)
+    bottom = bottom.astype(BF16).astype(F32)
     for f in range(plan.views):
         block = bottom[(f // 2) * plan.cols : (f // 2 + 1) * plan.cols]
         out_ref[f] = (latents_ref[f].astype(F32) + block).astype(BF16)
@@ -251,7 +256,7 @@
         (attn_gain, qkv, out_weight, other_out, *downs),
         flops=2 * 8 * plan.down_rows * chans * plan.slice_chans,
     )
-    got = exchange(back.reshape(peers, plan.back_rows, plan.back_width), by_x)
+    got = exchange(back.reshape(peers, plan.back_rows, plan.back_width), None if plan.by_column else by_x)
     (restored,) = call(
         functools.partial(end_kernel, plan),
         "restore",

time: 44 us -> 43.5 us (0.989)
  blocking collectives: 24.7 us -> 24.1 us
    all_to_all x2, blocking collectives: 24.7 us -> 24.1 us  [exchange(): lax.all_to_all(blocks, ('orbit', 'space'), 0, 0, tiled=True, axis_index_g...]
where the time goes in v4:
time: 43.5 us; the launch traced here: 43.3 us
  blocking collectives  24.1 us (55%)
  Pallas kernels  5.97 us (14%)
  waiting for transfers between devices  5.89 us (14%)
  starting transfers between devices  5.13 us (12%)
  local copies, waits for them, and re-layouts  2.04 us (5%)
    all_to_all x2, blocking collectives, exchange(): lax.all_to_all(blocks, ('orbit', 'space'), 0, 0, tiled=True, axis_index_g...  24.1 us
    pallas_call x7, Pallas kernels, call(): pl.pallas_call(kernel, out_shape=outs, in_specs=[pl.BlockSpec(memory_spac...  5.97 us
    ppermute x7, waiting for transfers between devices, swap(): lax.ppermute(block, 'space', [(s, s ^ distance) for s in range(space)])  5.89 us
    ppermute x7, starting transfers between devices, swap(): lax.ppermute(block, 'space', [(s, s ^ distance) for s in range(space)])  5.13 us
    unnamed x22, local copies, waits for them, and re-layouts  2.04 us
  transfers between devices with their start and end apart: 7, of which 3 were waited for; matrix products, arithmetic and copies ran while one was open for 0% of the time, Pallas kernels for 7%

profile of v4, /device:TPU:0, one launch (start us, length us, event | category | flops | bytes accessed | tf_op | source)
XLA Modules:
  0.0 43.3 jit_solution(16651510335174608912)
XLA Ops:
  0.0 2.9 %collective-permute-start = (bf16[64,1024]{1,0:T(8,128)(2,1)}, bf16[64,1024]{1,0:T(8,128)(2,1)S(1)}, u32[]{:S(2)}, u32[]{:S(2)}) collective-permute-start(bf16[64,1024]{1,0:T(8,128)(2,1)} %bitcast.17), channel_id=1, source_target_pairs={{0,2},{1,3},{2,0},{3,1},{4,6},{5,7},{6,4},{7,5},{8,10},{9,11},{10,... | collective-permute-start | bytes 393224 | tf_op jit(solution)/shard_map/ppermute | solution.py:206
  2.9 0.0 collective-permute-start.1
  2.9 0.5 %collective-permute-start.3 = (bf16[3,256,1024]{2,1,0:T(8,128)(2,1)}, bf16[3,256,1024]{2,1,0:T(8,128)(2,1)S(1)}, u32[]{:S(2)}, u32[]{:S(2)}) collective-permute-start(bf16[3,256,1024]{2,1,0:T(8,128)(2,1)} %own_ref.1), channel_id=1, source_target_pairs={{0,1},{1,0},{2,3},{3,2},{4,5},{5,4},{6,7},{7,6},{8,9},{9,8},{10,11... | collective-permute-start | bytes 4718600 | tf_op jit(solution)/shard_map/ppermute | solution.py:206
  3.5 0.0 collective-permute-start.4
  3.5 0.5 %collective-permute-start.5 = (bf16[256,1024]{1,0:T(8,128)(2,1)}, bf16[256,1024]{1,0:T(8,128)(2,1)S(1)}, u32[]{:S(2)}, u32[]{:S(2)}) collective-permute-start(bf16[256,1024]{1,0:T(8,128)(2,1)} %own_out.1), channel_id=1, source_target_pairs={{0,1},{1,0},{2,3},{3,2},{4,5},{5,4},{6,7},{7,6},{8,9},{9,8},{10,11... | collective-permute-start | bytes 1572872 | tf_op jit(solution)/shard_map/ppermute | solution.py:206
  4.0 0.0 slice-start
  4.0 0.0 copy-start.2
  4.0 1.1 %copy-done.2 = bf16[4,1,16,1024]{3,2,1,0:T(8,128)(2,1)S(1)} copy-done((bf16[4,1,16,1024]{3,2,1,0:T(8,128)(2,1)S(1)}, bf16[4,1,16,1024]{3,2,1,0:T(8,128)(2,1)}, u32[]{:S(2)}) %copy-start.2) | copy-done | bytes 131096
  5.0 0.0 copy-start.6
  5.0 0.9 %copy-done.6 = f32[1024]{0:T(1024)S(1)} copy-done((f32[1024]{0:T(1024)S(1)}, f32[1024]{0:T(1024)}, u32[]{:S(2)}) %copy-start.6) | copy-done | bytes 4120
  6.0 0.0 slice-start.1
  6.0 0.1 norm_own.1.refs_0_
  6.1 0.0 copy-start.4
  6.1 0.5 %collective-permute-done.refs_1_ = bf16[64,1024]{1,0:T(8,128)(2,1)S(1)} collective-permute-done((bf16[64,1024]{1,0:T(8,128)(2,1)}, bf16[64,1024]{1,0:T(8,128)(2,1)S(1)}, u32[]{:S(2)}, u32[]{:S(2)}) %collective-permute-start) | collective-permute-done | bytes 131104 | tf_op jit(solution)/shard_map/ppermute | solution.py:206
  6.6 0.0 collective-permute-done.1.refs_0_
  6.6 0.0 collective-permute-start.2
  6.7 0.2 norm.1
  6.8 2.4 %collective-permute-done.2.refs_3_ = bf16[64,1024]{1,0:T(8,128)(2,1)S(1)} collective-permute-done((bf16[64,1024]{1,0:T(8,128)(2,1)S(1)}, bf16[64,1024]{1,0:T(8,128)(2,1)S(1)}, u32[]{:S(2)}, u32[]{:S(2)}) %collective-permute-start.2) | collective-permute-done | bytes 131104 | tf_op jit(solution)/shard_map/ppermute | solution.py:206
  9.2 0.0 slice-done
  9.2 0.0 slice-done.1
  9.2 0.0 copy-done.4
  9.2 0.0 copy-start
  9.2 1.9 %conv.1 = bf16[256,256]{1,0:T(8,128)(2,1)S(1)} custom-call(f32[1,1024]{1,0:T(1,128)S(1)} %bitcast.23, bf16[3,3,256,1024]{3,2,1,0:T(8,128)(2,1)S(1)} %bitcast.12, bf16[256,256]{1,0:T(8,128)(2,1)S(1)} %copy-done.4, bf16[64,1024]{1,0:T(8,128)(2,1)S(1)} %norm_own.1.refs_0_, bf16[64,1024]{1,0:T(8,128)(2,1)S(1)} %get-tuple-element.20.refs_1_, ...), custom_call_target="tpu_custom_call" | custom-call | flops 1207959552 | bytes 5509120 | tf_op jit(solution)/shard_map/conv/pallas_call | solution.py:187
  11.1 0.0 collective-permute-done.5.other_out
  11.1 0.0 collective-permute-done.3.other_ref
  11.2 0.0 collective-permute-done.4.other_ref
  11.2 13.7 %all_to_all.10 = bf16[16,16,256]{2,1,0:T(8,128)(2,1)S(1)} all-to-all(bf16[16,16,256]{2,1,0:T(8,128)(2,1)S(1)} %bitcast.13), channel_id=1, replica_groups={{0,1,4,5,8,9,12,13,16,17,20,21,24,25,28,29},{2,3,6,7,10,11,14,15,18,19,..., dimensions={0} | all-to-all | bytes 262144 | tf_op jit(solution)/shard_map/all_to_all | solution.py:209
  24.8 0.0 copy-done
  24.8 0.0 copy-start.8
  24.8 0.7 %temporal.1.refs_0_ = bf16[64,1024]{1,0:T(8,128)(2,1)S(1)} custom-call(bf16[8,2,16,256]{3,2,1,0:T(8,128)(2,1)S(1)} %bitcast.15, bf16[3,256,1024]{2,1,0:T(8,128)(2,1)S(1)} %copy-done, bf16[3,256,1024]{2,1,0:T(8,128)(2,1)S(1)} %collective-permute-done.3.other_ref), custom_call_target="tpu_custom_call" | custom-call | flops 201326592 | bytes 3407872 | tf_op jit(solution)/shard_map/temporal/pallas_call | solution.py:187
  25.5 0.0 copy-start.1
  25.5 0.0 copy-start.7
  25.5 1.2 %collective-permute-start.6 = (bf16[64,1024]{1,0:T(8,128)(2,1)S(1)}, bf16[64,1024]{1,0:T(8,128)(2,1)S(1)}, u32[]{:S(2)}, u32[]{:S(2)}) collective-permute-start(bf16[64,1024]{1,0:T(8,128)(2,1)S(1)} %temporal.1.refs_0_), channel_id=1, source_target_pairs={{0,2},{1,3},{2,0},{3,1},{4,6},{5,7},{6,4},{7,5},{8,10},{9,11},{10,... | collective-permute-start | bytes 393224 | tf_op jit(solution)/shard_map/ppermute | solution.py:206
  26.7 0.0 copy-done.8
  26.7 0.9 %turn.1.qkv_ref = bf16[2,1024,768]{2,1,0:T(8,128)(2,1)S(1)} custom-call(bf16[3,256,1024]{2,1,0:T(8,128)(2,1)S(1)} %copy-done.8, bf16[3,256,1024]{2,1,0:T(8,128)(2,1)S(1)} %collective-permute-done.4.other_ref), custom_call_target="tpu_custom_call" | custom-call | flops 6000000000 | bytes 6291456 | tf_op jit(solution)/shard_map/turn/pallas_call | solution.py:187
  27.6 3.0 %collective-permute-done.6.refs_1_ = bf16[64,1024]{1,0:T(8,128)(2,1)S(1)} collective-permute-done((bf16[64,1024]{1,0:T(8,128)(2,1)S(1)}, bf16[64,1024]{1,0:T(8,128)(2,1)S(1)}, u32[]{:S(2)}, u32[]{:S(2)}) %collective-permute-start.6) | collective-permute-done | bytes 131104 | tf_op jit(solution)/shard_map/ppermute | solution.py:206
  30.6 0.0 copy-done.1
  30.6 0.0 copy-done.7
  30.6 0.0 copy-start.3
  30.6 0.0 copy-start.5
  30.6 1.4 %attend.1 = bf16[256,256]{1,0:T(8,128)(2,1)S(1)} custom-call(f32[1,1024]{1,0:T(1,128)S(1)} %bitcast.24, bf16[2,1024,768]{2,1,0:T(8,128)(2,1)S(1)} %turn.1.qkv_ref, bf16[256,1024]{1,0:T(8,128)(2,1)S(1)} %copy-done.1, bf16[256,1024]{1,0:T(8,128)(2,1)S(1)} %collective-permute-done.5.other_out, bf16[64,1024]{1,0:T(8,128)(2,1)S(1)} %temporal.1.refs_0_, ...), custom_call_target="tpu_custom_call" | custom-call | flops 268435456 | bytes 4591616 | tf_op jit(solution)/shard_map/attend/pallas_call | solution.py:187
  32.0 10.5 %all_to_all.11 = bf16[32,8,256]{2,1,0:T(8,128)(2,1)S(1)} all-to-all(bf16[32,8,256]{2,1,0:T(8,128)(2,1)S(1)} %bitcast.16), channel_id=1, replica_groups=mesh['orbit'=8,'space'=4] {'orbit','space'}, dimensions={0} | all-to-all | bytes 262144 | tf_op jit(solution)/shard_map/all_to_all | solution.py:209
  42.5 0.0 copy-done.3
  42.5 0.0 copy-done.5
  42.5 0.8 %restore.1 = bf16[4,16,1024]{2,1,0:T(8,128)(2,1)} custom-call(bf16[256,256]{1,0:T(8,128)(2,1)S(1)} %bitcast.14, bf16[128,256]{1,0:T(8,128)(2,1)S(1)} %copy-done.5, bf16[4,16,1024]{2,1,0:T(8,128)(2,1)S(1)} %bitcast.20), custom_call_target="tpu_custom_call" | custom-call | bytes 458752 | tf_op jit(solution)/shard_map/restore/pallas_call | solution.py:187
  (1 shorter events, 0.0 us)
Async XLA Ops:
  0.0 6.6 %collective-permute-start = (bf16[64,1024]{1,0:T(8,128)(2,1)}, bf16[64,1024]{1,0:T(8,128)(2,1)S(1)}, u32[]{:S(2)}, u32[]{:S(2)}) collective-permute-start(bf16[64,1024]{1,0:T(8,128)(2,1)} %bitcast.17), channel_id=1, source_target_pairs={{0,2},{1,3},{2,0},{3,1},{4,6},{5,7},{6,4},{7,5},{8,10},{9,11},{10,... | collective-permute-start | bytes 393224 | tf_op jit(solution)/shard_map/ppermute | solution.py:206
  2.9 3.7 %collective-permute-start.1 = (bf16[64,1024]{1,0:T(8,128)(2,1)}, bf16[64,1024]{1,0:T(8,128)(2,1)S(1)}, u32[]{:S(2)}, u32[]{:S(2)}) collective-permute-start(bf16[64,1024]{1,0:T(8,128)(2,1)} %bitcast.18), channel_id=1, source_target_pairs={{0,1},{1,0},{2,3},{3,2},{4,5},{5,4},{6,7},{7,6},{8,9},{9,8},{10,11... | collective-permute-start | bytes 393224 | tf_op jit(solution)/shard_map/ppermute | solution.py:206
  2.9 8.2 %collective-permute-start.3 = (bf16[3,256,1024]{2,1,0:T(8,128)(2,1)}, bf16[3,256,1024]{2,1,0:T(8,128)(2,1)S(1)}, u32[]{:S(2)}, u32[]{:S(2)}) collective-permute-start(bf16[3,256,1024]{2,1,0:T(8,128)(2,1)} %own_ref.1), channel_id=1, source_target_pairs={{0,1},{1,0},{2,3},{3,2},{4,5},{5,4},{6,7},{7,6},{8,9},{9,8},{10,11... | collective-permute-start | bytes 4718600 | tf_op jit(solution)/shard_map/ppermute | solution.py:206
  3.5 7.7 %collective-permute-start.4 = (bf16[3,256,1024]{2,1,0:T(8,128)(2,1)}, bf16[3,256,1024]{2,1,0:T(8,128)(2,1)S(1)}, u32[]{:S(2)}, u32[]{:S(2)}) collective-permute-start(bf16[3,256,1024]{2,1,0:T(8,128)(2,1)} %own_ref.2), channel_id=1, source_target_pairs={{0,1},{1,0},{2,3},{3,2},{4,5},{5,4},{6,7},{7,6},{8,9},{9,8},{10,11... | collective-permute-start | bytes 4718600 | tf_op jit(solution)/shard_map/ppermute | solution.py:206
  3.5 7.7 %collective-permute-start.5 = (bf16[256,1024]{1,0:T(8,128)(2,1)}, bf16[256,1024]{1,0:T(8,128)(2,1)S(1)}, u32[]{:S(2)}, u32[]{:S(2)}) collective-permute-start(bf16[256,1024]{1,0:T(8,128)(2,1)} %own_out.1), channel_id=1, source_target_pairs={{0,1},{1,0},{2,3},{3,2},{4,5},{5,4},{6,7},{7,6},{8,9},{9,8},{10,11... | collective-permute-start | bytes 1572872 | tf_op jit(solution)/shard_map/ppermute | solution.py:206
  4.0 5.2 %slice-start = ((s8[4718592]{0:T(1024)(128)(4,1)}), s8[4194304]{0:T(1024)(128)(4,1)S(1)}, s32[]{:S(2)}) async-start(s8[4718592]{0:T(1024)(128)(4,1)} %bitcast.11), calls=%async_computation.2 | async-start | bytes 8388608
  4.0 1.1 %copy-start.2 = (bf16[4,1,16,1024]{3,2,1,0:T(8,128)(2,1)S(1)}, bf16[4,1,16,1024]{3,2,1,0:T(8,128)(2,1)}, u32[]{:S(2)}) copy-start(bf16[4,1,16,1024]{3,2,1,0:T(8,128)(2,1)} %param.9) | copy-start | bytes 393220
  5.0 0.9 %copy-start.6 = (f32[1024]{0:T(1024)S(1)}, f32[1024]{0:T(1024)}, u32[]{:S(2)}) copy-start(f32[1024]{0:T(1024)} %param.10) | copy-start | bytes 12292
  6.0 3.2 %slice-start.1 = ((s8[4718592]{0:T(1024)(128)(4,1)}), s8[524288]{0:T(1024)(128)(4,1)S(1)}, s32[]{:S(2)}) async-start(s8[4718592]{0:T(1024)(128)(4,1)} %bitcast.11), calls=%async_computation.3 | async-start | bytes 1048576
  6.1 3.1 %copy-start.4 = (bf16[256,256]{1,0:T(8,128)(2,1)S(1)}, bf16[256,256]{1,0:T(8,128)(2,1)}, u32[]{:S(2)}) copy-start(bf16[256,256]{1,0:T(8,128)(2,1)} %constant.4.clone.order_ref) | copy-start | bytes 393220
  6.6 2.5 %collective-permute-start.2 = (bf16[64,1024]{1,0:T(8,128)(2,1)S(1)}, bf16[64,1024]{1,0:T(8,128)(2,1)S(1)}, u32[]{:S(2)}, u32[]{:S(2)}) collective-permute-start(bf16[64,1024]{1,0:T(8,128)(2,1)S(1)} %collective-permute-done.refs_1_), channel_id=1, source_target_pairs={{0,1},{1,0},{2,3},{3,2},{4,5},{5,4},{6,7},{7,6},{8,9},{9,8},{10,11... | collective-permute-start | bytes 393224 | tf_op jit(solution)/shard_map/ppermute | solution.py:206
  9.2 15.7 %copy-start = (bf16[3,256,1024]{2,1,0:T(8,128)(2,1)S(1)}, bf16[3,256,1024]{2,1,0:T(8,128)(2,1)}, u32[]{:S(2)}) copy-start(bf16[3,256,1024]{2,1,0:T(8,128)(2,1)} %own_ref.1) | copy-start | bytes 4718596
  24.8 1.9 %copy-start.8 = (bf16[3,256,1024]{2,1,0:T(8,128)(2,1)S(1)}, bf16[3,256,1024]{2,1,0:T(8,128)(2,1)}, u32[]{:S(2)}) copy-start(bf16[3,256,1024]{2,1,0:T(8,128)(2,1)} %own_ref.2) | copy-start | bytes 4718596
  25.5 5.1 %copy-start.1 = (bf16[256,1024]{1,0:T(8,128)(2,1)S(1)}, bf16[256,1024]{1,0:T(8,128)(2,1)}, u32[]{:S(2)}) copy-start(bf16[256,1024]{1,0:T(8,128)(2,1)} %own_out.1) | copy-start | bytes 1572868
  25.5 5.1 %copy-start.7 = (f32[1024]{0:T(1024)S(1)}, f32[1024]{0:T(1024)}, u32[]{:S(2)}) copy-start(f32[1024]{0:T(1024)} %param.13) | copy-start | bytes 12292
  25.5 5.0 %collective-permute-start.6 = (bf16[64,1024]{1,0:T(8,128)(2,1)S(1)}, bf16[64,1024]{1,0:T(8,128)(2,1)S(1)}, u32[]{:S(2)}, u32[]{:S(2)}) collective-permute-start(bf16[64,1024]{1,0:T(8,128)(2,1)S(1)} %temporal.1.refs_0_), channel_id=1, source_target_pairs={{0,2},{1,3},{2,0},{3,1},{4,6},{5,7},{6,4},{7,5},{8,10},{9,11},{10,... | collective-permute-start | bytes 393224 | tf_op jit(solution)/shard_map/ppermute | solution.py:206
  30.6 11.9 %copy-start.3 = (bf16[4,1,16,1024]{3,2,1,0:T(8,128)(2,1)S(1)}, bf16[4,1,16,1024]{3,2,1,0:T(8,128)(2,1)}, u32[]{:S(2)}) copy-start(bf16[4,1,16,1024]{3,2,1,0:T(8,128)(2,1)} %param.9) | copy-start | bytes 393220
  30.6 11.9 %copy-start.5 = (bf16[128,256]{1,0:T(8,128)(2,1)S(1)}, bf16[128,256]{1,0:T(8,128)(2,1)}, u32[]{:S(2)}) copy-start(bf16[128,256]{1,0:T(8,128)(2,1)} %constant.5.clone.order_ref) | copy-start | bytes 196612

commit v5 on v4

--- a/solution.py
+++ b/solution.py
@@ -216,7 +216,7 @@
     near = swap(own, 1)
     (normed,) = call(norm_kernel, "norm_own", [own.shape], (conv_gain, own), flops=60 * 10**9)
     far, near, normed = lax.optimization_barrier((far, near, normed))
-    other_temporal, other_qkv, other_out = [swap(w, 1) for w in (temporal_weight, qkv_weight, out_weight)]
+    other_temporal, other_out = swap(temporal_weight, 1), swap(out_weight, 1)
     across = [swap(block, 1) for block in far]
     ready = call(norm_kernel, "norm", [own.shape] * plan.x, (conv_gain, near, *far), flops=6 * 10**9)
 
@@ -229,8 +229,9 @@
         [pltpu.VMEM((space, views * cols, chans), BF16)],
         flops=2 * 9 * count * chans * plan.slice_chans,
     )
-    swapped = (other_temporal, other_qkv, other_out)
-    activated, (other_temporal, other_qkv, other_out) = lax.optimization_barrier((activated, swapped))
+    swapped = (other_temporal, other_out)
+    activated, swapped, qkv = lax.optimization_barrier((activated, swapped, qkv_weight))
+    (other_temporal, other_out), other_qkv = swapped, swap(qkv, 1)
     got = exchange(activated.reshape(orbit * CORES, plan.send_rows, plan.slice_chans), by_core)
     (down,) = call(
         functools.partial(temporal_kernel, plan),

time: 43.5 us -> 43.2 us (level)
  waiting for transfers between devices: 5.89 us -> 4.85 us
  blocking collectives: 24.1 us -> 24.8 us
    ppermute x7, waiting for transfers between devices: 5.89 us -> 4.85 us  [swap(): lax.ppermute(block, 'space', [(s, s ^ distance) for s in range(space)])]
    all_to_all x2, blocking collectives: 24.1 us -> 24.8 us  [exchange(): lax.all_to_all(blocks, ('orbit', 'space'), 0, 0, tiled=True, axis_index_g...]
  transfers between devices with their start and end apart: 7 -> 7, of which waited for: 3 -> 3; matrix products, arithmetic and copies ran while one was open for 0% -> 0% of each run, Pallas kernels for 7% -> 9%
where the time goes in v5:
time: 43.2 us; the launch traced here: 43 us
  blocking collectives  24.8 us (57%)
  Pallas kernels  5.97 us (14%)
  starting transfers between devices  5.21 us (12%)
  waiting for transfers between devices  4.85 us (11%)
  local copies, waits for them, and re-layouts  2.05 us (5%)
    all_to_all x2, blocking collectives, exchange(): lax.all_to_all(blocks, ('orbit', 'space'), 0, 0, tiled=True, axis_index_g...  24.8 us
    pallas_call x7, Pallas kernels, call(): pl.pallas_call(kernel, out_shape=outs, in_specs=[pl.BlockSpec(memory_spac...  5.97 us
    ppermute x7, starting transfers between devices, swap(): lax.ppermute(block, 'space', [(s, s ^ distance) for s in range(space)])  5.21 us
    ppermute x7, waiting for transfers between devices, swap(): lax.ppermute(block, 'space', [(s, s ^ distance) for s in range(space)])  4.85 us
    unnamed x22, local copies, waits for them, and re-layouts  2.05 us
  transfers between devices with their start and end apart: 7, of which 3 were waited for; matrix products, arithmetic and copies ran while one was open for 0% of the time, Pallas kernels for 9%

profile of v5, /device:TPU:0, one launch (start us, length us, event | category | flops | bytes accessed | tf_op | source)
XLA Modules:
  0.0 43.0 jit_solution(13608796791316391336)
XLA Ops:
  0.0 2.9 %collective-permute-start = (bf16[64,1024]{1,0:T(8,128)(2,1)}, bf16[64,1024]{1,0:T(8,128)(2,1)S(1)}, u32[]{:S(2)}, u32[]{:S(2)}) collective-permute-start(bf16[64,1024]{1,0:T(8,128)(2,1)} %bitcast.17), channel_id=1, source_target_pairs={{0,2},{1,3},{2,0},{3,1},{4,6},{5,7},{6,4},{7,5},{8,10},{9,11},{10,... | collective-permute-start | bytes 393224 | tf_op jit(solution)/shard_map/ppermute | solution.py:206
  2.9 0.0 collective-permute-start.1
  2.9 0.5 %collective-permute-start.3 = (bf16[3,256,1024]{2,1,0:T(8,128)(2,1)}, bf16[3,256,1024]{2,1,0:T(8,128)(2,1)S(1)}, u32[]{:S(2)}, u32[]{:S(2)}) collective-permute-start(bf16[3,256,1024]{2,1,0:T(8,128)(2,1)} %own_ref.1), channel_id=1, source_target_pairs={{0,1},{1,0},{2,3},{3,2},{4,5},{5,4},{6,7},{7,6},{8,9},{9,8},{10,11... | collective-permute-start | bytes 4718600 | tf_op jit(solution)/shard_map/ppermute | solution.py:206
  3.5 0.0 collective-permute-start.4
  3.5 0.0 slice-start
  3.5 0.0 copy-start.2
  3.5 1.1 %copy-done.2 = bf16[4,1,16,1024]{3,2,1,0:T(8,128)(2,1)S(1)} copy-done((bf16[4,1,16,1024]{3,2,1,0:T(8,128)(2,1)S(1)}, bf16[4,1,16,1024]{3,2,1,0:T(8,128)(2,1)}, u32[]{:S(2)}) %copy-start.2) | copy-done | bytes 131096
  4.5 0.0 copy-start.6
  4.5 0.9 %copy-done.6 = f32[1024]{0:T(1024)S(1)} copy-done((f32[1024]{0:T(1024)S(1)}, f32[1024]{0:T(1024)}, u32[]{:S(2)}) %copy-start.6) | copy-done | bytes 4120
  5.5 0.0 slice-start.1
  5.5 0.1 norm_own.1.refs_0_
  5.6 0.0 copy-start.4
  5.6 1.0 %collective-permute-done.refs_1_ = bf16[64,1024]{1,0:T(8,128)(2,1)S(1)} collective-permute-done((bf16[64,1024]{1,0:T(8,128)(2,1)}, bf16[64,1024]{1,0:T(8,128)(2,1)S(1)}, u32[]{:S(2)}, u32[]{:S(2)}) %collective-permute-start) | collective-permute-done | bytes 131104 | tf_op jit(solution)/shard_map/ppermute | solution.py:206
  6.6 0.0 collective-permute-done.1.refs_0_
  6.6 0.0 collective-permute-start.2
  6.7 0.2 norm.1
  6.8 1.2 %collective-permute-done.2.refs_3_ = bf16[64,1024]{1,0:T(8,128)(2,1)S(1)} collective-permute-done((bf16[64,1024]{1,0:T(8,128)(2,1)S(1)}, bf16[64,1024]{1,0:T(8,128)(2,1)S(1)}, u32[]{:S(2)}, u32[]{:S(2)}) %collective-permute-start.2) | collective-permute-done | bytes 131104 | tf_op jit(solution)/shard_map/ppermute | solution.py:206
  8.0 0.0 slice-done
  8.0 0.0 slice-done.1
  8.0 0.0 copy-done.4
  8.0 0.0 copy-start.8
  8.0 0.0 copy-start
  8.0 1.9 %conv.1 = bf16[256,256]{1,0:T(8,128)(2,1)S(1)} custom-call(f32[1,1024]{1,0:T(1,128)S(1)} %bitcast.23, bf16[3,3,256,1024]{3,2,1,0:T(8,128)(2,1)S(1)} %bitcast.12, bf16[256,256]{1,0:T(8,128)(2,1)S(1)} %copy-done.4, bf16[64,1024]{1,0:T(8,128)(2,1)S(1)} %norm_own.1.refs_0_, bf16[64,1024]{1,0:T(8,128)(2,1)S(1)} %get-tuple-element.20.refs_1_, ...), custom_call_target="tpu_custom_call" | custom-call | flops 1207959552 | bytes 5509120 | tf_op jit(solution)/shard_map/conv/pallas_call | solution.py:187
  10.0 0.0 collective-permute-done.4.other_out
  10.0 0.0 collective-permute-done.3.other_ref
  10.0 0.0 copy-done.8
  10.0 0.2 collective-permute-start.5
  10.2 13.9 %all_to_all.10 = bf16[16,16,256]{2,1,0:T(8,128)(2,1)S(1)} all-to-all(bf16[16,16,256]{2,1,0:T(8,128)(2,1)S(1)} %bitcast.13), channel_id=1, replica_groups={{0,1,4,5,8,9,12,13,16,17,20,21,24,25,28,29},{2,3,6,7,10,11,14,15,18,19,..., dimensions={0} | all-to-all | bytes 262144 | tf_op jit(solution)/shard_map/all_to_all | solution.py:209
  24.1 0.0 copy-done
  24.1 0.7 %temporal.1.refs_0_ = bf16[64,1024]{1,0:T(8,128)(2,1)S(1)} custom-call(bf16[8,2,16,256]{3,2,1,0:T(8,128)(2,1)S(1)} %bitcast.15, bf16[3,256,1024]{2,1,0:T(8,128)(2,1)S(1)} %copy-done, bf16[3,256,1024]{2,1,0:T(8,128)(2,1)S(1)} %collective-permute-done.3.other_ref), custom_call_target="tpu_custom_call" | custom-call | flops 201326592 | bytes 3407872 | tf_op jit(solution)/shard_map/temporal/pallas_call | solution.py:187
  24.8 0.0 copy-start.1
  24.8 0.0 copy-start.7
  24.8 0.0 collective-permute-done.5.other_ref
  24.8 1.6 %collective-permute-start.6 = (bf16[64,1024]{1,0:T(8,128)(2,1)S(1)}, bf16[64,1024]{1,0:T(8,128)(2,1)S(1)}, u32[]{:S(2)}, u32[]{:S(2)}) collective-permute-start(bf16[64,1024]{1,0:T(8,128)(2,1)S(1)} %temporal.1.refs_0_), channel_id=1, source_target_pairs={{0,2},{1,3},{2,0},{3,1},{4,6},{5,7},{6,4},{7,5},{8,10},{9,11},{10,... | collective-permute-start | bytes 393224 | tf_op jit(solution)/shard_map/ppermute | solution.py:206
  26.4 0.9 %turn.1.qkv_ref = bf16[2,1024,768]{2,1,0:T(8,128)(2,1)S(1)} custom-call(bf16[3,256,1024]{2,1,0:T(8,128)(2,1)S(1)} %copy-done.8, bf16[3,256,1024]{2,1,0:T(8,128)(2,1)S(1)} %collective-permute-done.5.other_ref), custom_call_target="tpu_custom_call" | custom-call | flops 6000000000 | bytes 6291456 | tf_op jit(solution)/shard_map/turn/pallas_call | solution.py:187
  27.3 2.6 %collective-permute-done.6.refs_1_ = bf16[64,1024]{1,0:T(8,128)(2,1)S(1)} collective-permute-done((bf16[64,1024]{1,0:T(8,128)(2,1)S(1)}, bf16[64,1024]{1,0:T(8,128)(2,1)S(1)}, u32[]{:S(2)}, u32[]{:S(2)}) %collective-permute-start.6) | collective-permute-done | bytes 131104 | tf_op jit(solution)/shard_map/ppermute | solution.py:206
  29.9 0.0 copy-done.1
  29.9 0.0 copy-done.7
  29.9 0.0 copy-start.3
  29.9 0.0 copy-start.5
  29.9 1.4 %attend.1 = bf16[256,256]{1,0:T(8,128)(2,1)S(1)} custom-call(f32[1,1024]{1,0:T(1,128)S(1)} %bitcast.24, bf16[2,1024,768]{2,1,0:T(8,128)(2,1)S(1)} %turn.1.qkv_ref, bf16[256,1024]{1,0:T(8,128)(2,1)S(1)} %copy-done.1, bf16[256,1024]{1,0:T(8,128)(2,1)S(1)} %collective-permute-done.4.other_out, bf16[64,1024]{1,0:T(8,128)(2,1)S(1)} %temporal.1.refs_0_, ...), custom_call_target="tpu_custom_call" | custom-call | flops 268435456 | bytes 4591616 | tf_op jit(solution)/shard_map/attend/pallas_call | solution.py:187
  31.3 10.8 %all_to_all.11 = bf16[32,8,256]{2,1,0:T(8,128)(2,1)S(1)} all-to-all(bf16[32,8,256]{2,1,0:T(8,128)(2,1)S(1)} %bitcast.16), channel_id=1, replica_groups=mesh['orbit'=8,'space'=4] {'orbit','space'}, dimensions={0} | all-to-all | bytes 262144 | tf_op jit(solution)/shard_map/all_to_all | solution.py:209
  42.2 0.0 copy-done.3
  42.2 0.0 copy-done.5
  42.2 0.8 %restore.1 = bf16[4,16,1024]{2,1,0:T(8,128)(2,1)} custom-call(bf16[256,256]{1,0:T(8,128)(2,1)S(1)} %bitcast.14, bf16[128,256]{1,0:T(8,128)(2,1)S(1)} %copy-done.5, bf16[4,16,1024]{2,1,0:T(8,128)(2,1)S(1)} %bitcast.20), custom_call_target="tpu_custom_call" | custom-call | bytes 458752 | tf_op jit(solution)/shard_map/restore/pallas_call | solution.py:187
  (1 shorter events, 0.0 us)
Async XLA Ops:
  0.0 6.6 %collective-permute-start = (bf16[64,1024]{1,0:T(8,128)(2,1)}, bf16[64,1024]{1,0:T(8,128)(2,1)S(1)}, u32[]{:S(2)}, u32[]{:S(2)}) collective-permute-start(bf16[64,1024]{1,0:T(8,128)(2,1)} %bitcast.17), channel_id=1, source_target_pairs={{0,2},{1,3},{2,0},{3,1},{4,6},{5,7},{6,4},{7,5},{8,10},{9,11},{10,... | collective-permute-start | bytes 393224 | tf_op jit(solution)/shard_map/ppermute | solution.py:206
  2.9 3.7 %collective-permute-start.1 = (bf16[64,1024]{1,0:T(8,128)(2,1)}, bf16[64,1024]{1,0:T(8,128)(2,1)S(1)}, u32[]{:S(2)}, u32[]{:S(2)}) collective-permute-start(bf16[64,1024]{1,0:T(8,128)(2,1)} %bitcast.18), channel_id=1, source_target_pairs={{0,1},{1,0},{2,3},{3,2},{4,5},{5,4},{6,7},{7,6},{8,9},{9,8},{10,11... | collective-permute-start | bytes 393224 | tf_op jit(solution)/shard_map/ppermute | solution.py:206
  2.9 7.0 %collective-permute-start.3 = (bf16[3,256,1024]{2,1,0:T(8,128)(2,1)}, bf16[3,256,1024]{2,1,0:T(8,128)(2,1)S(1)}, u32[]{:S(2)}, u32[]{:S(2)}) collective-permute-start(bf16[3,256,1024]{2,1,0:T(8,128)(2,1)} %own_ref.1), channel_id=1, source_target_pairs={{0,1},{1,0},{2,3},{3,2},{4,5},{5,4},{6,7},{7,6},{8,9},{9,8},{10,11... | collective-permute-start | bytes 4718600 | tf_op jit(solution)/shard_map/ppermute | solution.py:206
  3.5 6.5 %collective-permute-start.4 = (bf16[256,1024]{1,0:T(8,128)(2,1)}, bf16[256,1024]{1,0:T(8,128)(2,1)S(1)}, u32[]{:S(2)}, u32[]{:S(2)}) collective-permute-start(bf16[256,1024]{1,0:T(8,128)(2,1)} %own_out.1), channel_id=1, source_target_pairs={{0,1},{1,0},{2,3},{3,2},{4,5},{5,4},{6,7},{7,6},{8,9},{9,8},{10,11... | collective-permute-start | bytes 1572872 | tf_op jit(solution)/shard_map/ppermute | solution.py:206
  3.5 4.5 %slice-start = ((s8[4718592]{0:T(1024)(128)(4,1)}), s8[4194304]{0:T(1024)(128)(4,1)S(1)}, s32[]{:S(2)}) async-start(s8[4718592]{0:T(1024)(128)(4,1)} %bitcast.11), calls=%async_computation.2 | async-start | bytes 8388608
  3.5 1.1 %copy-start.2 = (bf16[4,1,16,1024]{3,2,1,0:T(8,128)(2,1)S(1)}, bf16[4,1,16,1024]{3,2,1,0:T(8,128)(2,1)}, u32[]{:S(2)}) copy-start(bf16[4,1,16,1024]{3,2,1,0:T(8,128)(2,1)} %param.9) | copy-start | bytes 393220
  4.5 0.9 %copy-start.6 = (f32[1024]{0:T(1024)S(1)}, f32[1024]{0:T(1024)}, u32[]{:S(2)}) copy-start(f32[1024]{0:T(1024)} %param.10) | copy-start | bytes 12292
  5.5 2.5 %slice-start.1 = ((s8[4718592]{0:T(1024)(128)(4,1)}), s8[524288]{0:T(1024)(128)(4,1)S(1)}, s32[]{:S(2)}) async-start(s8[4718592]{0:T(1024)(128)(4,1)} %bitcast.11), calls=%async_computation.3 | async-start | bytes 1048576
  5.6 2.4 %copy-start.4 = (bf16[256,256]{1,0:T(8,128)(2,1)S(1)}, bf16[256,256]{1,0:T(8,128)(2,1)}, u32[]{:S(2)}) copy-start(bf16[256,256]{1,0:T(8,128)(2,1)} %constant.4.clone.order_ref) | copy-start | bytes 393220
  6.6 1.3 %collective-permute-start.2 = (bf16[64,1024]{1,0:T(8,128)(2,1)S(1)}, bf16[64,1024]{1,0:T(8,128)(2,1)S(1)}, u32[]{:S(2)}, u32[]{:S(2)}) collective-permute-start(bf16[64,1024]{1,0:T(8,128)(2,1)S(1)} %collective-permute-done.refs_1_), channel_id=1, source_target_pairs={{0,1},{1,0},{2,3},{3,2},{4,5},{5,4},{6,7},{7,6},{8,9},{9,8},{10,11... | collective-permute-start | bytes 393224 | tf_op jit(solution)/shard_map/ppermute | solution.py:206
  8.0 2.0 %copy-start.8 = (bf16[3,256,1024]{2,1,0:T(8,128)(2,1)S(1)}, bf16[3,256,1024]{2,1,0:T(8,128)(2,1)}, u32[]{:S(2)}) copy-start(bf16[3,256,1024]{2,1,0:T(8,128)(2,1)} %own_ref.2) | copy-start | bytes 4718596
  8.0 16.1 %copy-start = (bf16[3,256,1024]{2,1,0:T(8,128)(2,1)S(1)}, bf16[3,256,1024]{2,1,0:T(8,128)(2,1)}, u32[]{:S(2)}) copy-start(bf16[3,256,1024]{2,1,0:T(8,128)(2,1)} %own_ref.1) | copy-start | bytes 4718596
  10.0 14.8 %collective-permute-start.5 = (bf16[3,256,1024]{2,1,0:T(8,128)(2,1)S(1)}, bf16[3,256,1024]{2,1,0:T(8,128)(2,1)S(1)}, u32[]{:S(2)}, u32[]{:S(2)}) collective-permute-start(bf16[3,256,1024]{2,1,0:T(8,128)(2,1)S(1)} %copy-done.8), channel_id=1, source_target_pairs={{0,1},{1,0},{2,3},{3,2},{4,5},{5,4},{6,7},{7,6},{8,9},{9,8},{10,11... | collective-permute-start | bytes 4718600 | tf_op jit(solution)/shard_map/ppermute | solution.py:206
  24.8 5.1 %copy-start.1 = (bf16[256,1024]{1,0:T(8,128)(2,1)S(1)}, bf16[256,1024]{1,0:T(8,128)(2,1)}, u32[]{:S(2)}) copy-start(bf16[256,1024]{1,0:T(8,128)(2,1)} %own_out.1) | copy-start | bytes 1572868
  24.8 5.1 %copy-start.7 = (f32[1024]{0:T(1024)S(1)}, f32[1024]{0:T(1024)}, u32[]{:S(2)}) copy-start(f32[1024]{0:T(1024)} %param.13) | copy-start | bytes 12292
  24.8 5.0 %collective-permute-start.6 = (bf16[64,1024]{1,0:T(8,128)(2,1)S(1)}, bf16[64,1024]{1,0:T(8,128)(2,1)S(1)}, u32[]{:S(2)}, u32[]{:S(2)}) collective-permute-start(bf16[64,1024]{1,0:T(8,128)(2,1)S(1)} %temporal.1.refs_0_), channel_id=1, source_target_pairs={{0,2},{1,3},{2,0},{3,1},{4,6},{5,7},{6,4},{7,5},{8,10},{9,11},{10,... | collective-permute-start | bytes 393224 | tf_op jit(solution)/shard_map/ppermute | solution.py:206
  29.9 12.3 %copy-start.3 = (bf16[4,1,16,1024]{3,2,1,0:T(8,128)(2,1)S(1)}, bf16[4,1,16,1024]{3,2,1,0:T(8,128)(2,1)}, u32[]{:S(2)}) copy-start(bf16[4,1,16,1024]{3,2,1,0:T(8,128)(2,1)} %param.9) | copy-start | bytes 393220
  29.9 12.3 %copy-start.5 = (bf16[128,256]{1,0:T(8,128)(2,1)S(1)}, bf16[128,256]{1,0:T(8,128)(2,1)}, u32[]{:S(2)}) copy-start(bf16[128,256]{1,0:T(8,128)(2,1)} %constant.5.clone.order_ref) | copy-start | bytes 196612

commit v6 on v5

--- a/solution.py
+++ b/solution.py
@@ -64,40 +64,45 @@
         return jnp.asarray(target.reshape(1, -1) == np.arange(count).reshape(-1, 1), BF16)
 
 
-def norm_kernel(gain_ref, *refs):
-    count = len(refs) // 2
-    for x_ref, out_ref in zip(refs[:count], refs[count:]):
-        out_ref[...] = rms_scale(x_ref[...].astype(F32), gain_ref[...]).astype(BF16)
-
-
-def conv_kernel(plan, gain_ref, weight_ref, order_ref, *refs):
-    x_refs, (out_ref, normed) = refs[:-2], refs[-2:]
+def turn_conv_kernel(weight_ref, out_ref):
+    taps, _, depth, chans = weight_ref.shape
+    for i in range(taps):
+        out_ref[i] = weight_ref[i].reshape(taps * depth, chans).T
+
+
+def add_rows(plan, blocks, places, weight_ref, total):
     per_row, cols, depth = plan.views * plan.cols, plan.cols, plan.slice_chans
-    gain = gain_ref[...]
-    space = lax.axis_index("space")
-    ready = plan.x + 1
-    for k, x_ref in enumerate(x_refs):
-        block = x_ref[...]
-        if k >= ready:
-            block = rms_scale(block.astype(F32), gain).astype(BF16)
-        index = k if k < 2 else (k - 1) * CORES if k < ready else (k - ready + 1) * CORES + 1
-        normed[space ^ index] = block
-    count = plan.space * per_row
-    rows = normed[...].reshape(count, plan.chans)
+    rows = jnp.concatenate(blocks)
+    count = rows.shape[0]
     column = lax.broadcasted_iota(jnp.int32, (count, 1), 0) & (cols - 1)
-    total = None
-    for j in (1, 0, 2):
-        part = dot_trans(rows, weight_ref[1, j])
-        above = dot_trans(rows[: count - per_row], weight_ref[0, j])
-        below = dot_trans(rows[per_row:], weight_ref[2, j])
-        edge = jnp.zeros((per_row, depth), F32)
-        part = part + jnp.concatenate([edge, above]) + jnp.concatenate([below, edge])
-        if j == 0:
-            part = jnp.where(column == 0, 0.0, pltpu.roll(part, 1, 0))
-        if j == 2:
-            part = jnp.where(column == cols - 1, 0.0, pltpu.roll(part, count - 1, 0))
-        total = part if total is None else total + part
-    activated = (total / (1.0 + jnp.exp(-total))).astype(BF16)
+    for i in range(3):
+        part = dot(rows, weight_ref[i])
+        left, middle, right = [part[:, j * depth : (j + 1) * depth] for j in range(3)]
+        left = jnp.where(column == 0, 0.0, pltpu.roll(left, 1, 0))
+        right = jnp.where(column == cols - 1, 0.0, pltpu.roll(right, count - 1, 0))
+        part = left + middle + right
+        for n, place in enumerate(places):
+            total[place + 2 - i] += part[n * per_row : (n + 1) * per_row]
+
+
+def early_kernel(plan, gain_ref, weight_ref, *refs):
+    raw_refs, total_ref = refs[:-1], refs[-1]
+    gain, space = gain_ref[...], lax.axis_index("space")
+    blocks = [rms_scale(ref[...].astype(F32), gain).astype(BF16) for ref in raw_refs]
+    places = [space, space ^ 1] + [space ^ (x * CORES) for x in range(1, plan.x)]
+    total_ref[...] = jnp.zeros_like(total_ref)
+    add_rows(plan, blocks, places, weight_ref, total_ref)
+
+
+def late_kernel(plan, gain_ref, weight_ref, order_ref, early_ref, *refs):
+    raw_refs, (out_ref, total) = refs[:-2], refs[-2:]
+    gain, space = gain_ref[...], lax.axis_index("space")
+    blocks = [rms_scale(ref[...].astype(F32), gain).astype(BF16) for ref in raw_refs]
+    places = [space ^ (x * CORES + 1) for x in range(1, plan.x)]
+    total[...] = early_ref[...]
+    add_rows(plan, blocks, places, weight_ref, total)
+    whole = total[1 : plan.space + 1].reshape(plan.space * plan.views * plan.cols, plan.slice_chans)
+    activated = (whole / (1.0 + jnp.exp(-whole))).astype(BF16)
     out_ref[...] = dot(order_ref[...], activated).astype(BF16)
 
 
@@ -214,20 +219,27 @@
     own = latents.reshape(views * cols, chans)
     far = [swap(own, x * CORES) for x in range(1, plan.x)]
     near = swap(own, 1)
-    (normed,) = call(norm_kernel, "norm_own", [own.shape], (conv_gain, own), flops=60 * 10**9)
-    far, near, normed = lax.optimization_barrier((far, near, normed))
+    depth, per_row = plan.slice_chans, views * cols
+    (taps,) = call(turn_conv_kernel, "turn_conv", [(3, chans, 3 * depth)], (spatial_weight,), flops=60 * 10**9)
     other_temporal, other_out = swap(temporal_weight, 1), swap(out_weight, 1)
+    far, near, taps = lax.optimization_barrier((far, near, taps))
     across = [swap(block, 1) for block in far]
-    ready = call(norm_kernel, "norm", [own.shape] * plan.x, (conv_gain, near, *far), flops=6 * 10**9)
-
-    count = space * views * cols
+    total_shape = (space + 2, per_row, depth)
+    (early,) = call(
+        functools.partial(early_kernel, plan),
+        "conv_early",
+        [jax.ShapeDtypeStruct(total_shape, F32)],
+        (conv_gain, taps, own, near, *far),
+        flops=6 * 10**9,
+    )
+    count = space * per_row
     (activated,) = call(
-        functools.partial(conv_kernel, plan),
-        "conv",
-        [(count, plan.slice_chans)],
-        (conv_gain, spatial_weight, plan.send_order(), normed, *ready, *across),
-        [pltpu.VMEM((space, views * cols, chans), BF16)],
-        flops=2 * 9 * count * chans * plan.slice_chans,
+        functools.partial(late_kernel, plan),
+        "conv_late",
+        [(count, depth)],
+        (conv_gain, taps, plan.send_order(), early, *across),
+        [pltpu.VMEM(total_shape, F32)],
+        flops=2 * 9 * count * chans * depth,
     )
     swapped = (other_temporal, other_out)
     activated, swapped, qkv = lax.optimization_barrier((activated, swapped, qkv_weight))

time: 43.2 us -> 42.8 us (level)
  waiting for transfers between devices: 4.85 us -> 2.99 us
  Pallas kernels: 5.97 us -> 7.56 us
  blocking collectives: 24.8 us -> 24.2 us
    ppermute x7, waiting for transfers between devices: 4.85 us -> 2.99 us  [swap(): lax.ppermute(block, 'space', [(s, s ^ distance) for s in range(space)])]
    pallas_call x7, Pallas kernels: 5.97 us -> 7.56 us  [call(): pl.pallas_call(kernel, out_shape=outs, in_specs=[pl.BlockSpec(memory_spac...]
    all_to_all x2, blocking collectives: 24.8 us -> 24.2 us  [exchange(): lax.all_to_all(blocks, ('orbit', 'space'), 0, 0, tiled=True, axis_index_g...]
    unnamed x22 -> x18, local copies, waits for them, and re-layouts: 2.05 us -> 2.39 us
  transfers between devices with their start and end apart: 7 -> 7, of which waited for: 3 -> 1; matrix products, arithmetic and copies ran while one was open for 0% -> 0% of each run, Pallas kernels for 9% -> 13%
where the time goes in v6:
time: 42.8 us; the launch traced here: 42.6 us
  blocking collectives  24.2 us (57%)
  Pallas kernels  7.56 us (18%)
  starting transfers between devices  5.35 us (12%)
  waiting for transfers between devices  2.99 us (7%)
  local copies, waits for them, and re-layouts  2.39 us (6%)
    all_to_all x2, blocking collectives, exchange(): lax.all_to_all(blocks, ('orbit', 'space'), 0, 0, tiled=True, axis_index_g...  24.2 us
    pallas_call x7, Pallas kernels, call(): pl.pallas_call(kernel, out_shape=outs, in_specs=[pl.BlockSpec(memory_spac...  7.56 us
    ppermute x7, starting transfers between devices, swap(): lax.ppermute(block, 'space', [(s, s ^ distance) for s in range(space)])  5.35 us
    ppermute x7, waiting for transfers between devices, swap(): lax.ppermute(block, 'space', [(s, s ^ distance) for s in range(space)])  2.99 us
    unnamed x18, local copies, waits for them, and re-layouts  2.39 us
  transfers between devices with their start and end apart: 7, of which 1 were waited for; matrix products, arithmetic and copies ran while one was open for 0% of the time, Pallas kernels for 13%

profile of v6, /device:TPU:0, one launch (start us, length us, event | category | flops | bytes accessed | tf_op | source)
XLA Modules:
  0.0 42.6 jit_solution(5267922917743713077)
XLA Ops:
  0.0 0.0 copy-start.2
  0.0 0.0 copy-start.5
  0.0 2.9 %collective-permute-start = (bf16[64,1024]{1,0:T(8,128)(2,1)}, bf16[64,1024]{1,0:T(8,128)(2,1)S(1)}, u32[]{:S(2)}, u32[]{:S(2)}) collective-permute-start(bf16[64,1024]{1,0:T(8,128)(2,1)} %bitcast.15), channel_id=1, source_target_pairs={{0,2},{1,3},{2,0},{3,1},{4,6},{5,7},{6,4},{7,5},{8,10},{9,11},{10,... | collective-permute-start | bytes 393224 | tf_op jit(solution)/shard_map/ppermute | solution.py:211
  2.9 0.0 collective-permute-start.1
  2.9 0.5 %collective-permute-start.3 = (bf16[3,256,1024]{2,1,0:T(8,128)(2,1)}, bf16[3,256,1024]{2,1,0:T(8,128)(2,1)S(1)}, u32[]{:S(2)}, u32[]{:S(2)}) collective-permute-start(bf16[3,256,1024]{2,1,0:T(8,128)(2,1)} %own_ref.1), channel_id=1, source_target_pairs={{0,1},{1,0},{2,3},{3,2},{4,5},{5,4},{6,7},{7,6},{8,9},{9,8},{10,11... | collective-permute-start | bytes 4718600 | tf_op jit(solution)/shard_map/ppermute | solution.py:211
  3.5 0.0 collective-permute-start.4
  3.5 0.0 copy-start.7
  3.5 2.3 %copy-done.7 = bf16[3,3,256,1024]{3,2,1,0:T(8,128)(2,1)S(1)} copy-done((bf16[3,3,256,1024]{3,2,1,0:T(8,128)(2,1)S(1)}, bf16[3,3,256,1024]{3,2,1,0:T(8,128)(2,1)}, u32[]{:S(2)}) %copy-start.7) | copy-done | bytes 4718616
  5.8 1.3 %turn_conv.1.weight_ref = bf16[3,1024,768]{2,1,0:T(8,128)(2,1)S(1)} custom-call(bf16[3,3,256,1024]{3,2,1,0:T(8,128)(2,1)S(1)} %copy-done.7), custom_call_target="tpu_custom_call" | custom-call | flops 60000002048 | bytes 9437184 | tf_op jit(solution)/shard_map/turn_conv/pallas_call | solution.py:192
  7.1 0.0 collective-permute-done.refs_2_
  7.1 0.0 collective-permute-done.1.refs_1_
  7.1 0.6 %collective-permute-start.2 = (bf16[64,1024]{1,0:T(8,128)(2,1)S(1)}, bf16[64,1024]{1,0:T(8,128)(2,1)S(1)}, u32[]{:S(2)}, u32[]{:S(2)}) collective-permute-start(bf16[64,1024]{1,0:T(8,128)(2,1)S(1)} %collective-permute-done.refs_2_), channel_id=1, source_target_pairs={{0,1},{1,0},{2,3},{3,2},{4,5},{5,4},{6,7},{7,6},{8,9},{9,8},{10,11... | collective-permute-start | bytes 393224 | tf_op jit(solution)/shard_map/ppermute | solution.py:211
  7.7 0.0 copy-done.2
  7.7 0.0 copy-done.5
  7.7 0.0 copy-start.3
  7.7 1.2 %conv_early.1.early_ref = f32[6,64,256]{2,1,0:T(8,128)S(1)} custom-call(f32[1,1024]{1,0:T(1,128)S(1)} %bitcast.19, bf16[3,1024,768]{2,1,0:T(8,128)(2,1)S(1)} %turn_conv.1.weight_ref, bf16[64,1024]{1,0:T(8,128)(2,1)S(1)} %bitcast.17, bf16[64,1024]{1,0:T(8,128)(2,1)S(1)} %collective-permute-done.1.refs_1_, bf16[64,1024]{1,0:T(8,128)(2,1)S(1)} %collective-permute-done.refs_2_), custom_call_target="tpu_custom_call" | custom-call | flops 6000000000 | bytes 5509120 | tf_op jit(solution)/shard_map/conv_early/pallas_call | solution.py:192
  8.9 0.0 copy-start.8
  8.9 0.0 copy-start
  8.9 0.0 collective-permute-done.2.refs_0_
  8.9 0.0 copy-done.3
  8.9 1.3 %conv_late.1 = bf16[256,256]{1,0:T(8,128)(2,1)S(1)} custom-call(f32[1,1024]{1,0:T(1,128)S(1)} %bitcast.20, bf16[3,1024,768]{2,1,0:T(8,128)(2,1)S(1)} %turn_conv.1.weight_ref, bf16[256,256]{1,0:T(8,128)(2,1)S(1)} %copy-done.3, f32[6,64,256]{2,1,0:T(8,128)S(1)} %conv_early.1.early_ref, bf16[64,1024]{1,0:T(8,128)(2,1)S(1)} %collective-permute-done.2.refs_0_), custom_call_target="tpu_custom_call" | custom-call | flops 1207959552 | bytes 5509120 | tf_op jit(solution)/shard_map/conv_late/pallas_call | solution.py:192
  10.3 0.0 collective-permute-done.4.other_out
  10.3 0.0 collective-permute-done.3.other_ref
  10.3 0.0 copy-done.8
  10.3 0.1 collective-permute-start.5
  10.4 13.7 %all_to_all.10 = bf16[16,16,256]{2,1,0:T(8,128)(2,1)S(1)} all-to-all(bf16[16,16,256]{2,1,0:T(8,128)(2,1)S(1)} %bitcast.11), channel_id=1, replica_groups={{0,1,4,5,8,9,12,13,16,17,20,21,24,25,28,29},{2,3,6,7,10,11,14,15,18,19,..., dimensions={0} | all-to-all | bytes 262144 | tf_op jit(solution)/shard_map/all_to_all | solution.py:214
  24.1 0.0 copy-done
  24.2 0.7 %temporal.1.refs_0_ = bf16[64,1024]{1,0:T(8,128)(2,1)S(1)} custom-call(bf16[8,2,16,256]{3,2,1,0:T(8,128)(2,1)S(1)} %bitcast.13, bf16[3,256,1024]{2,1,0:T(8,128)(2,1)S(1)} %copy-done, bf16[3,256,1024]{2,1,0:T(8,128)(2,1)S(1)} %collective-permute-done.3.other_ref), custom_call_target="tpu_custom_call" | custom-call | flops 201326592 | bytes 3407872 | tf_op jit(solution)/shard_map/temporal/pallas_call | solution.py:192
  24.8 0.0 copy-start.1
  24.8 0.0 copy-start.6
  24.8 0.0 collective-permute-done.5.other_ref
  24.9 1.2 %collective-permute-start.6 = (bf16[64,1024]{1,0:T(8,128)(2,1)S(1)}, bf16[64,1024]{1,0:T(8,128)(2,1)S(1)}, u32[]{:S(2)}, u32[]{:S(2)}) collective-permute-start(bf16[64,1024]{1,0:T(8,128)(2,1)S(1)} %temporal.1.refs_0_), channel_id=1, source_target_pairs={{0,2},{1,3},{2,0},{3,1},{4,6},{5,7},{6,4},{7,5},{8,10},{9,11},{10,... | collective-permute-start | bytes 393224 | tf_op jit(solution)/shard_map/ppermute | solution.py:211
  26.0 0.9 %turn.1.qkv_ref = bf16[2,1024,768]{2,1,0:T(8,128)(2,1)S(1)} custom-call(bf16[3,256,1024]{2,1,0:T(8,128)(2,1)S(1)} %copy-done.8, bf16[3,256,1024]{2,1,0:T(8,128)(2,1)S(1)} %collective-permute-done.5.other_ref), custom_call_target="tpu_custom_call" | custom-call | flops 6000000000 | bytes 6291456 | tf_op jit(solution)/shard_map/turn/pallas_call | solution.py:192
  26.9 3.0 %collective-permute-done.6.refs_1_ = bf16[64,1024]{1,0:T(8,128)(2,1)S(1)} collective-permute-done((bf16[64,1024]{1,0:T(8,128)(2,1)S(1)}, bf16[64,1024]{1,0:T(8,128)(2,1)S(1)}, u32[]{:S(2)}, u32[]{:S(2)}) %collective-permute-start.6) | collective-permute-done | bytes 131104 | tf_op jit(solution)/shard_map/ppermute | solution.py:211
  29.9 0.0 copy-done.1
  29.9 0.0 copy-done.6
  29.9 0.0 copy-start.4
  29.9 1.4 %attend.1 = bf16[256,256]{1,0:T(8,128)(2,1)S(1)} custom-call(f32[1,1024]{1,0:T(1,128)S(1)} %bitcast.21, bf16[2,1024,768]{2,1,0:T(8,128)(2,1)S(1)} %turn.1.qkv_ref, bf16[256,1024]{1,0:T(8,128)(2,1)S(1)} %copy-done.1, bf16[256,1024]{1,0:T(8,128)(2,1)S(1)} %collective-permute-done.4.other_out, bf16[64,1024]{1,0:T(8,128)(2,1)S(1)} %temporal.1.refs_0_, ...), custom_call_target="tpu_custom_call" | custom-call | flops 268435456 | bytes 4591616 | tf_op jit(solution)/shard_map/attend/pallas_call | solution.py:192
  31.3 10.5 %all_to_all.11 = bf16[32,8,256]{2,1,0:T(8,128)(2,1)S(1)} all-to-all(bf16[32,8,256]{2,1,0:T(8,128)(2,1)S(1)} %bitcast.14), channel_id=1, replica_groups=mesh['orbit'=8,'space'=4] {'orbit','space'}, dimensions={0} | all-to-all | bytes 262144 | tf_op jit(solution)/shard_map/all_to_all | solution.py:214
  41.8 0.0 copy-done.4
  41.8 0.8 %restore.1 = bf16[4,16,1024]{2,1,0:T(8,128)(2,1)} custom-call(bf16[256,256]{1,0:T(8,128)(2,1)S(1)} %bitcast.12, bf16[128,256]{1,0:T(8,128)(2,1)S(1)} %copy-done.4, bf16[4,16,1024]{2,1,0:T(8,128)(2,1)S(1)} %bitcast.18), custom_call_target="tpu_custom_call" | custom-call | bytes 458752 | tf_op jit(solution)/shard_map/restore/pallas_call | solution.py:192
Async XLA Ops:
  0.0 7.7 %copy-start.2 = (bf16[4,1,16,1024]{3,2,1,0:T(8,128)(2,1)S(1)}, bf16[4,1,16,1024]{3,2,1,0:T(8,128)(2,1)}, u32[]{:S(2)}) copy-start(bf16[4,1,16,1024]{3,2,1,0:T(8,128)(2,1)} %param.9) | copy-start | bytes 393220
  0.0 7.7 %copy-start.5 = (f32[1024]{0:T(1024)S(1)}, f32[1024]{0:T(1024)}, u32[]{:S(2)}) copy-start(f32[1024]{0:T(1024)} %param.10) | copy-start | bytes 12292
  0.0 7.1 %collective-permute-start = (bf16[64,1024]{1,0:T(8,128)(2,1)}, bf16[64,1024]{1,0:T(8,128)(2,1)S(1)}, u32[]{:S(2)}, u32[]{:S(2)}) collective-permute-start(bf16[64,1024]{1,0:T(8,128)(2,1)} %bitcast.15), channel_id=1, source_target_pairs={{0,2},{1,3},{2,0},{3,1},{4,6},{5,7},{6,4},{7,5},{8,10},{9,11},{10,... | collective-permute-start | bytes 393224 | tf_op jit(solution)/shard_map/ppermute | solution.py:211
  2.9 4.1 %collective-permute-start.1 = (bf16[64,1024]{1,0:T(8,128)(2,1)}, bf16[64,1024]{1,0:T(8,128)(2,1)S(1)}, u32[]{:S(2)}, u32[]{:S(2)}) collective-permute-start(bf16[64,1024]{1,0:T(8,128)(2,1)} %bitcast.16), channel_id=1, source_target_pairs={{0,1},{1,0},{2,3},{3,2},{4,5},{5,4},{6,7},{7,6},{8,9},{9,8},{10,11... | collective-permute-start | bytes 393224 | tf_op jit(solution)/shard_map/ppermute | solution.py:211
  2.9 7.3 %collective-permute-start.3 = (bf16[3,256,1024]{2,1,0:T(8,128)(2,1)}, bf16[3,256,1024]{2,1,0:T(8,128)(2,1)S(1)}, u32[]{:S(2)}, u32[]{:S(2)}) collective-permute-start(bf16[3,256,1024]{2,1,0:T(8,128)(2,1)} %own_ref.1), channel_id=1, source_target_pairs={{0,1},{1,0},{2,3},{3,2},{4,5},{5,4},{6,7},{7,6},{8,9},{9,8},{10,11... | collective-permute-start | bytes 4718600 | tf_op jit(solution)/shard_map/ppermute | solution.py:211
  3.5 6.8 %collective-permute-start.4 = (bf16[256,1024]{1,0:T(8,128)(2,1)}, bf16[256,1024]{1,0:T(8,128)(2,1)S(1)}, u32[]{:S(2)}, u32[]{:S(2)}) collective-permute-start(bf16[256,1024]{1,0:T(8,128)(2,1)} %own_out.1), channel_id=1, source_target_pairs={{0,1},{1,0},{2,3},{3,2},{4,5},{5,4},{6,7},{7,6},{8,9},{9,8},{10,11... | collective-permute-start | bytes 1572872 | tf_op jit(solution)/shard_map/ppermute | solution.py:211
  3.5 2.3 %copy-start.7 = (bf16[3,3,256,1024]{3,2,1,0:T(8,128)(2,1)S(1)}, bf16[3,3,256,1024]{3,2,1,0:T(8,128)(2,1)}, u32[]{:S(2)}) copy-start(bf16[3,3,256,1024]{3,2,1,0:T(8,128)(2,1)} %weight_ref.1) | copy-start | bytes 14155780
  7.1 1.8 %collective-permute-start.2 = (bf16[64,1024]{1,0:T(8,128)(2,1)S(1)}, bf16[64,1024]{1,0:T(8,128)(2,1)S(1)}, u32[]{:S(2)}, u32[]{:S(2)}) collective-permute-start(bf16[64,1024]{1,0:T(8,128)(2,1)S(1)} %collective-permute-done.refs_2_), channel_id=1, source_target_pairs={{0,1},{1,0},{2,3},{3,2},{4,5},{5,4},{6,7},{7,6},{8,9},{9,8},{10,11... | collective-permute-start | bytes 393224 | tf_op jit(solution)/shard_map/ppermute | solution.py:211
  7.7 1.3 %copy-start.3 = (bf16[256,256]{1,0:T(8,128)(2,1)S(1)}, bf16[256,256]{1,0:T(8,128)(2,1)}, u32[]{:S(2)}) copy-start(bf16[256,256]{1,0:T(8,128)(2,1)} %constant.4.clone.order_ref) | copy-start | bytes 393220
  8.9 1.4 %copy-start.8 = (bf16[3,256,1024]{2,1,0:T(8,128)(2,1)S(1)}, bf16[3,256,1024]{2,1,0:T(8,128)(2,1)}, u32[]{:S(2)}) copy-start(bf16[3,256,1024]{2,1,0:T(8,128)(2,1)} %own_ref.2) | copy-start | bytes 4718596
  8.9 15.3 %copy-start = (bf16[3,256,1024]{2,1,0:T(8,128)(2,1)S(1)}, bf16[3,256,1024]{2,1,0:T(8,128)(2,1)}, u32[]{:S(2)}) copy-start(bf16[3,256,1024]{2,1,0:T(8,128)(2,1)} %own_ref.1) | copy-start | bytes 4718596
  10.3 14.5 %collective-permute-start.5 = (bf16[3,256,1024]{2,1,0:T(8,128)(2,1)S(1)}, bf16[3,256,1024]{2,1,0:T(8,128)(2,1)S(1)}, u32[]{:S(2)}, u32[]{:S(2)}) collective-permute-start(bf16[3,256,1024]{2,1,0:T(8,128)(2,1)S(1)} %copy-done.8), channel_id=1, source_target_pairs={{0,1},{1,0},{2,3},{3,2},{4,5},{5,4},{6,7},{7,6},{8,9},{9,8},{10,11... | collective-permute-start | bytes 4718600 | tf_op jit(solution)/shard_map/ppermute | solution.py:211
  24.8 5.1 %copy-start.1 = (bf16[256,1024]{1,0:T(8,128)(2,1)S(1)}, bf16[256,1024]{1,0:T(8,128)(2,1)}, u32[]{:S(2)}) copy-start(bf16[256,1024]{1,0:T(8,128)(2,1)} %own_out.1) | copy-start | bytes 1572868
  24.8 5.1 %copy-start.6 = (f32[1024]{0:T(1024)S(1)}, f32[1024]{0:T(1024)}, u32[]{:S(2)}) copy-start(f32[1024]{0:T(1024)} %param.13) | copy-start | bytes 12292
  24.9 5.0 %collective-permute-start.6 = (bf16[64,1024]{1,0:T(8,128)(2,1)S(1)}, bf16[64,1024]{1,0:T(8,128)(2,1)S(1)}, u32[]{:S(2)}, u32[]{:S(2)}) collective-permute-start(bf16[64,1024]{1,0:T(8,128)(2,1)S(1)} %temporal.1.refs_0_), channel_id=1, source_target_pairs={{0,2},{1,3},{2,0},{3,1},{4,6},{5,7},{6,4},{7,5},{8,10},{9,11},{10,... | collective-permute-start | bytes 393224 | tf_op jit(solution)/shard_map/ppermute | solution.py:211
  29.9 11.9 %copy-start.4 = (bf16[128,256]{1,0:T(8,128)(2,1)S(1)}, bf16[128,256]{1,0:T(8,128)(2,1)}, u32[]{:S(2)}) copy-start(bf16[128,256]{1,0:T(8,128)(2,1)} %constant.5.clone.order_ref) | copy-start | bytes 196612

commit v7 on v6

--- a/solution.py
+++ b/solution.py
@@ -22,8 +22,8 @@
     return lax.dot_general(left, right, (((1,), (1,)), ((), ())), preferred_element_type=F32)
 
 
-def rms_scale(wide, gain):
-    return wide * lax.rsqrt(jnp.mean(wide * wide, axis=-1, keepdims=True) + 1e-06) * gain
+def rms(wide):
+    return lax.rsqrt(jnp.mean(wide * wide, axis=-1, keepdims=True) + 1e-06)
 
 
 def picks(source, width):
@@ -70,37 +70,39 @@
         out_ref[i] = weight_ref[i].reshape(taps * depth, chans).T
 
 
-def add_rows(plan, blocks, places, weight_ref, total):
+def add_rows(plan, blocks, gain, places, weight_ref, total):
     per_row, cols, depth = plan.views * plan.cols, plan.cols, plan.slice_chans
-    rows = jnp.concatenate(blocks)
-    count = rows.shape[0]
+    wide = jnp.concatenate([block.astype(F32) for block in blocks])
+    count = wide.shape[0]
+    rows, scale = (wide * gain).astype(BF16), rms(wide)
     column = lax.broadcasted_iota(jnp.int32, (count, 1), 0) & (cols - 1)
     for i in range(3):
         part = dot(rows, weight_ref[i])
         left, middle, right = [part[:, j * depth : (j + 1) * depth] for j in range(3)]
+        left, right = left * scale, right * scale
         left = jnp.where(column == 0, 0.0, pltpu.roll(left, 1, 0))
         right = jnp.where(column == cols - 1, 0.0, pltpu.roll(right, count - 1, 0))
-        part = left + middle + right
+        part = left + middle * scale + right
         for n, place in enumerate(places):
             total[place + 2 - i] += part[n * per_row : (n + 1) * per_row]
 
 
 def early_kernel(plan, gain_ref, weight_ref, *refs):
     raw_refs, total_ref = refs[:-1], refs[-1]
-    gain, space = gain_ref[...], lax.axis_index("space")
-    blocks = [rms_scale(ref[...].astype(F32), gain).astype(BF16) for ref in raw_refs]
+    space = lax.axis_index("space")
+    blocks = [ref[...] for ref in raw_refs]
     places = [space, space ^ 1] + [space ^ (x * CORES) for x in range(1, plan.x)]
     total_ref[...] = jnp.zeros_like(total_ref)
-    add_rows(plan, blocks, places, weight_ref, total_ref)
+    add_rows(plan, blocks, gain_ref[...], places, weight_ref, total_ref)
 
 
 def late_kernel(plan, gain_ref, weight_ref, order_ref, early_ref, *refs):
     raw_refs, (out_ref, total) = refs[:-2], refs[-2:]
-    gain, space = gain_ref[...], lax.axis_index("space")
-    blocks = [rms_scale(ref[...].astype(F32), gain).astype(BF16) for ref in raw_refs]
+    space = lax.axis_index("space")
+    blocks = [ref[...] for ref in raw_refs]
     places = [space ^ (x * CORES + 1) for x in range(1, plan.x)]
     total[...] = early_ref[...]
-    add_rows(plan, blocks, places, weight_ref, total)
+    add_rows(plan, blocks, gain_ref[...], places, weight_ref, total)
     whole = total[1 : plan.space + 1].reshape(plan.space * plan.views * plan.cols, plan.slice_chans)
     activated = (whole / (1.0 + jnp.exp(-whole))).astype(BF16)
     out_ref[...] = dot(order_ref[...], activated).astype(BF16)
@@ -137,7 +139,7 @@
     for ref in down_refs[1:]:
         down = down + ref[...].astype(F32)
     down = down.astype(BF16).astype(F32)
-    normed = rms_scale(down, gain_ref[...]).astype(BF16)
+    gained, scale = (down * gain_ref[...]).astype(BF16), rms(down)
     channel_head = lax.broadcasted_iota(jnp.int32, (1, depth), 1) >> (HD.bit_length() - 1)
     key_head = lax.broadcasted_iota(jnp.int32, (1, heads * rows), 1) >> (rows.bit_length() - 1)
     key_row_head = lax.broadcasted_iota(jnp.int32, (heads * rows, 1), 0) >> (rows.bit_length() - 1)
@@ -156,7 +158,7 @@
     first = lax.axis_index("space") < CORES
     projected = jnp.where(first, 1.0, 0.0) * down
     both = range(CORES)
-    qkv = [dot(normed, qkv_ref[k]).astype(BF16) for k in both]
+    qkv = [(dot(gained, qkv_ref[k]) * scale).astype(BF16) for k in both]
     keys = [by_head(qkv[k][:, depth : 2 * depth]) for k in both]
     values = [by_head(qkv[k][:, 2 * depth :]) for k in both]
     scores = [dot_trans(qkv[k][:, :depth], keys[k]) * (HD**-0.5) for k in both]

time: 42.8 us -> 42.6 us (level)
  transfers between devices with their start and end apart: 7 -> 7, of which waited for: 1 -> 1; matrix products, arithmetic and copies ran while one was open for 0% -> 0% of each run, Pallas kernels for 13% -> 12%
where the time goes in v7:
time: 42.6 us; the launch traced here: 42.4 us
  blocking collectives  24.2 us (57%)
  Pallas kernels  7.37 us (17%)
  starting transfers between devices  5.31 us (12%)
  waiting for transfers between devices  3.01 us (7%)
  local copies, waits for them, and re-layouts  2.46 us (6%)
    all_to_all x2, blocking collectives, exchange(): lax.all_to_all(blocks, ('orbit', 'space'), 0, 0, tiled=True, axis_index_g...  24.2 us
    pallas_call x7, Pallas kernels, call(): pl.pallas_call(kernel, out_shape=outs, in_specs=[pl.BlockSpec(memory_spac...  7.37 us
    ppermute x7, starting transfers between devices, swap(): lax.ppermute(block, 'space', [(s, s ^ distance) for s in range(space)])  5.31 us
    ppermute x7, waiting for transfers between devices, swap(): lax.ppermute(block, 'space', [(s, s ^ distance) for s in range(space)])  3.01 us
    unnamed x18, local copies, waits for them, and re-layouts  2.46 us
  transfers between devices with their start and end apart: 7, of which 1 were waited for; matrix products, arithmetic and copies ran while one was open for 0% of the time, Pallas kernels for 12%

profile of v7, /device:TPU:0, one launch (start us, length us, event | category | flops | bytes accessed | tf_op | source)
XLA Modules:
  0.0 42.4 jit_solution(17889788196766343976)
XLA Ops:
  0.0 0.0 copy-start.2
  0.0 0.0 copy-start.5
  0.0 2.9 %collective-permute-start = (bf16[64,1024]{1,0:T(8,128)(2,1)}, bf16[64,1024]{1,0:T(8,128)(2,1)S(1)}, u32[]{:S(2)}, u32[]{:S(2)}) collective-permute-start(bf16[64,1024]{1,0:T(8,128)(2,1)} %bitcast.15), channel_id=1, source_target_pairs={{0,2},{1,3},{2,0},{3,1},{4,6},{5,7},{6,4},{7,5},{8,10},{9,11},{10,... | collective-permute-start | bytes 393224 | tf_op jit(solution)/shard_map/ppermute | solution.py:213
  2.9 0.0 collective-permute-start.1
  2.9 0.5 %collective-permute-start.3 = (bf16[3,256,1024]{2,1,0:T(8,128)(2,1)}, bf16[3,256,1024]{2,1,0:T(8,128)(2,1)S(1)}, u32[]{:S(2)}, u32[]{:S(2)}) collective-permute-start(bf16[3,256,1024]{2,1,0:T(8,128)(2,1)} %own_ref.1), channel_id=1, source_target_pairs={{0,1},{1,0},{2,3},{3,2},{4,5},{5,4},{6,7},{7,6},{8,9},{9,8},{10,11... | collective-permute-start | bytes 4718600 | tf_op jit(solution)/shard_map/ppermute | solution.py:213
  3.5 0.0 collective-permute-start.4
  3.5 0.0 copy-start.7
  3.5 2.3 %copy-done.7 = bf16[3,3,256,1024]{3,2,1,0:T(8,128)(2,1)S(1)} copy-done((bf16[3,3,256,1024]{3,2,1,0:T(8,128)(2,1)S(1)}, bf16[3,3,256,1024]{3,2,1,0:T(8,128)(2,1)}, u32[]{:S(2)}) %copy-start.7) | copy-done | bytes 4718616
  5.8 1.3 %turn_conv.1.weight_ref = bf16[3,1024,768]{2,1,0:T(8,128)(2,1)S(1)} custom-call(bf16[3,3,256,1024]{3,2,1,0:T(8,128)(2,1)S(1)} %copy-done.7), custom_call_target="tpu_custom_call" | custom-call | flops 60000002048 | bytes 9437184 | tf_op jit(solution)/shard_map/turn_conv/pallas_call | solution.py:194
  7.1 0.0 collective-permute-done.refs_2_
  7.1 0.0 collective-permute-done.1.refs_1_
  7.1 0.6 %collective-permute-start.2 = (bf16[64,1024]{1,0:T(8,128)(2,1)S(1)}, bf16[64,1024]{1,0:T(8,128)(2,1)S(1)}, u32[]{:S(2)}, u32[]{:S(2)}) collective-permute-start(bf16[64,1024]{1,0:T(8,128)(2,1)S(1)} %collective-permute-done.refs_2_), channel_id=1, source_target_pairs={{0,1},{1,0},{2,3},{3,2},{4,5},{5,4},{6,7},{7,6},{8,9},{9,8},{10,11... | collective-permute-start | bytes 393224 | tf_op jit(solution)/shard_map/ppermute | solution.py:213
  7.7 0.0 copy-done.2
  7.7 0.0 copy-done.5
  7.7 0.0 copy-start.3
  7.7 1.2 %conv_early.1.early_ref = f32[6,64,256]{2,1,0:T(8,128)S(1)} custom-call(f32[1,1024]{1,0:T(1,128)S(1)} %bitcast.19, bf16[3,1024,768]{2,1,0:T(8,128)(2,1)S(1)} %turn_conv.1.weight_ref, bf16[64,1024]{1,0:T(8,128)(2,1)S(1)} %bitcast.17, bf16[64,1024]{1,0:T(8,128)(2,1)S(1)} %collective-permute-done.1.refs_1_, bf16[64,1024]{1,0:T(8,128)(2,1)S(1)} %collective-permute-done.refs_2_), custom_call_target="tpu_custom_call" | custom-call | flops 6000000000 | bytes 5509120 | tf_op jit(solution)/shard_map/conv_early/pallas_call | solution.py:194
  8.8 0.0 copy-start.8
  8.9 0.0 copy-start
  8.9 0.0 collective-permute-done.2.refs_0_
  8.9 0.0 copy-done.3
  8.9 1.3 %conv_late.1 = bf16[256,256]{1,0:T(8,128)(2,1)S(1)} custom-call(f32[1,1024]{1,0:T(1,128)S(1)} %bitcast.20, bf16[3,1024,768]{2,1,0:T(8,128)(2,1)S(1)} %turn_conv.1.weight_ref, bf16[256,256]{1,0:T(8,128)(2,1)S(1)} %copy-done.3, f32[6,64,256]{2,1,0:T(8,128)S(1)} %conv_early.1.early_ref, bf16[64,1024]{1,0:T(8,128)(2,1)S(1)} %collective-permute-done.2.refs_0_), custom_call_target="tpu_custom_call" | custom-call | flops 1207959552 | bytes 5509120 | tf_op jit(solution)/shard_map/conv_late/pallas_call | solution.py:194
  10.1 0.0 collective-permute-done.4.other_out
  10.2 0.0 collective-permute-done.3.other_ref
  10.2 0.1 copy-done.8
  10.3 0.1 collective-permute-start.5
  10.4 13.7 %all_to_all.10 = bf16[16,16,256]{2,1,0:T(8,128)(2,1)S(1)} all-to-all(bf16[16,16,256]{2,1,0:T(8,128)(2,1)S(1)} %bitcast.11), channel_id=1, replica_groups={{0,1,4,5,8,9,12,13,16,17,20,21,24,25,28,29},{2,3,6,7,10,11,14,15,18,19,..., dimensions={0} | all-to-all | bytes 262144 | tf_op jit(solution)/shard_map/all_to_all | solution.py:216
  24.1 0.0 copy-done
  24.1 0.7 %temporal.1.refs_0_ = bf16[64,1024]{1,0:T(8,128)(2,1)S(1)} custom-call(bf16[8,2,16,256]{3,2,1,0:T(8,128)(2,1)S(1)} %bitcast.13, bf16[3,256,1024]{2,1,0:T(8,128)(2,1)S(1)} %copy-done, bf16[3,256,1024]{2,1,0:T(8,128)(2,1)S(1)} %collective-permute-done.3.other_ref), custom_call_target="tpu_custom_call" | custom-call | flops 201326592 | bytes 3407872 | tf_op jit(solution)/shard_map/temporal/pallas_call | solution.py:194
  24.7 0.0 copy-start.1
  24.7 0.0 copy-start.6
  24.8 0.0 collective-permute-done.5.other_ref
  24.8 1.2 %collective-permute-start.6 = (bf16[64,1024]{1,0:T(8,128)(2,1)S(1)}, bf16[64,1024]{1,0:T(8,128)(2,1)S(1)}, u32[]{:S(2)}, u32[]{:S(2)}) collective-permute-start(bf16[64,1024]{1,0:T(8,128)(2,1)S(1)} %temporal.1.refs_0_), channel_id=1, source_target_pairs={{0,2},{1,3},{2,0},{3,1},{4,6},{5,7},{6,4},{7,5},{8,10},{9,11},{10,... | collective-permute-start | bytes 393224 | tf_op jit(solution)/shard_map/ppermute | solution.py:213
  25.9 0.9 %turn.1.qkv_ref = bf16[2,1024,768]{2,1,0:T(8,128)(2,1)S(1)} custom-call(bf16[3,256,1024]{2,1,0:T(8,128)(2,1)S(1)} %copy-done.8, bf16[3,256,1024]{2,1,0:T(8,128)(2,1)S(1)} %collective-permute-done.5.other_ref), custom_call_target="tpu_custom_call" | custom-call | flops 6000000000 | bytes 6291456 | tf_op jit(solution)/shard_map/turn/pallas_call | solution.py:194
  26.8 3.0 %collective-permute-done.6.refs_1_ = bf16[64,1024]{1,0:T(8,128)(2,1)S(1)} collective-permute-done((bf16[64,1024]{1,0:T(8,128)(2,1)S(1)}, bf16[64,1024]{1,0:T(8,128)(2,1)S(1)}, u32[]{:S(2)}, u32[]{:S(2)}) %collective-permute-start.6) | collective-permute-done | bytes 131104 | tf_op jit(solution)/shard_map/ppermute | solution.py:213
  29.8 0.0 copy-done.1
  29.8 0.0 copy-done.6
  29.8 0.0 copy-start.4
  29.8 1.3 %attend.1 = bf16[256,256]{1,0:T(8,128)(2,1)S(1)} custom-call(f32[1,1024]{1,0:T(1,128)S(1)} %bitcast.21, bf16[2,1024,768]{2,1,0:T(8,128)(2,1)S(1)} %turn.1.qkv_ref, bf16[256,1024]{1,0:T(8,128)(2,1)S(1)} %copy-done.1, bf16[256,1024]{1,0:T(8,128)(2,1)S(1)} %collective-permute-done.4.other_out, bf16[64,1024]{1,0:T(8,128)(2,1)S(1)} %temporal.1.refs_0_, ...), custom_call_target="tpu_custom_call" | custom-call | flops 268435456 | bytes 4591616 | tf_op jit(solution)/shard_map/attend/pallas_call | solution.py:194
  31.1 10.5 %all_to_all.11 = bf16[32,8,256]{2,1,0:T(8,128)(2,1)S(1)} all-to-all(bf16[32,8,256]{2,1,0:T(8,128)(2,1)S(1)} %bitcast.14), channel_id=1, replica_groups=mesh['orbit'=8,'space'=4] {'orbit','space'}, dimensions={0} | all-to-all | bytes 262144 | tf_op jit(solution)/shard_map/all_to_all | solution.py:216
  41.6 0.0 copy-done.4
  41.6 0.8 %restore.1 = bf16[4,16,1024]{2,1,0:T(8,128)(2,1)} custom-call(bf16[256,256]{1,0:T(8,128)(2,1)S(1)} %bitcast.12, bf16[128,256]{1,0:T(8,128)(2,1)S(1)} %copy-done.4, bf16[4,16,1024]{2,1,0:T(8,128)(2,1)S(1)} %bitcast.18), custom_call_target="tpu_custom_call" | custom-call | bytes 458752 | tf_op jit(solution)/shard_map/restore/pallas_call | solution.py:194
Async XLA Ops:
  0.0 7.7 %copy-start.2 = (bf16[4,1,16,1024]{3,2,1,0:T(8,128)(2,1)S(1)}, bf16[4,1,16,1024]{3,2,1,0:T(8,128)(2,1)}, u32[]{:S(2)}) copy-start(bf16[4,1,16,1024]{3,2,1,0:T(8,128)(2,1)} %param.9) | copy-start | bytes 393220
  0.0 7.7 %copy-start.5 = (f32[1024]{0:T(1024)S(1)}, f32[1024]{0:T(1024)}, u32[]{:S(2)}) copy-start(f32[1024]{0:T(1024)} %param.10) | copy-start | bytes 12292
  0.0 7.1 %collective-permute-start = (bf16[64,1024]{1,0:T(8,128)(2,1)}, bf16[64,1024]{1,0:T(8,128)(2,1)S(1)}, u32[]{:S(2)}, u32[]{:S(2)}) collective-permute-start(bf16[64,1024]{1,0:T(8,128)(2,1)} %bitcast.15), channel_id=1, source_target_pairs={{0,2},{1,3},{2,0},{3,1},{4,6},{5,7},{6,4},{7,5},{8,10},{9,11},{10,... | collective-permute-start | bytes 393224 | tf_op jit(solution)/shard_map/ppermute | solution.py:213
  2.9 4.1 %collective-permute-start.1 = (bf16[64,1024]{1,0:T(8,128)(2,1)}, bf16[64,1024]{1,0:T(8,128)(2,1)S(1)}, u32[]{:S(2)}, u32[]{:S(2)}) collective-permute-start(bf16[64,1024]{1,0:T(8,128)(2,1)} %bitcast.16), channel_id=1, source_target_pairs={{0,1},{1,0},{2,3},{3,2},{4,5},{5,4},{6,7},{7,6},{8,9},{9,8},{10,11... | collective-permute-start | bytes 393224 | tf_op jit(solution)/shard_map/ppermute | solution.py:213
  2.9 7.2 %collective-permute-start.3 = (bf16[3,256,1024]{2,1,0:T(8,128)(2,1)}, bf16[3,256,1024]{2,1,0:T(8,128)(2,1)S(1)}, u32[]{:S(2)}, u32[]{:S(2)}) collective-permute-start(bf16[3,256,1024]{2,1,0:T(8,128)(2,1)} %own_ref.1), channel_id=1, source_target_pairs={{0,1},{1,0},{2,3},{3,2},{4,5},{5,4},{6,7},{7,6},{8,9},{9,8},{10,11... | collective-permute-start | bytes 4718600 | tf_op jit(solution)/shard_map/ppermute | solution.py:213
  3.5 6.7 %collective-permute-start.4 = (bf16[256,1024]{1,0:T(8,128)(2,1)}, bf16[256,1024]{1,0:T(8,128)(2,1)S(1)}, u32[]{:S(2)}, u32[]{:S(2)}) collective-permute-start(bf16[256,1024]{1,0:T(8,128)(2,1)} %own_out.1), channel_id=1, source_target_pairs={{0,1},{1,0},{2,3},{3,2},{4,5},{5,4},{6,7},{7,6},{8,9},{9,8},{10,11... | collective-permute-start | bytes 1572872 | tf_op jit(solution)/shard_map/ppermute | solution.py:213
  3.5 2.3 %copy-start.7 = (bf16[3,3,256,1024]{3,2,1,0:T(8,128)(2,1)S(1)}, bf16[3,3,256,1024]{3,2,1,0:T(8,128)(2,1)}, u32[]{:S(2)}) copy-start(bf16[3,3,256,1024]{3,2,1,0:T(8,128)(2,1)} %weight_ref.1) | copy-start | bytes 14155780
  7.1 1.8 %collective-permute-start.2 = (bf16[64,1024]{1,0:T(8,128)(2,1)S(1)}, bf16[64,1024]{1,0:T(8,128)(2,1)S(1)}, u32[]{:S(2)}, u32[]{:S(2)}) collective-permute-start(bf16[64,1024]{1,0:T(8,128)(2,1)S(1)} %collective-permute-done.refs_2_), channel_id=1, source_target_pairs={{0,1},{1,0},{2,3},{3,2},{4,5},{5,4},{6,7},{7,6},{8,9},{9,8},{10,11... | collective-permute-start | bytes 393224 | tf_op jit(solution)/shard_map/ppermute | solution.py:213
  7.7 1.2 %copy-start.3 = (bf16[256,256]{1,0:T(8,128)(2,1)S(1)}, bf16[256,256]{1,0:T(8,128)(2,1)}, u32[]{:S(2)}) copy-start(bf16[256,256]{1,0:T(8,128)(2,1)} %constant.4.clone.order_ref) | copy-start | bytes 393220
  8.8 1.4 %copy-start.8 = (bf16[3,256,1024]{2,1,0:T(8,128)(2,1)S(1)}, bf16[3,256,1024]{2,1,0:T(8,128)(2,1)}, u32[]{:S(2)}) copy-start(bf16[3,256,1024]{2,1,0:T(8,128)(2,1)} %own_ref.2) | copy-start | bytes 4718596
  8.9 15.2 %copy-start = (bf16[3,256,1024]{2,1,0:T(8,128)(2,1)S(1)}, bf16[3,256,1024]{2,1,0:T(8,128)(2,1)}, u32[]{:S(2)}) copy-start(bf16[3,256,1024]{2,1,0:T(8,128)(2,1)} %own_ref.1) | copy-start | bytes 4718596
  10.3 14.5 %collective-permute-start.5 = (bf16[3,256,1024]{2,1,0:T(8,128)(2,1)S(1)}, bf16[3,256,1024]{2,1,0:T(8,128)(2,1)S(1)}, u32[]{:S(2)}, u32[]{:S(2)}) collective-permute-start(bf16[3,256,1024]{2,1,0:T(8,128)(2,1)S(1)} %copy-done.8), channel_id=1, source_target_pairs={{0,1},{1,0},{2,3},{3,2},{4,5},{5,4},{6,7},{7,6},{8,9},{9,8},{10,11... | collective-permute-start | bytes 4718600 | tf_op jit(solution)/shard_map/ppermute | solution.py:213
  24.7 5.1 %copy-start.1 = (bf16[256,1024]{1,0:T(8,128)(2,1)S(1)}, bf16[256,1024]{1,0:T(8,128)(2,1)}, u32[]{:S(2)}) copy-start(bf16[256,1024]{1,0:T(8,128)(2,1)} %own_out.1) | copy-start | bytes 1572868
  24.7 5.1 %copy-start.6 = (f32[1024]{0:T(1024)S(1)}, f32[1024]{0:T(1024)}, u32[]{:S(2)}) copy-start(f32[1024]{0:T(1024)} %param.13) | copy-start | bytes 12292
  24.8 5.0 %collective-permute-start.6 = (bf16[64,1024]{1,0:T(8,128)(2,1)S(1)}, bf16[64,1024]{1,0:T(8,128)(2,1)S(1)}, u32[]{:S(2)}, u32[]{:S(2)}) collective-permute-start(bf16[64,1024]{1,0:T(8,128)(2,1)S(1)} %temporal.1.refs_0_), channel_id=1, source_target_pairs={{0,2},{1,3},{2,0},{3,1},{4,6},{5,7},{6,4},{7,5},{8,10},{9,11},{10,... | collective-permute-start | bytes 393224 | tf_op jit(solution)/shard_map/ppermute | solution.py:213
  29.8 11.8 %copy-start.4 = (bf16[128,256]{1,0:T(8,128)(2,1)S(1)}, bf16[128,256]{1,0:T(8,128)(2,1)}, u32[]{:S(2)}) copy-start(bf16[128,256]{1,0:T(8,128)(2,1)} %constant.5.clone.order_ref) | copy-start | bytes 196612

commit v8 on v6

--- a/solution.py
+++ b/solution.py
@@ -22,8 +22,12 @@
     return lax.dot_general(left, right, (((1,), (1,)), ((), ())), preferred_element_type=F32)
 
 
+def rms(wide):
+    return lax.rsqrt(jnp.mean(wide * wide, axis=-1, keepdims=True) + 1e-06)
+
+
 def rms_scale(wide, gain):
-    return wide * lax.rsqrt(jnp.mean(wide * wide, axis=-1, keepdims=True) + 1e-06) * gain
+    return wide * rms(wide) * gain
 
 
 def picks(source, width):
@@ -137,7 +141,7 @@
     for ref in down_refs[1:]:
         down = down + ref[...].astype(F32)
     down = down.astype(BF16).astype(F32)
-    normed = rms_scale(down, gain_ref[...]).astype(BF16)
+    gained, scale = (down * gain_ref[...]).astype(BF16), rms(down)
     channel_head = lax.broadcasted_iota(jnp.int32, (1, depth), 1) >> (HD.bit_length() - 1)
     key_head = lax.broadcasted_iota(jnp.int32, (1, heads * rows), 1) >> (rows.bit_length() - 1)
     key_row_head = lax.broadcasted_iota(jnp.int32, (heads * rows, 1), 0) >> (rows.bit_length() - 1)
@@ -156,7 +160,7 @@
     first = lax.axis_index("space") < CORES
     projected = jnp.where(first, 1.0, 0.0) * down
     both = range(CORES)
-    qkv = [dot(normed, qkv_ref[k]).astype(BF16) for k in both]
+    qkv = [(dot(gained, qkv_ref[k]) * scale).astype(BF16) for k in both]
     keys = [by_head(qkv[k][:, depth : 2 * depth]) for k in both]
     values = [by_head(qkv[k][:, 2 * depth :]) for k in both]
     scores = [dot_trans(qkv[k][:, :depth], keys[k]) * (HD**-0.5) for k in both]

time: 42.8 us -> 42.7 us (level)
  no operation moved by 1% of the time
where the time goes in v8:
time: 42.7 us; the launch traced here: 42.5 us
  blocking collectives  24.2 us (57%)
  Pallas kernels  7.49 us (18%)
  starting transfers between devices  5.35 us (13%)
  waiting for transfers between devices  2.99 us (7%)
  local copies, waits for them, and re-layouts  2.39 us (6%)
    all_to_all x2, blocking collectives, exchange(): lax.all_to_all(blocks, ('orbit', 'space'), 0, 0, tiled=True, axis_index_g...  24.2 us
    pallas_call x7, Pallas kernels, call(): pl.pallas_call(kernel, out_shape=outs, in_specs=[pl.BlockSpec(memory_spac...  7.49 us
    ppermute x7, starting transfers between devices, swap(): lax.ppermute(block, 'space', [(s, s ^ distance) for s in range(space)])  5.35 us
    ppermute x7, waiting for transfers between devices, swap(): lax.ppermute(block, 'space', [(s, s ^ distance) for s in range(space)])  2.99 us
    unnamed x18, local copies, waits for them, and re-layouts  2.39 us
  transfers between devices with their start and end apart: 7, of which 1 were waited for; matrix products, arithmetic and copies ran while one was open for 0% of the time, Pallas kernels for 13%

profile of v8, /device:TPU:0, one launch (start us, length us, event | category | flops | bytes accessed | tf_op | source)
XLA Modules:
  0.0 42.5 jit_solution(9649641204433511716)
XLA Ops:
  0.0 0.0 copy-start.2
  0.0 0.0 copy-start.5
  0.0 2.9 %collective-permute-start = (bf16[64,1024]{1,0:T(8,128)(2,1)}, bf16[64,1024]{1,0:T(8,128)(2,1)S(1)}, u32[]{:S(2)}, u32[]{:S(2)}) collective-permute-start(bf16[64,1024]{1,0:T(8,128)(2,1)} %bitcast.15), channel_id=1, source_target_pairs={{0,2},{1,3},{2,0},{3,1},{4,6},{5,7},{6,4},{7,5},{8,10},{9,11},{10,... | collective-permute-start | bytes 393224 | tf_op jit(solution)/shard_map/ppermute | solution.py:215
  2.9 0.0 collective-permute-start.1
  2.9 0.5 %collective-permute-start.3 = (bf16[3,256,1024]{2,1,0:T(8,128)(2,1)}, bf16[3,256,1024]{2,1,0:T(8,128)(2,1)S(1)}, u32[]{:S(2)}, u32[]{:S(2)}) collective-permute-start(bf16[3,256,1024]{2,1,0:T(8,128)(2,1)} %own_ref.1), channel_id=1, source_target_pairs={{0,1},{1,0},{2,3},{3,2},{4,5},{5,4},{6,7},{7,6},{8,9},{9,8},{10,11... | collective-permute-start | bytes 4718600 | tf_op jit(solution)/shard_map/ppermute | solution.py:215
  3.5 0.0 collective-permute-start.4
  3.5 0.0 copy-start.7
  3.5 2.3 %copy-done.7 = bf16[3,3,256,1024]{3,2,1,0:T(8,128)(2,1)S(1)} copy-done((bf16[3,3,256,1024]{3,2,1,0:T(8,128)(2,1)S(1)}, bf16[3,3,256,1024]{3,2,1,0:T(8,128)(2,1)}, u32[]{:S(2)}) %copy-start.7) | copy-done | bytes 4718616
  5.8 1.3 %turn_conv.1.weight_ref = bf16[3,1024,768]{2,1,0:T(8,128)(2,1)S(1)} custom-call(bf16[3,3,256,1024]{3,2,1,0:T(8,128)(2,1)S(1)} %copy-done.7), custom_call_target="tpu_custom_call" | custom-call | flops 60000002048 | bytes 9437184 | tf_op jit(solution)/shard_map/turn_conv/pallas_call | solution.py:196
  7.1 0.0 collective-permute-done.refs_2_
  7.1 0.0 collective-permute-done.1.refs_1_
  7.1 0.6 %collective-permute-start.2 = (bf16[64,1024]{1,0:T(8,128)(2,1)S(1)}, bf16[64,1024]{1,0:T(8,128)(2,1)S(1)}, u32[]{:S(2)}, u32[]{:S(2)}) collective-permute-start(bf16[64,1024]{1,0:T(8,128)(2,1)S(1)} %collective-permute-done.refs_2_), channel_id=1, source_target_pairs={{0,1},{1,0},{2,3},{3,2},{4,5},{5,4},{6,7},{7,6},{8,9},{9,8},{10,11... | collective-permute-start | bytes 393224 | tf_op jit(solution)/shard_map/ppermute | solution.py:215
  7.7 0.0 copy-done.2
  7.7 0.0 copy-done.5
  7.7 0.0 copy-start.3
  7.7 1.2 %conv_early.1.early_ref = f32[6,64,256]{2,1,0:T(8,128)S(1)} custom-call(f32[1,1024]{1,0:T(1,128)S(1)} %bitcast.19, bf16[3,1024,768]{2,1,0:T(8,128)(2,1)S(1)} %turn_conv.1.weight_ref, bf16[64,1024]{1,0:T(8,128)(2,1)S(1)} %bitcast.17, bf16[64,1024]{1,0:T(8,128)(2,1)S(1)} %collective-permute-done.1.refs_1_, bf16[64,1024]{1,0:T(8,128)(2,1)S(1)} %collective-permute-done.refs_2_), custom_call_target="tpu_custom_call" | custom-call | flops 6000000000 | bytes 5509120 | tf_op jit(solution)/shard_map/conv_early/pallas_call | solution.py:196
  8.9 0.0 copy-start.8
  8.9 0.0 copy-start
  8.9 0.0 collective-permute-done.2.refs_0_
  8.9 0.0 copy-done.3
  8.9 1.3 %conv_late.1 = bf16[256,256]{1,0:T(8,128)(2,1)S(1)} custom-call(f32[1,1024]{1,0:T(1,128)S(1)} %bitcast.20, bf16[3,1024,768]{2,1,0:T(8,128)(2,1)S(1)} %turn_conv.1.weight_ref, bf16[256,256]{1,0:T(8,128)(2,1)S(1)} %copy-done.3, f32[6,64,256]{2,1,0:T(8,128)S(1)} %conv_early.1.early_ref, bf16[64,1024]{1,0:T(8,128)(2,1)S(1)} %collective-permute-done.2.refs_0_), custom_call_target="tpu_custom_call" | custom-call | flops 1207959552 | bytes 5509120 | tf_op jit(solution)/shard_map/conv_late/pallas_call | solution.py:196
  10.3 0.0 collective-permute-done.4.other_out
  10.3 0.0 collective-permute-done.3.other_ref
  10.3 0.0 copy-done.8
  10.3 0.1 collective-permute-start.5
  10.4 13.7 %all_to_all.10 = bf16[16,16,256]{2,1,0:T(8,128)(2,1)S(1)} all-to-all(bf16[16,16,256]{2,1,0:T(8,128)(2,1)S(1)} %bitcast.11), channel_id=1, replica_groups={{0,1,4,5,8,9,12,13,16,17,20,21,24,25,28,29},{2,3,6,7,10,11,14,15,18,19,..., dimensions={0} | all-to-all | bytes 262144 | tf_op jit(solution)/shard_map/all_to_all | solution.py:218
  24.1 0.0 copy-done
  24.2 0.7 %temporal.1.refs_0_ = bf16[64,1024]{1,0:T(8,128)(2,1)S(1)} custom-call(bf16[8,2,16,256]{3,2,1,0:T(8,128)(2,1)S(1)} %bitcast.13, bf16[3,256,1024]{2,1,0:T(8,128)(2,1)S(1)} %copy-done, bf16[3,256,1024]{2,1,0:T(8,128)(2,1)S(1)} %collective-permute-done.3.other_ref), custom_call_target="tpu_custom_call" | custom-call | flops 201326592 | bytes 3407872 | tf_op jit(solution)/shard_map/temporal/pallas_call | solution.py:196
  24.8 0.0 copy-start.1
  24.8 0.0 copy-start.6
  24.8 0.0 collective-permute-done.5.other_ref
  24.9 1.2 %collective-permute-start.6 = (bf16[64,1024]{1,0:T(8,128)(2,1)S(1)}, bf16[64,1024]{1,0:T(8,128)(2,1)S(1)}, u32[]{:S(2)}, u32[]{:S(2)}) collective-permute-start(bf16[64,1024]{1,0:T(8,128)(2,1)S(1)} %temporal.1.refs_0_), channel_id=1, source_target_pairs={{0,2},{1,3},{2,0},{3,1},{4,6},{5,7},{6,4},{7,5},{8,10},{9,11},{10,... | collective-permute-start | bytes 393224 | tf_op jit(solution)/shard_map/ppermute | solution.py:215
  26.0 0.9 %turn.1.qkv_ref = bf16[2,1024,768]{2,1,0:T(8,128)(2,1)S(1)} custom-call(bf16[3,256,1024]{2,1,0:T(8,128)(2,1)S(1)} %copy-done.8, bf16[3,256,1024]{2,1,0:T(8,128)(2,1)S(1)} %collective-permute-done.5.other_ref), custom_call_target="tpu_custom_call" | custom-call | flops 6000000000 | bytes 6291456 | tf_op jit(solution)/shard_map/turn/pallas_call | solution.py:196
  26.9 3.0 %collective-permute-done.6.refs_1_ = bf16[64,1024]{1,0:T(8,128)(2,1)S(1)} collective-permute-done((bf16[64,1024]{1,0:T(8,128)(2,1)S(1)}, bf16[64,1024]{1,0:T(8,128)(2,1)S(1)}, u32[]{:S(2)}, u32[]{:S(2)}) %collective-permute-start.6) | collective-permute-done | bytes 131104 | tf_op jit(solution)/shard_map/ppermute | solution.py:215
  29.9 0.0 copy-done.1
  29.9 0.0 copy-done.6
  29.9 0.0 copy-start.4
  29.9 1.3 %attend.1 = bf16[256,256]{1,0:T(8,128)(2,1)S(1)} custom-call(f32[1,1024]{1,0:T(1,128)S(1)} %bitcast.21, bf16[2,1024,768]{2,1,0:T(8,128)(2,1)S(1)} %turn.1.qkv_ref, bf16[256,1024]{1,0:T(8,128)(2,1)S(1)} %copy-done.1, bf16[256,1024]{1,0:T(8,128)(2,1)S(1)} %collective-permute-done.4.other_out, bf16[64,1024]{1,0:T(8,128)(2,1)S(1)} %temporal.1.refs_0_, ...), custom_call_target="tpu_custom_call" | custom-call | flops 268435456 | bytes 4591616 | tf_op jit(solution)/shard_map/attend/pallas_call | solution.py:196
  31.2 10.5 %all_to_all.11 = bf16[32,8,256]{2,1,0:T(8,128)(2,1)S(1)} all-to-all(bf16[32,8,256]{2,1,0:T(8,128)(2,1)S(1)} %bitcast.14), channel_id=1, replica_groups=mesh['orbit'=8,'space'=4] {'orbit','space'}, dimensions={0} | all-to-all | bytes 262144 | tf_op jit(solution)/shard_map/all_to_all | solution.py:218
  41.7 0.0 copy-done.4
  41.7 0.8 %restore.1 = bf16[4,16,1024]{2,1,0:T(8,128)(2,1)} custom-call(bf16[256,256]{1,0:T(8,128)(2,1)S(1)} %bitcast.12, bf16[128,256]{1,0:T(8,128)(2,1)S(1)} %copy-done.4, bf16[4,16,1024]{2,1,0:T(8,128)(2,1)S(1)} %bitcast.18), custom_call_target="tpu_custom_call" | custom-call | bytes 458752 | tf_op jit(solution)/shard_map/restore/pallas_call | solution.py:196
Async XLA Ops:
  0.0 7.7 %copy-start.2 = (bf16[4,1,16,1024]{3,2,1,0:T(8,128)(2,1)S(1)}, bf16[4,1,16,1024]{3,2,1,0:T(8,128)(2,1)}, u32[]{:S(2)}) copy-start(bf16[4,1,16,1024]{3,2,1,0:T(8,128)(2,1)} %param.9) | copy-start | bytes 393220
  0.0 7.7 %copy-start.5 = (f32[1024]{0:T(1024)S(1)}, f32[1024]{0:T(1024)}, u32[]{:S(2)}) copy-start(f32[1024]{0:T(1024)} %param.10) | copy-start | bytes 12292
  0.0 7.1 %collective-permute-start = (bf16[64,1024]{1,0:T(8,128)(2,1)}, bf16[64,1024]{1,0:T(8,128)(2,1)S(1)}, u32[]{:S(2)}, u32[]{:S(2)}) collective-permute-start(bf16[64,1024]{1,0:T(8,128)(2,1)} %bitcast.15), channel_id=1, source_target_pairs={{0,2},{1,3},{2,0},{3,1},{4,6},{5,7},{6,4},{7,5},{8,10},{9,11},{10,... | collective-permute-start | bytes 393224 | tf_op jit(solution)/shard_map/ppermute | solution.py:215
  2.9 4.1 %collective-permute-start.1 = (bf16[64,1024]{1,0:T(8,128)(2,1)}, bf16[64,1024]{1,0:T(8,128)(2,1)S(1)}, u32[]{:S(2)}, u32[]{:S(2)}) collective-permute-start(bf16[64,1024]{1,0:T(8,128)(2,1)} %bitcast.16), channel_id=1, source_target_pairs={{0,1},{1,0},{2,3},{3,2},{4,5},{5,4},{6,7},{7,6},{8,9},{9,8},{10,11... | collective-permute-start | bytes 393224 | tf_op jit(solution)/shard_map/ppermute | solution.py:215
  2.9 7.3 %collective-permute-start.3 = (bf16[3,256,1024]{2,1,0:T(8,128)(2,1)}, bf16[3,256,1024]{2,1,0:T(8,128)(2,1)S(1)}, u32[]{:S(2)}, u32[]{:S(2)}) collective-permute-start(bf16[3,256,1024]{2,1,0:T(8,128)(2,1)} %own_ref.1), channel_id=1, source_target_pairs={{0,1},{1,0},{2,3},{3,2},{4,5},{5,4},{6,7},{7,6},{8,9},{9,8},{10,11... | collective-permute-start | bytes 4718600 | tf_op jit(solution)/shard_map/ppermute | solution.py:215
  3.5 6.8 %collective-permute-start.4 = (bf16[256,1024]{1,0:T(8,128)(2,1)}, bf16[256,1024]{1,0:T(8,128)(2,1)S(1)}, u32[]{:S(2)}, u32[]{:S(2)}) collective-permute-start(bf16[256,1024]{1,0:T(8,128)(2,1)} %own_out.1), channel_id=1, source_target_pairs={{0,1},{1,0},{2,3},{3,2},{4,5},{5,4},{6,7},{7,6},{8,9},{9,8},{10,11... | collective-permute-start | bytes 1572872 | tf_op jit(solution)/shard_map/ppermute | solution.py:215
  3.5 2.3 %copy-start.7 = (bf16[3,3,256,1024]{3,2,1,0:T(8,128)(2,1)S(1)}, bf16[3,3,256,1024]{3,2,1,0:T(8,128)(2,1)}, u32[]{:S(2)}) copy-start(bf16[3,3,256,1024]{3,2,1,0:T(8,128)(2,1)} %weight_ref.1) | copy-start | bytes 14155780
  7.1 1.8 %collective-permute-start.2 = (bf16[64,1024]{1,0:T(8,128)(2,1)S(1)}, bf16[64,1024]{1,0:T(8,128)(2,1)S(1)}, u32[]{:S(2)}, u32[]{:S(2)}) collective-permute-start(bf16[64,1024]{1,0:T(8,128)(2,1)S(1)} %collective-permute-done.refs_2_), channel_id=1, source_target_pairs={{0,1},{1,0},{2,3},{3,2},{4,5},{5,4},{6,7},{7,6},{8,9},{9,8},{10,11... | collective-permute-start | bytes 393224 | tf_op jit(solution)/shard_map/ppermute | solution.py:215
  7.7 1.3 %copy-start.3 = (bf16[256,256]{1,0:T(8,128)(2,1)S(1)}, bf16[256,256]{1,0:T(8,128)(2,1)}, u32[]{:S(2)}) copy-start(bf16[256,256]{1,0:T(8,128)(2,1)} %constant.4.clone.order_ref) | copy-start | bytes 393220
  8.9 1.4 %copy-start.8 = (bf16[3,256,1024]{2,1,0:T(8,128)(2,1)S(1)}, bf16[3,256,1024]{2,1,0:T(8,128)(2,1)}, u32[]{:S(2)}) copy-start(bf16[3,256,1024]{2,1,0:T(8,128)(2,1)} %own_ref.2) | copy-start | bytes 4718596
  8.9 15.3 %copy-start = (bf16[3,256,1024]{2,1,0:T(8,128)(2,1)S(1)}, bf16[3,256,1024]{2,1,0:T(8,128)(2,1)}, u32[]{:S(2)}) copy-start(bf16[3,256,1024]{2,1,0:T(8,128)(2,1)} %own_ref.1) | copy-start | bytes 4718596
  10.3 14.5 %collective-permute-start.5 = (bf16[3,256,1024]{2,1,0:T(8,128)(2,1)S(1)}, bf16[3,256,1024]{2,1,0:T(8,128)(2,1)S(1)}, u32[]{:S(2)}, u32[]{:S(2)}) collective-permute-start(bf16[3,256,1024]{2,1,0:T(8,128)(2,1)S(1)} %copy-done.8), channel_id=1, source_target_pairs={{0,1},{1,0},{2,3},{3,2},{4,5},{5,4},{6,7},{7,6},{8,9},{9,8},{10,11... | collective-permute-start | bytes 4718600 | tf_op jit(solution)/shard_map/ppermute | solution.py:215
  24.8 5.1 %copy-start.1 = (bf16[256,1024]{1,0:T(8,128)(2,1)S(1)}, bf16[256,1024]{1,0:T(8,128)(2,1)}, u32[]{:S(2)}) copy-start(bf16[256,1024]{1,0:T(8,128)(2,1)} %own_out.1) | copy-start | bytes 1572868
  24.8 5.1 %copy-start.6 = (f32[1024]{0:T(1024)S(1)}, f32[1024]{0:T(1024)}, u32[]{:S(2)}) copy-start(f32[1024]{0:T(1024)} %param.13) | copy-start | bytes 12292
  24.9 5.0 %collective-permute-start.6 = (bf16[64,1024]{1,0:T(8,128)(2,1)S(1)}, bf16[64,1024]{1,0:T(8,128)(2,1)S(1)}, u32[]{:S(2)}, u32[]{:S(2)}) collective-permute-start(bf16[64,1024]{1,0:T(8,128)(2,1)S(1)} %temporal.1.refs_0_), channel_id=1, source_target_pairs={{0,2},{1,3},{2,0},{3,1},{4,6},{5,7},{6,4},{7,5},{8,10},{9,11},{10,... | collective-permute-start | bytes 393224 | tf_op jit(solution)/shard_map/ppermute | solution.py:215
  29.9 11.8 %copy-start.4 = (bf16[128,256]{1,0:T(8,128)(2,1)S(1)}, bf16[128,256]{1,0:T(8,128)(2,1)}, u32[]{:S(2)}) copy-start(bf16[128,256]{1,0:T(8,128)(2,1)} %constant.5.clone.order_ref) | copy-start | bytes 196612

commit v9 on v8

--- a/solution.py
+++ b/solution.py
@@ -43,6 +43,7 @@
         self.by_column = share % CORES == 0
         self.ncol = share // CORES if self.by_column else share
         self.rows = space if self.by_column else self.x
+        self.strided = self.by_column and self.ncol == 1 and slice_chans % 128 == 0
         self.pixels = self.rows * self.ncol
         self.pairs = views // 2
         self.down_rows = self.pairs * orbit * self.pixels
@@ -86,7 +87,8 @@
         right = jnp.where(column == cols - 1, 0.0, pltpu.roll(right, count - 1, 0))
         part = left + middle + right
         for n, place in enumerate(places):
-            total[place + 2 - i] += part[n * per_row : (n + 1) * per_row]
+            start = pl.multiple_of((place + 2 - i) * per_row, per_row)
+            total[pl.ds(start, per_row)] += part[n * per_row : (n + 1) * per_row]
 
 
 def early_kernel(plan, gain_ref, weight_ref, *refs):
@@ -98,16 +100,28 @@
     add_rows(plan, blocks, places, weight_ref, total_ref)
 
 
-def late_kernel(plan, gain_ref, weight_ref, order_ref, early_ref, *refs):
-    raw_refs, (out_ref, total) = refs[:-2], refs[-2:]
+def late_kernel(plan, gain_ref, weight_ref, early_ref, *refs):
+    order_refs, raw_refs, (out_ref, total, tiles) = refs[: 1 - plan.strided], refs[1 - plan.strided : -3], refs[-3:]
     gain, space = gain_ref[...], lax.axis_index("space")
     blocks = [rms_scale(ref[...].astype(F32), gain).astype(BF16) for ref in raw_refs]
     places = [space ^ (x * CORES + 1) for x in range(1, plan.x)]
     total[...] = early_ref[...]
     add_rows(plan, blocks, places, weight_ref, total)
-    whole = total[1 : plan.space + 1].reshape(plan.space * plan.views * plan.cols, plan.slice_chans)
-    activated = (whole / (1.0 + jnp.exp(-whole))).astype(BF16)
-    out_ref[...] = dot(order_ref[...], activated).astype(BF16)
+    per_row, cols, depth = plan.views * plan.cols, plan.cols, plan.slice_chans
+    if plan.strided:
+        lanes = [slice(k * 128, (k + 1) * 128) for k in range(depth // 128)]
+        for k, lane in enumerate(lanes):
+            whole = total[per_row : (plan.space + 1) * per_row, lane]
+            tiles[k] = whole / (1.0 + jnp.exp(-whole))
+        half = plan.send_rows // 2
+        for column in range(cols):
+            for k, lane in enumerate(lanes):
+                picked = [tiles[k, pl.ds(odd * cols + column, half, stride=2 * cols), :] for odd in range(2)]
+                out_ref[column * plan.send_rows : (column + 1) * plan.send_rows, lane] = jnp.concatenate(picked).astype(BF16)
+    else:
+        whole = total[per_row : (plan.space + 1) * per_row]
+        activated = (whole / (1.0 + jnp.exp(-whole))).astype(BF16)
+        out_ref[...] = dot(order_refs[0][...], activated).astype(BF16)
 
 
 def temporal_kernel(plan, got_ref, own_ref, other_ref, out_ref):
@@ -228,7 +242,8 @@
     other_temporal, other_out = swap(temporal_weight, 1), swap(out_weight, 1)
     far, near, taps = lax.optimization_barrier((far, near, taps))
     across = [swap(block, 1) for block in far]
-    total_shape = (space + 2, per_row, depth)
+    total_shape = ((space + 2) * per_row, depth)
+    order = [] if plan.strided else [plan.send_order()]
     (early,) = call(
         functools.partial(early_kernel, plan),
         "conv_early",
@@ -241,8 +256,8 @@
         functools.partial(late_kernel, plan),
         "conv_late",
         [(count, depth)],
-        (conv_gain, taps, plan.send_order(), early, *across),
-        [pltpu.VMEM(total_shape, F32)],
+        (conv_gain, taps, early, *order, *across),
+        [pltpu.VMEM(total_shape, F32), pltpu.VMEM((max(depth // 128, 1), count, 128), F32)],
         flops=2 * 9 * count * chans * depth,
     )
     swapped = (other_temporal, other_out)

time: 42.7 us -> 42.7 us (level)
    unnamed x18 -> x16, local copies, waits for them, and re-layouts: 2.39 us -> 2.47 us
  transfers between devices with their start and end apart: 7 -> 7, of which waited for: 1 -> 1; matrix products, arithmetic and copies ran while one was open for 0% -> 0% of each run, Pallas kernels for 13% -> 12%
where the time goes in v9:
time: 42.7 us; the launch traced here: 42.5 us
  blocking collectives  24.2 us (57%)
  Pallas kernels  7.41 us (17%)
  starting transfers between devices  5.28 us (12%)
  waiting for transfers between devices  2.98 us (7%)
  local copies, waits for them, and re-layouts  2.47 us (6%)
    all_to_all x2, blocking collectives, exchange(): lax.all_to_all(blocks, ('orbit', 'space'), 0, 0, tiled=True, axis_index_g...  24.2 us
    pallas_call x7, Pallas kernels, call(): pl.pallas_call(kernel, out_shape=outs, in_specs=[pl.BlockSpec(memory_spac...  7.41 us
    ppermute x7, starting transfers between devices, swap(): lax.ppermute(block, 'space', [(s, s ^ distance) for s in range(space)])  5.28 us
    ppermute x7, waiting for transfers between devices, swap(): lax.ppermute(block, 'space', [(s, s ^ distance) for s in range(space)])  2.98 us
    unnamed x16, local copies, waits for them, and re-layouts  2.47 us
  transfers between devices with their start and end apart: 7, of which 1 were waited for; matrix products, arithmetic and copies ran while one was open for 0% of the time, Pallas kernels for 12%

profile of v9, /device:TPU:0, one launch (start us, length us, event | category | flops | bytes accessed | tf_op | source)
XLA Modules:
  0.0 42.5 jit_solution(3518688602137228579)
XLA Ops:
  0.0 0.0 copy-start.2
  0.0 0.0 copy-start.4
  0.0 2.9 %collective-permute-start = (bf16[64,1024]{1,0:T(8,128)(2,1)}, bf16[64,1024]{1,0:T(8,128)(2,1)S(1)}, u32[]{:S(2)}, u32[]{:S(2)}) collective-permute-start(bf16[64,1024]{1,0:T(8,128)(2,1)} %bitcast.15), channel_id=1, source_target_pairs={{0,2},{1,3},{2,0},{3,1},{4,6},{5,7},{6,4},{7,5},{8,10},{9,11},{10,... | collective-permute-start | bytes 393224 | tf_op jit(solution)/shard_map/ppermute | solution.py:229
  2.9 0.0 collective-permute-start.1
  2.9 0.5 %collective-permute-start.3 = (bf16[3,256,1024]{2,1,0:T(8,128)(2,1)}, bf16[3,256,1024]{2,1,0:T(8,128)(2,1)S(1)}, u32[]{:S(2)}, u32[]{:S(2)}) collective-permute-start(bf16[3,256,1024]{2,1,0:T(8,128)(2,1)} %own_ref.1), channel_id=1, source_target_pairs={{0,1},{1,0},{2,3},{3,2},{4,5},{5,4},{6,7},{7,6},{8,9},{9,8},{10,11... | collective-permute-start | bytes 4718600 | tf_op jit(solution)/shard_map/ppermute | solution.py:229
  3.5 0.0 collective-permute-start.4
  3.5 0.0 copy-start.6
  3.5 2.3 %copy-done.6 = bf16[3,3,256,1024]{3,2,1,0:T(8,128)(2,1)S(1)} copy-done((bf16[3,3,256,1024]{3,2,1,0:T(8,128)(2,1)S(1)}, bf16[3,3,256,1024]{3,2,1,0:T(8,128)(2,1)}, u32[]{:S(2)}) %copy-start.6) | copy-done | bytes 4718616
  5.8 1.3 %turn_conv.1.weight_ref = bf16[3,1024,768]{2,1,0:T(8,128)(2,1)S(1)} custom-call(bf16[3,3,256,1024]{3,2,1,0:T(8,128)(2,1)S(1)} %copy-done.6), custom_call_target="tpu_custom_call" | custom-call | flops 60000002048 | bytes 9437184 | tf_op jit(solution)/shard_map/turn_conv/pallas_call | solution.py:210
  7.1 0.0 collective-permute-done.refs_2_
  7.1 0.0 collective-permute-done.1.refs_1_
  7.1 0.6 %collective-permute-start.2 = (bf16[64,1024]{1,0:T(8,128)(2,1)S(1)}, bf16[64,1024]{1,0:T(8,128)(2,1)S(1)}, u32[]{:S(2)}, u32[]{:S(2)}) collective-permute-start(bf16[64,1024]{1,0:T(8,128)(2,1)S(1)} %collective-permute-done.refs_2_), channel_id=1, source_target_pairs={{0,1},{1,0},{2,3},{3,2},{4,5},{5,4},{6,7},{7,6},{8,9},{9,8},{10,11... | collective-permute-start | bytes 393224 | tf_op jit(solution)/shard_map/ppermute | solution.py:229
  7.7 0.0 copy-done.2
  7.7 0.0 copy-done.4
  7.7 1.2 %conv_early.1.early_ref = f32[384,256]{1,0:T(8,128)S(1)} custom-call(f32[1,1024]{1,0:T(1,128)S(1)} %bitcast.19, bf16[3,1024,768]{2,1,0:T(8,128)(2,1)S(1)} %turn_conv.1.weight_ref, bf16[64,1024]{1,0:T(8,128)(2,1)S(1)} %bitcast.17, bf16[64,1024]{1,0:T(8,128)(2,1)S(1)} %collective-permute-done.1.refs_1_, bf16[64,1024]{1,0:T(8,128)(2,1)S(1)} %collective-permute-done.refs_2_), custom_call_target="tpu_custom_call" | custom-call | flops 6000000000 | bytes 5509120 | tf_op jit(solution)/shard_map/conv_early/pallas_call | solution.py:210
  8.9 0.0 copy-start.7
  8.9 0.0 copy-start
  8.9 0.0 collective-permute-done.2.refs_0_
  8.9 1.3 %conv_late.1 = bf16[256,256]{1,0:T(8,128)(2,1)S(1)} custom-call(f32[1,1024]{1,0:T(1,128)S(1)} %bitcast.20, bf16[3,1024,768]{2,1,0:T(8,128)(2,1)S(1)} %turn_conv.1.weight_ref, f32[384,256]{1,0:T(8,128)S(1)} %conv_early.1.early_ref, bf16[64,1024]{1,0:T(8,128)(2,1)S(1)} %collective-permute-done.2.refs_0_), custom_call_target="tpu_custom_call" | custom-call | flops 1207959552 | bytes 5378048 | tf_op jit(solution)/shard_map/conv_late/pallas_call | solution.py:210
  10.2 0.0 collective-permute-done.4.other_out
  10.2 0.0 collective-permute-done.3.other_ref
  10.2 0.1 copy-done.7
  10.3 0.1 collective-permute-start.5
  10.4 13.7 %all_to_all.10 = bf16[16,16,256]{2,1,0:T(8,128)(2,1)S(1)} all-to-all(bf16[16,16,256]{2,1,0:T(8,128)(2,1)S(1)} %bitcast.11), channel_id=1, replica_groups={{0,1,4,5,8,9,12,13,16,17,20,21,24,25,28,29},{2,3,6,7,10,11,14,15,18,19,..., dimensions={0} | all-to-all | bytes 262144 | tf_op jit(solution)/shard_map/all_to_all | solution.py:232
  24.1 0.0 copy-done
  24.1 0.7 %temporal.1.refs_0_ = bf16[64,1024]{1,0:T(8,128)(2,1)S(1)} custom-call(bf16[8,2,16,256]{3,2,1,0:T(8,128)(2,1)S(1)} %bitcast.13, bf16[3,256,1024]{2,1,0:T(8,128)(2,1)S(1)} %copy-done, bf16[3,256,1024]{2,1,0:T(8,128)(2,1)S(1)} %collective-permute-done.3.other_ref), custom_call_target="tpu_custom_call" | custom-call | flops 201326592 | bytes 3407872 | tf_op jit(solution)/shard_map/temporal/pallas_call | solution.py:210
  24.7 0.0 copy-start.1
  24.8 0.0 copy-start.5
  24.8 0.0 collective-permute-done.5.other_ref
  24.8 1.2 %collective-permute-start.6 = (bf16[64,1024]{1,0:T(8,128)(2,1)S(1)}, bf16[64,1024]{1,0:T(8,128)(2,1)S(1)}, u32[]{:S(2)}, u32[]{:S(2)}) collective-permute-start(bf16[64,1024]{1,0:T(8,128)(2,1)S(1)} %temporal.1.refs_0_), channel_id=1, source_target_pairs={{0,2},{1,3},{2,0},{3,1},{4,6},{5,7},{6,4},{7,5},{8,10},{9,11},{10,... | collective-permute-start | bytes 393224 | tf_op jit(solution)/shard_map/ppermute | solution.py:229
  26.0 0.9 %turn.1.qkv_ref = bf16[2,1024,768]{2,1,0:T(8,128)(2,1)S(1)} custom-call(bf16[3,256,1024]{2,1,0:T(8,128)(2,1)S(1)} %copy-done.7, bf16[3,256,1024]{2,1,0:T(8,128)(2,1)S(1)} %collective-permute-done.5.other_ref), custom_call_target="tpu_custom_call" | custom-call | flops 6000000000 | bytes 6291456 | tf_op jit(solution)/shard_map/turn/pallas_call | solution.py:210
  26.8 3.0 %collective-permute-done.6.refs_1_ = bf16[64,1024]{1,0:T(8,128)(2,1)S(1)} collective-permute-done((bf16[64,1024]{1,0:T(8,128)(2,1)S(1)}, bf16[64,1024]{1,0:T(8,128)(2,1)S(1)}, u32[]{:S(2)}, u32[]{:S(2)}) %collective-permute-start.6) | collective-permute-done | bytes 131104 | tf_op jit(solution)/shard_map/ppermute | solution.py:229
  29.8 0.0 copy-done.1
  29.8 0.0 copy-done.5
  29.8 0.0 copy-start.3
  29.8 1.3 %attend.1 = bf16[256,256]{1,0:T(8,128)(2,1)S(1)} custom-call(f32[1,1024]{1,0:T(1,128)S(1)} %bitcast.21, bf16[2,1024,768]{2,1,0:T(8,128)(2,1)S(1)} %turn.1.qkv_ref, bf16[256,1024]{1,0:T(8,128)(2,1)S(1)} %copy-done.1, bf16[256,1024]{1,0:T(8,128)(2,1)S(1)} %collective-permute-done.4.other_out, bf16[64,1024]{1,0:T(8,128)(2,1)S(1)} %temporal.1.refs_0_, ...), custom_call_target="tpu_custom_call" | custom-call | flops 268435456 | bytes 4591616 | tf_op jit(solution)/shard_map/attend/pallas_call | solution.py:210
  31.1 10.5 %all_to_all.11 = bf16[32,8,256]{2,1,0:T(8,128)(2,1)S(1)} all-to-all(bf16[32,8,256]{2,1,0:T(8,128)(2,1)S(1)} %bitcast.14), channel_id=1, replica_groups=mesh['orbit'=8,'space'=4] {'orbit','space'}, dimensions={0} | all-to-all | bytes 262144 | tf_op jit(solution)/shard_map/all_to_all | solution.py:232
  41.6 0.0 copy-done.3
  41.6 0.8 %restore.1 = bf16[4,16,1024]{2,1,0:T(8,128)(2,1)} custom-call(bf16[256,256]{1,0:T(8,128)(2,1)S(1)} %bitcast.12, bf16[128,256]{1,0:T(8,128)(2,1)S(1)} %copy-done.3, bf16[4,16,1024]{2,1,0:T(8,128)(2,1)S(1)} %bitcast.18), custom_call_target="tpu_custom_call" | custom-call | bytes 458752 | tf_op jit(solution)/shard_map/restore/pallas_call | solution.py:210
Async XLA Ops:
  0.0 7.7 %copy-start.2 = (bf16[4,1,16,1024]{3,2,1,0:T(8,128)(2,1)S(1)}, bf16[4,1,16,1024]{3,2,1,0:T(8,128)(2,1)}, u32[]{:S(2)}) copy-start(bf16[4,1,16,1024]{3,2,1,0:T(8,128)(2,1)} %param.8) | copy-start | bytes 393220
  0.0 7.7 %copy-start.4 = (f32[1024]{0:T(1024)S(1)}, f32[1024]{0:T(1024)}, u32[]{:S(2)}) copy-start(f32[1024]{0:T(1024)} %param.9) | copy-start | bytes 12292
  0.0 7.1 %collective-permute-start = (bf16[64,1024]{1,0:T(8,128)(2,1)}, bf16[64,1024]{1,0:T(8,128)(2,1)S(1)}, u32[]{:S(2)}, u32[]{:S(2)}) collective-permute-start(bf16[64,1024]{1,0:T(8,128)(2,1)} %bitcast.15), channel_id=1, source_target_pairs={{0,2},{1,3},{2,0},{3,1},{4,6},{5,7},{6,4},{7,5},{8,10},{9,11},{10,... | collective-permute-start | bytes 393224 | tf_op jit(solution)/shard_map/ppermute | solution.py:229
  2.9 4.1 %collective-permute-start.1 = (bf16[64,1024]{1,0:T(8,128)(2,1)}, bf16[64,1024]{1,0:T(8,128)(2,1)S(1)}, u32[]{:S(2)}, u32[]{:S(2)}) collective-permute-start(bf16[64,1024]{1,0:T(8,128)(2,1)} %bitcast.16), channel_id=1, source_target_pairs={{0,1},{1,0},{2,3},{3,2},{4,5},{5,4},{6,7},{7,6},{8,9},{9,8},{10,11... | collective-permute-start | bytes 393224 | tf_op jit(solution)/shard_map/ppermute | solution.py:229
  2.9 7.2 %collective-permute-start.3 = (bf16[3,256,1024]{2,1,0:T(8,128)(2,1)}, bf16[3,256,1024]{2,1,0:T(8,128)(2,1)S(1)}, u32[]{:S(2)}, u32[]{:S(2)}) collective-permute-start(bf16[3,256,1024]{2,1,0:T(8,128)(2,1)} %own_ref.1), channel_id=1, source_target_pairs={{0,1},{1,0},{2,3},{3,2},{4,5},{5,4},{6,7},{7,6},{8,9},{9,8},{10,11... | collective-permute-start | bytes 4718600 | tf_op jit(solution)/shard_map/ppermute | solution.py:229
  3.5 6.7 %collective-permute-start.4 = (bf16[256,1024]{1,0:T(8,128)(2,1)}, bf16[256,1024]{1,0:T(8,128)(2,1)S(1)}, u32[]{:S(2)}, u32[]{:S(2)}) collective-permute-start(bf16[256,1024]{1,0:T(8,128)(2,1)} %own_out.1), channel_id=1, source_target_pairs={{0,1},{1,0},{2,3},{3,2},{4,5},{5,4},{6,7},{7,6},{8,9},{9,8},{10,11... | collective-permute-start | bytes 1572872 | tf_op jit(solution)/shard_map/ppermute | solution.py:229
  3.5 2.3 %copy-start.6 = (bf16[3,3,256,1024]{3,2,1,0:T(8,128)(2,1)S(1)}, bf16[3,3,256,1024]{3,2,1,0:T(8,128)(2,1)}, u32[]{:S(2)}) copy-start(bf16[3,3,256,1024]{3,2,1,0:T(8,128)(2,1)} %weight_ref.1) | copy-start | bytes 14155780
  7.1 1.8 %collective-permute-start.2 = (bf16[64,1024]{1,0:T(8,128)(2,1)S(1)}, bf16[64,1024]{1,0:T(8,128)(2,1)S(1)}, u32[]{:S(2)}, u32[]{:S(2)}) collective-permute-start(bf16[64,1024]{1,0:T(8,128)(2,1)S(1)} %collective-permute-done.refs_2_), channel_id=1, source_target_pairs={{0,1},{1,0},{2,3},{3,2},{4,5},{5,4},{6,7},{7,6},{8,9},{9,8},{10,11... | collective-permute-start | bytes 393224 | tf_op jit(solution)/shard_map/ppermute | solution.py:229
  8.9 1.4 %copy-start.7 = (bf16[3,256,1024]{2,1,0:T(8,128)(2,1)S(1)}, bf16[3,256,1024]{2,1,0:T(8,128)(2,1)}, u32[]{:S(2)}) copy-start(bf16[3,256,1024]{2,1,0:T(8,128)(2,1)} %own_ref.2) | copy-start | bytes 4718596
  8.9 15.2 %copy-start = (bf16[3,256,1024]{2,1,0:T(8,128)(2,1)S(1)}, bf16[3,256,1024]{2,1,0:T(8,128)(2,1)}, u32[]{:S(2)}) copy-start(bf16[3,256,1024]{2,1,0:T(8,128)(2,1)} %own_ref.1) | copy-start | bytes 4718596
  10.3 14.5 %collective-permute-start.5 = (bf16[3,256,1024]{2,1,0:T(8,128)(2,1)S(1)}, bf16[3,256,1024]{2,1,0:T(8,128)(2,1)S(1)}, u32[]{:S(2)}, u32[]{:S(2)}) collective-permute-start(bf16[3,256,1024]{2,1,0:T(8,128)(2,1)S(1)} %copy-done.7), channel_id=1, source_target_pairs={{0,1},{1,0},{2,3},{3,2},{4,5},{5,4},{6,7},{7,6},{8,9},{9,8},{10,11... | collective-permute-start | bytes 4718600 | tf_op jit(solution)/shard_map/ppermute | solution.py:229
  24.7 5.1 %copy-start.1 = (bf16[256,1024]{1,0:T(8,128)(2,1)S(1)}, bf16[256,1024]{1,0:T(8,128)(2,1)}, u32[]{:S(2)}) copy-start(bf16[256,1024]{1,0:T(8,128)(2,1)} %own_out.1) | copy-start | bytes 1572868
  24.8 5.1 %copy-start.5 = (f32[1024]{0:T(1024)S(1)}, f32[1024]{0:T(1024)}, u32[]{:S(2)}) copy-start(f32[1024]{0:T(1024)} %param.12) | copy-start | bytes 12292
  24.8 5.0 %collective-permute-start.6 = (bf16[64,1024]{1,0:T(8,128)(2,1)S(1)}, bf16[64,1024]{1,0:T(8,128)(2,1)S(1)}, u32[]{:S(2)}, u32[]{:S(2)}) collective-permute-start(bf16[64,1024]{1,0:T(8,128)(2,1)S(1)} %temporal.1.refs_0_), channel_id=1, source_target_pairs={{0,2},{1,3},{2,0},{3,1},{4,6},{5,7},{6,4},{7,5},{8,10},{9,11},{10,... | collective-permute-start | bytes 393224 | tf_op jit(solution)/shard_map/ppermute | solution.py:229
  29.8 11.8 %copy-start.3 = (bf16[128,256]{1,0:T(8,128)(2,1)S(1)}, bf16[128,256]{1,0:T(8,128)(2,1)}, u32[]{:S(2)}) copy-start(bf16[128,256]{1,0:T(8,128)(2,1)} %constant.2.clone.order_ref) | copy-start | bytes 196612

commit v10 on v9

--- a/solution.py
+++ b/solution.py
@@ -129,16 +129,15 @@
     half, depth = plan.send_rows // 2, plan.slice_chans
     row = lax.broadcasted_iota(jnp.int32, (plan.down_rows, 1), 0)
     first = (row & (plan.back - 1)) < plan.ncol
-    total = None
+    lefts, rights = [], []
     for index, weight_ref in ((core, own_ref), (1 - core, other_ref)):
         block = got_ref[:, index].astype(F32)
         even = block[:, :half].reshape(plan.down_rows, depth)
         odd = block[:, half:].reshape(plan.down_rows, depth)
         before = jnp.where(first, pltpu.roll(odd, half - plan.back + plan.ncol, 0), pltpu.roll(odd, plan.ncol, 0))
-        for k, rows in enumerate((before, even, odd)):
-            part = dot(rows.astype(BF16), weight_ref[k])
-            total = part if total is None else total + part
-    out_ref[...] = total.astype(BF16)
+        lefts += [before.astype(BF16), even.astype(BF16), odd.astype(BF16)]
+        rights.append(weight_ref[...].reshape(3 * depth, plan.chans))
+    out_ref[...] = dot(jnp.concatenate(lefts, axis=1), jnp.concatenate(rights)).astype(BF16)
 
 
 def turn_kernel(own_ref, other_ref, out_ref):

time: 42.7 us -> 42.7 us (level)
  no operation moved by 1% of the time
where the time goes in v10:
time: 42.7 us; the launch traced here: 42.5 us
  blocking collectives  24.2 us (57%)
  Pallas kernels  7.4 us (17%)
  starting transfers between devices  5.28 us (12%)
  waiting for transfers between devices  2.98 us (7%)
  local copies, waits for them, and re-layouts  2.47 us (6%)
    all_to_all x2, blocking collectives, exchange(): lax.all_to_all(blocks, ('orbit', 'space'), 0, 0, tiled=True, axis_index_g...  24.2 us
    pallas_call x7, Pallas kernels, call(): pl.pallas_call(kernel, out_shape=outs, in_specs=[pl.BlockSpec(memory_spac...  7.4 us
    ppermute x7, starting transfers between devices, swap(): lax.ppermute(block, 'space', [(s, s ^ distance) for s in range(space)])  5.28 us
    ppermute x7, waiting for transfers between devices, swap(): lax.ppermute(block, 'space', [(s, s ^ distance) for s in range(space)])  2.98 us
    unnamed x16, local copies, waits for them, and re-layouts  2.47 us
  transfers between devices with their start and end apart: 7, of which 1 were waited for; matrix products, arithmetic and copies ran while one was open for 0% of the time, Pallas kernels for 12%

profile of v10, /device:TPU:0, one launch (start us, length us, event | category | flops | bytes accessed | tf_op | source)
XLA Modules:
  0.0 42.5 jit_solution(17640512971562551431)
XLA Ops:
  0.0 0.0 copy-start.2
  0.0 0.0 copy-start.4
  0.0 2.9 %collective-permute-start = (bf16[64,1024]{1,0:T(8,128)(2,1)}, bf16[64,1024]{1,0:T(8,128)(2,1)S(1)}, u32[]{:S(2)}, u32[]{:S(2)}) collective-permute-start(bf16[64,1024]{1,0:T(8,128)(2,1)} %bitcast.15), channel_id=1, source_target_pairs={{0,2},{1,3},{2,0},{3,1},{4,6},{5,7},{6,4},{7,5},{8,10},{9,11},{10,... | collective-permute-start | bytes 393224 | tf_op jit(solution)/shard_map/ppermute | solution.py:228
  2.9 0.0 collective-permute-start.1
  2.9 0.5 %collective-permute-start.3 = (bf16[3,256,1024]{2,1,0:T(8,128)(2,1)}, bf16[3,256,1024]{2,1,0:T(8,128)(2,1)S(1)}, u32[]{:S(2)}, u32[]{:S(2)}) collective-permute-start(bf16[3,256,1024]{2,1,0:T(8,128)(2,1)} %own_ref.1), channel_id=1, source_target_pairs={{0,1},{1,0},{2,3},{3,2},{4,5},{5,4},{6,7},{7,6},{8,9},{9,8},{10,11... | collective-permute-start | bytes 4718600 | tf_op jit(solution)/shard_map/ppermute | solution.py:228
  3.5 0.0 collective-permute-start.4
  3.5 0.0 copy-start.6
  3.5 2.3 %copy-done.6 = bf16[3,3,256,1024]{3,2,1,0:T(8,128)(2,1)S(1)} copy-done((bf16[3,3,256,1024]{3,2,1,0:T(8,128)(2,1)S(1)}, bf16[3,3,256,1024]{3,2,1,0:T(8,128)(2,1)}, u32[]{:S(2)}) %copy-start.6) | copy-done | bytes 4718616
  5.8 1.3 %turn_conv.1.weight_ref = bf16[3,1024,768]{2,1,0:T(8,128)(2,1)S(1)} custom-call(bf16[3,3,256,1024]{3,2,1,0:T(8,128)(2,1)S(1)} %copy-done.6), custom_call_target="tpu_custom_call" | custom-call | flops 60000002048 | bytes 9437184 | tf_op jit(solution)/shard_map/turn_conv/pallas_call | solution.py:209
  7.1 0.0 collective-permute-done.refs_2_
  7.1 0.0 collective-permute-done.1.refs_1_
  7.1 0.6 %collective-permute-start.2 = (bf16[64,1024]{1,0:T(8,128)(2,1)S(1)}, bf16[64,1024]{1,0:T(8,128)(2,1)S(1)}, u32[]{:S(2)}, u32[]{:S(2)}) collective-permute-start(bf16[64,1024]{1,0:T(8,128)(2,1)S(1)} %collective-permute-done.refs_2_), channel_id=1, source_target_pairs={{0,1},{1,0},{2,3},{3,2},{4,5},{5,4},{6,7},{7,6},{8,9},{9,8},{10,11... | collective-permute-start | bytes 393224 | tf_op jit(solution)/shard_map/ppermute | solution.py:228
  7.7 0.0 copy-done.2
  7.7 0.0 copy-done.4
  7.7 1.2 %conv_early.1.early_ref = f32[384,256]{1,0:T(8,128)S(1)} custom-call(f32[1,1024]{1,0:T(1,128)S(1)} %bitcast.19, bf16[3,1024,768]{2,1,0:T(8,128)(2,1)S(1)} %turn_conv.1.weight_ref, bf16[64,1024]{1,0:T(8,128)(2,1)S(1)} %bitcast.17, bf16[64,1024]{1,0:T(8,128)(2,1)S(1)} %collective-permute-done.1.refs_1_, bf16[64,1024]{1,0:T(8,128)(2,1)S(1)} %collective-permute-done.refs_2_), custom_call_target="tpu_custom_call" | custom-call | flops 6000000000 | bytes 5509120 | tf_op jit(solution)/shard_map/conv_early/pallas_call | solution.py:209
  8.9 0.0 copy-start.7
  8.9 0.0 copy-start
  8.9 0.0 collective-permute-done.2.refs_0_
  8.9 1.3 %conv_late.1 = bf16[256,256]{1,0:T(8,128)(2,1)S(1)} custom-call(f32[1,1024]{1,0:T(1,128)S(1)} %bitcast.20, bf16[3,1024,768]{2,1,0:T(8,128)(2,1)S(1)} %turn_conv.1.weight_ref, f32[384,256]{1,0:T(8,128)S(1)} %conv_early.1.early_ref, bf16[64,1024]{1,0:T(8,128)(2,1)S(1)} %collective-permute-done.2.refs_0_), custom_call_target="tpu_custom_call" | custom-call | flops 1207959552 | bytes 5378048 | tf_op jit(solution)/shard_map/conv_late/pallas_call | solution.py:209
  10.2 0.0 collective-permute-done.4.other_out
  10.2 0.0 collective-permute-done.3.other_ref
  10.2 0.1 copy-done.7
  10.3 0.1 collective-permute-start.5
  10.4 13.7 %all_to_all.10 = bf16[16,16,256]{2,1,0:T(8,128)(2,1)S(1)} all-to-all(bf16[16,16,256]{2,1,0:T(8,128)(2,1)S(1)} %bitcast.11), channel_id=1, replica_groups={{0,1,4,5,8,9,12,13,16,17,20,21,24,25,28,29},{2,3,6,7,10,11,14,15,18,19,..., dimensions={0} | all-to-all | bytes 262144 | tf_op jit(solution)/shard_map/all_to_all | solution.py:231
  24.1 0.0 copy-done
  24.1 0.7 %temporal.1.refs_0_ = bf16[64,1024]{1,0:T(8,128)(2,1)S(1)} custom-call(bf16[8,2,16,256]{3,2,1,0:T(8,128)(2,1)S(1)} %bitcast.13, bf16[3,256,1024]{2,1,0:T(8,128)(2,1)S(1)} %copy-done, bf16[3,256,1024]{2,1,0:T(8,128)(2,1)S(1)} %collective-permute-done.3.other_ref), custom_call_target="tpu_custom_call" | custom-call | flops 201326592 | bytes 3407872 | tf_op jit(solution)/shard_map/temporal/pallas_call | solution.py:209
  24.7 0.0 copy-start.1
  24.8 0.0 copy-start.5
  24.8 0.0 collective-permute-done.5.other_ref
  24.8 1.2 %collective-permute-start.6 = (bf16[64,1024]{1,0:T(8,128)(2,1)S(1)}, bf16[64,1024]{1,0:T(8,128)(2,1)S(1)}, u32[]{:S(2)}, u32[]{:S(2)}) collective-permute-start(bf16[64,1024]{1,0:T(8,128)(2,1)S(1)} %temporal.1.refs_0_), channel_id=1, source_target_pairs={{0,2},{1,3},{2,0},{3,1},{4,6},{5,7},{6,4},{7,5},{8,10},{9,11},{10,... | collective-permute-start | bytes 393224 | tf_op jit(solution)/shard_map/ppermute | solution.py:228
  26.0 0.9 %turn.1.qkv_ref = bf16[2,1024,768]{2,1,0:T(8,128)(2,1)S(1)} custom-call(bf16[3,256,1024]{2,1,0:T(8,128)(2,1)S(1)} %copy-done.7, bf16[3,256,1024]{2,1,0:T(8,128)(2,1)S(1)} %collective-permute-done.5.other_ref), custom_call_target="tpu_custom_call" | custom-call | flops 6000000000 | bytes 6291456 | tf_op jit(solution)/shard_map/turn/pallas_call | solution.py:209
  26.8 3.0 %collective-permute-done.6.refs_1_ = bf16[64,1024]{1,0:T(8,128)(2,1)S(1)} collective-permute-done((bf16[64,1024]{1,0:T(8,128)(2,1)S(1)}, bf16[64,1024]{1,0:T(8,128)(2,1)S(1)}, u32[]{:S(2)}, u32[]{:S(2)}) %collective-permute-start.6) | collective-permute-done | bytes 131104 | tf_op jit(solution)/shard_map/ppermute | solution.py:228
  29.8 0.0 copy-done.1
  29.8 0.0 copy-done.5
  29.8 0.0 copy-start.3
  29.8 1.3 %attend.1 = bf16[256,256]{1,0:T(8,128)(2,1)S(1)} custom-call(f32[1,1024]{1,0:T(1,128)S(1)} %bitcast.21, bf16[2,1024,768]{2,1,0:T(8,128)(2,1)S(1)} %turn.1.qkv_ref, bf16[256,1024]{1,0:T(8,128)(2,1)S(1)} %copy-done.1, bf16[256,1024]{1,0:T(8,128)(2,1)S(1)} %collective-permute-done.4.other_out, bf16[64,1024]{1,0:T(8,128)(2,1)S(1)} %temporal.1.refs_0_, ...), custom_call_target="tpu_custom_call" | custom-call | flops 268435456 | bytes 4591616 | tf_op jit(solution)/shard_map/attend/pallas_call | solution.py:209
  31.1 10.5 %all_to_all.11 = bf16[32,8,256]{2,1,0:T(8,128)(2,1)S(1)} all-to-all(bf16[32,8,256]{2,1,0:T(8,128)(2,1)S(1)} %bitcast.14), channel_id=1, replica_groups=mesh['orbit'=8,'space'=4] {'orbit','space'}, dimensions={0} | all-to-all | bytes 262144 | tf_op jit(solution)/shard_map/all_to_all | solution.py:231
  41.6 0.0 copy-done.3
  41.6 0.8 %restore.1 = bf16[4,16,1024]{2,1,0:T(8,128)(2,1)} custom-call(bf16[256,256]{1,0:T(8,128)(2,1)S(1)} %bitcast.12, bf16[128,256]{1,0:T(8,128)(2,1)S(1)} %copy-done.3, bf16[4,16,1024]{2,1,0:T(8,128)(2,1)S(1)} %bitcast.18), custom_call_target="tpu_custom_call" | custom-call | bytes 458752 | tf_op jit(solution)/shard_map/restore/pallas_call | solution.py:209
Async XLA Ops:
  0.0 7.7 %copy-start.2 = (bf16[4,1,16,1024]{3,2,1,0:T(8,128)(2,1)S(1)}, bf16[4,1,16,1024]{3,2,1,0:T(8,128)(2,1)}, u32[]{:S(2)}) copy-start(bf16[4,1,16,1024]{3,2,1,0:T(8,128)(2,1)} %param.8) | copy-start | bytes 393220
  0.0 7.7 %copy-start.4 = (f32[1024]{0:T(1024)S(1)}, f32[1024]{0:T(1024)}, u32[]{:S(2)}) copy-start(f32[1024]{0:T(1024)} %param.9) | copy-start | bytes 12292
  0.0 7.1 %collective-permute-start = (bf16[64,1024]{1,0:T(8,128)(2,1)}, bf16[64,1024]{1,0:T(8,128)(2,1)S(1)}, u32[]{:S(2)}, u32[]{:S(2)}) collective-permute-start(bf16[64,1024]{1,0:T(8,128)(2,1)} %bitcast.15), channel_id=1, source_target_pairs={{0,2},{1,3},{2,0},{3,1},{4,6},{5,7},{6,4},{7,5},{8,10},{9,11},{10,... | collective-permute-start | bytes 393224 | tf_op jit(solution)/shard_map/ppermute | solution.py:228
  2.9 4.1 %collective-permute-start.1 = (bf16[64,1024]{1,0:T(8,128)(2,1)}, bf16[64,1024]{1,0:T(8,128)(2,1)S(1)}, u32[]{:S(2)}, u32[]{:S(2)}) collective-permute-start(bf16[64,1024]{1,0:T(8,128)(2,1)} %bitcast.16), channel_id=1, source_target_pairs={{0,1},{1,0},{2,3},{3,2},{4,5},{5,4},{6,7},{7,6},{8,9},{9,8},{10,11... | collective-permute-start | bytes 393224 | tf_op jit(solution)/shard_map/ppermute | solution.py:228
  2.9 7.2 %collective-permute-start.3 = (bf16[3,256,1024]{2,1,0:T(8,128)(2,1)}, bf16[3,256,1024]{2,1,0:T(8,128)(2,1)S(1)}, u32[]{:S(2)}, u32[]{:S(2)}) collective-permute-start(bf16[3,256,1024]{2,1,0:T(8,128)(2,1)} %own_ref.1), channel_id=1, source_target_pairs={{0,1},{1,0},{2,3},{3,2},{4,5},{5,4},{6,7},{7,6},{8,9},{9,8},{10,11... | collective-permute-start | bytes 4718600 | tf_op jit(solution)/shard_map/ppermute | solution.py:228
  3.5 6.7 %collective-permute-start.4 = (bf16[256,1024]{1,0:T(8,128)(2,1)}, bf16[256,1024]{1,0:T(8,128)(2,1)S(1)}, u32[]{:S(2)}, u32[]{:S(2)}) collective-permute-start(bf16[256,1024]{1,0:T(8,128)(2,1)} %own_out.1), channel_id=1, source_target_pairs={{0,1},{1,0},{2,3},{3,2},{4,5},{5,4},{6,7},{7,6},{8,9},{9,8},{10,11... | collective-permute-start | bytes 1572872 | tf_op jit(solution)/shard_map/ppermute | solution.py:228
  3.5 2.3 %copy-start.6 = (bf16[3,3,256,1024]{3,2,1,0:T(8,128)(2,1)S(1)}, bf16[3,3,256,1024]{3,2,1,0:T(8,128)(2,1)}, u32[]{:S(2)}) copy-start(bf16[3,3,256,1024]{3,2,1,0:T(8,128)(2,1)} %weight_ref.1) | copy-start | bytes 14155780
  7.1 1.8 %collective-permute-start.2 = (bf16[64,1024]{1,0:T(8,128)(2,1)S(1)}, bf16[64,1024]{1,0:T(8,128)(2,1)S(1)}, u32[]{:S(2)}, u32[]{:S(2)}) collective-permute-start(bf16[64,1024]{1,0:T(8,128)(2,1)S(1)} %collective-permute-done.refs_2_), channel_id=1, source_target_pairs={{0,1},{1,0},{2,3},{3,2},{4,5},{5,4},{6,7},{7,6},{8,9},{9,8},{10,11... | collective-permute-start | bytes 393224 | tf_op jit(solution)/shard_map/ppermute | solution.py:228
  8.9 1.4 %copy-start.7 = (bf16[3,256,1024]{2,1,0:T(8,128)(2,1)S(1)}, bf16[3,256,1024]{2,1,0:T(8,128)(2,1)}, u32[]{:S(2)}) copy-start(bf16[3,256,1024]{2,1,0:T(8,128)(2,1)} %own_ref.2) | copy-start | bytes 4718596
  8.9 15.2 %copy-start = (bf16[3,256,1024]{2,1,0:T(8,128)(2,1)S(1)}, bf16[3,256,1024]{2,1,0:T(8,128)(2,1)}, u32[]{:S(2)}) copy-start(bf16[3,256,1024]{2,1,0:T(8,128)(2,1)} %own_ref.1) | copy-start | bytes 4718596
  10.3 14.5 %collective-permute-start.5 = (bf16[3,256,1024]{2,1,0:T(8,128)(2,1)S(1)}, bf16[3,256,1024]{2,1,0:T(8,128)(2,1)S(1)}, u32[]{:S(2)}, u32[]{:S(2)}) collective-permute-start(bf16[3,256,1024]{2,1,0:T(8,128)(2,1)S(1)} %copy-done.7), channel_id=1, source_target_pairs={{0,1},{1,0},{2,3},{3,2},{4,5},{5,4},{6,7},{7,6},{8,9},{9,8},{10,11... | collective-permute-start | bytes 4718600 | tf_op jit(solution)/shard_map/ppermute | solution.py:228
  24.7 5.1 %copy-start.1 = (bf16[256,1024]{1,0:T(8,128)(2,1)S(1)}, bf16[256,1024]{1,0:T(8,128)(2,1)}, u32[]{:S(2)}) copy-start(bf16[256,1024]{1,0:T(8,128)(2,1)} %own_out.1) | copy-start | bytes 1572868
  24.8 5.1 %copy-start.5 = (f32[1024]{0:T(1024)S(1)}, f32[1024]{0:T(1024)}, u32[]{:S(2)}) copy-start(f32[1024]{0:T(1024)} %param.12) | copy-start | bytes 12292
  24.8 5.0 %collective-permute-start.6 = (bf16[64,1024]{1,0:T(8,128)(2,1)S(1)}, bf16[64,1024]{1,0:T(8,128)(2,1)S(1)}, u32[]{:S(2)}, u32[]{:S(2)}) collective-permute-start(bf16[64,1024]{1,0:T(8,128)(2,1)S(1)} %temporal.1.refs_0_), channel_id=1, source_target_pairs={{0,2},{1,3},{2,0},{3,1},{4,6},{5,7},{6,4},{7,5},{8,10},{9,11},{10,... | collective-permute-start | bytes 393224 | tf_op jit(solution)/shard_map/ppermute | solution.py:228
  29.8 11.8 %copy-start.3 = (bf16[128,256]{1,0:T(8,128)(2,1)S(1)}, bf16[128,256]{1,0:T(8,128)(2,1)}, u32[]{:S(2)}) copy-start(bf16[128,256]{1,0:T(8,128)(2,1)} %constant.2.clone.order_ref) | copy-start | bytes 196612

commit v11 on v10

--- a/solution.py
+++ b/solution.py
@@ -186,7 +186,8 @@
             top = peak if h == 0 else jnp.where(key_head >= h, peak, top)
         weights.append(jnp.exp(score - top).astype(BF16))
     mixed = [(dot(w, v) / dot(w, spread)).astype(BF16) for w, v in zip(weights, values)]
-    projected = projected + dot(mixed[0], own_out[...]) + dot(mixed[1], other_out[...])
+    weight = jnp.concatenate([own_out[...], other_out[...]])
+    projected = projected + dot(jnp.concatenate(mixed, axis=1), weight)
     width = plan.back_width
     parts = [projected[:, k * width : (k + 1) * width] for k in range(plan.lanes)]
     parts = [part.reshape(plan.peers, plan.back, width) for part in parts]

time: 42.7 us -> 42.7 us (level)
  no operation moved by 1% of the time
where the time goes in v11:
time: 42.7 us; the launch traced here: 42.5 us
  blocking collectives  24.2 us (57%)
  Pallas kernels  7.41 us (17%)
  starting transfers between devices  5.28 us (12%)
  waiting for transfers between devices  2.98 us (7%)
  local copies, waits for them, and re-layouts  2.47 us (6%)
    all_to_all x2, blocking collectives, exchange(): lax.all_to_all(blocks, ('orbit', 'space'), 0, 0, tiled=True, axis_index_g...  24.2 us
    pallas_call x7, Pallas kernels, call(): pl.pallas_call(kernel, out_shape=outs, in_specs=[pl.BlockSpec(memory_spac...  7.41 us
    ppermute x7, starting transfers between devices, swap(): lax.ppermute(block, 'space', [(s, s ^ distance) for s in range(space)])  5.28 us
    ppermute x7, waiting for transfers between devices, swap(): lax.ppermute(block, 'space', [(s, s ^ distance) for s in range(space)])  2.98 us
    unnamed x16, local copies, waits for them, and re-layouts  2.47 us
  transfers between devices with their start and end apart: 7, of which 1 were waited for; matrix products, arithmetic and copies ran while one was open for 0% of the time, Pallas kernels for 12%

profile of v11, /device:TPU:0, one launch (start us, length us, event | category | flops | bytes accessed | tf_op | source)
XLA Modules:
  0.0 42.5 jit_solution(12244509555352767827)
XLA Ops:
  0.0 0.0 copy-start.2
  0.0 0.0 copy-start.4
  0.0 2.9 %collective-permute-start = (bf16[64,1024]{1,0:T(8,128)(2,1)}, bf16[64,1024]{1,0:T(8,128)(2,1)S(1)}, u32[]{:S(2)}, u32[]{:S(2)}) collective-permute-start(bf16[64,1024]{1,0:T(8,128)(2,1)} %bitcast.15), channel_id=1, source_target_pairs={{0,2},{1,3},{2,0},{3,1},{4,6},{5,7},{6,4},{7,5},{8,10},{9,11},{10,... | collective-permute-start | bytes 393224 | tf_op jit(solution)/shard_map/ppermute | solution.py:229
  2.9 0.0 collective-permute-start.1
  2.9 0.5 %collective-permute-start.3 = (bf16[3,256,1024]{2,1,0:T(8,128)(2,1)}, bf16[3,256,1024]{2,1,0:T(8,128)(2,1)S(1)}, u32[]{:S(2)}, u32[]{:S(2)}) collective-permute-start(bf16[3,256,1024]{2,1,0:T(8,128)(2,1)} %own_ref.1), channel_id=1, source_target_pairs={{0,1},{1,0},{2,3},{3,2},{4,5},{5,4},{6,7},{7,6},{8,9},{9,8},{10,11... | collective-permute-start | bytes 4718600 | tf_op jit(solution)/shard_map/ppermute | solution.py:229
  3.5 0.0 collective-permute-start.4
  3.5 0.0 copy-start.6
  3.5 2.3 %copy-done.6 = bf16[3,3,256,1024]{3,2,1,0:T(8,128)(2,1)S(1)} copy-done((bf16[3,3,256,1024]{3,2,1,0:T(8,128)(2,1)S(1)}, bf16[3,3,256,1024]{3,2,1,0:T(8,128)(2,1)}, u32[]{:S(2)}) %copy-start.6) | copy-done | bytes 4718616
  5.8 1.3 %turn_conv.1.weight_ref = bf16[3,1024,768]{2,1,0:T(8,128)(2,1)S(1)} custom-call(bf16[3,3,256,1024]{3,2,1,0:T(8,128)(2,1)S(1)} %copy-done.6), custom_call_target="tpu_custom_call" | custom-call | flops 60000002048 | bytes 9437184 | tf_op jit(solution)/shard_map/turn_conv/pallas_call | solution.py:210
  7.1 0.0 collective-permute-done.refs_2_
  7.1 0.0 collective-permute-done.1.refs_1_
  7.1 0.6 %collective-permute-start.2 = (bf16[64,1024]{1,0:T(8,128)(2,1)S(1)}, bf16[64,1024]{1,0:T(8,128)(2,1)S(1)}, u32[]{:S(2)}, u32[]{:S(2)}) collective-permute-start(bf16[64,1024]{1,0:T(8,128)(2,1)S(1)} %collective-permute-done.refs_2_), channel_id=1, source_target_pairs={{0,1},{1,0},{2,3},{3,2},{4,5},{5,4},{6,7},{7,6},{8,9},{9,8},{10,11... | collective-permute-start | bytes 393224 | tf_op jit(solution)/shard_map/ppermute | solution.py:229
  7.7 0.0 copy-done.2
  7.7 0.0 copy-done.4
  7.7 1.2 %conv_early.1.early_ref = f32[384,256]{1,0:T(8,128)S(1)} custom-call(f32[1,1024]{1,0:T(1,128)S(1)} %bitcast.19, bf16[3,1024,768]{2,1,0:T(8,128)(2,1)S(1)} %turn_conv.1.weight_ref, bf16[64,1024]{1,0:T(8,128)(2,1)S(1)} %bitcast.17, bf16[64,1024]{1,0:T(8,128)(2,1)S(1)} %collective-permute-done.1.refs_1_, bf16[64,1024]{1,0:T(8,128)(2,1)S(1)} %collective-permute-done.refs_2_), custom_call_target="tpu_custom_call" | custom-call | flops 6000000000 | bytes 5509120 | tf_op jit(solution)/shard_map/conv_early/pallas_call | solution.py:210
  8.9 0.0 copy-start.7
  8.9 0.0 copy-start
  8.9 0.0 collective-permute-done.2.refs_0_
  8.9 1.3 %conv_late.1 = bf16[256,256]{1,0:T(8,128)(2,1)S(1)} custom-call(f32[1,1024]{1,0:T(1,128)S(1)} %bitcast.20, bf16[3,1024,768]{2,1,0:T(8,128)(2,1)S(1)} %turn_conv.1.weight_ref, f32[384,256]{1,0:T(8,128)S(1)} %conv_early.1.early_ref, bf16[64,1024]{1,0:T(8,128)(2,1)S(1)} %collective-permute-done.2.refs_0_), custom_call_target="tpu_custom_call" | custom-call | flops 1207959552 | bytes 5378048 | tf_op jit(solution)/shard_map/conv_late/pallas_call | solution.py:210
  10.2 0.0 collective-permute-done.4.other_out
  10.2 0.0 collective-permute-done.3.other_ref
  10.2 0.1 copy-done.7
  10.3 0.1 collective-permute-start.5
  10.4 13.7 %all_to_all.10 = bf16[16,16,256]{2,1,0:T(8,128)(2,1)S(1)} all-to-all(bf16[16,16,256]{2,1,0:T(8,128)(2,1)S(1)} %bitcast.11), channel_id=1, replica_groups={{0,1,4,5,8,9,12,13,16,17,20,21,24,25,28,29},{2,3,6,7,10,11,14,15,18,19,..., dimensions={0} | all-to-all | bytes 262144 | tf_op jit(solution)/shard_map/all_to_all | solution.py:232
  24.1 0.0 copy-done
  24.1 0.7 %temporal.1.refs_0_ = bf16[64,1024]{1,0:T(8,128)(2,1)S(1)} custom-call(bf16[8,2,16,256]{3,2,1,0:T(8,128)(2,1)S(1)} %bitcast.13, bf16[3,256,1024]{2,1,0:T(8,128)(2,1)S(1)} %copy-done, bf16[3,256,1024]{2,1,0:T(8,128)(2,1)S(1)} %collective-permute-done.3.other_ref), custom_call_target="tpu_custom_call" | custom-call | flops 201326592 | bytes 3407872 | tf_op jit(solution)/shard_map/temporal/pallas_call | solution.py:210
  24.7 0.0 copy-start.1
  24.8 0.0 copy-start.5
  24.8 0.0 collective-permute-done.5.other_ref
  24.8 1.2 %collective-permute-start.6 = (bf16[64,1024]{1,0:T(8,128)(2,1)S(1)}, bf16[64,1024]{1,0:T(8,128)(2,1)S(1)}, u32[]{:S(2)}, u32[]{:S(2)}) collective-permute-start(bf16[64,1024]{1,0:T(8,128)(2,1)S(1)} %temporal.1.refs_0_), channel_id=1, source_target_pairs={{0,2},{1,3},{2,0},{3,1},{4,6},{5,7},{6,4},{7,5},{8,10},{9,11},{10,... | collective-permute-start | bytes 393224 | tf_op jit(solution)/shard_map/ppermute | solution.py:229
  26.0 0.9 %turn.1.qkv_ref = bf16[2,1024,768]{2,1,0:T(8,128)(2,1)S(1)} custom-call(bf16[3,256,1024]{2,1,0:T(8,128)(2,1)S(1)} %copy-done.7, bf16[3,256,1024]{2,1,0:T(8,128)(2,1)S(1)} %collective-permute-done.5.other_ref), custom_call_target="tpu_custom_call" | custom-call | flops 6000000000 | bytes 6291456 | tf_op jit(solution)/shard_map/turn/pallas_call | solution.py:210
  26.8 3.0 %collective-permute-done.6.refs_1_ = bf16[64,1024]{1,0:T(8,128)(2,1)S(1)} collective-permute-done((bf16[64,1024]{1,0:T(8,128)(2,1)S(1)}, bf16[64,1024]{1,0:T(8,128)(2,1)S(1)}, u32[]{:S(2)}, u32[]{:S(2)}) %collective-permute-start.6) | collective-permute-done | bytes 131104 | tf_op jit(solution)/shard_map/ppermute | solution.py:229
  29.8 0.0 copy-done.1
  29.8 0.0 copy-done.5
  29.8 0.0 copy-start.3
  29.8 1.3 %attend.1 = bf16[256,256]{1,0:T(8,128)(2,1)S(1)} custom-call(f32[1,1024]{1,0:T(1,128)S(1)} %bitcast.21, bf16[2,1024,768]{2,1,0:T(8,128)(2,1)S(1)} %turn.1.qkv_ref, bf16[256,1024]{1,0:T(8,128)(2,1)S(1)} %copy-done.1, bf16[256,1024]{1,0:T(8,128)(2,1)S(1)} %collective-permute-done.4.other_out, bf16[64,1024]{1,0:T(8,128)(2,1)S(1)} %temporal.1.refs_0_, ...), custom_call_target="tpu_custom_call" | custom-call | flops 268435456 | bytes 4591616 | tf_op jit(solution)/shard_map/attend/pallas_call | solution.py:210
  31.2 10.5 %all_to_all.11 = bf16[32,8,256]{2,1,0:T(8,128)(2,1)S(1)} all-to-all(bf16[32,8,256]{2,1,0:T(8,128)(2,1)S(1)} %bitcast.14), channel_id=1, replica_groups=mesh['orbit'=8,'space'=4] {'orbit','space'}, dimensions={0} | all-to-all | bytes 262144 | tf_op jit(solution)/shard_map/all_to_all | solution.py:232
  41.6 0.0 copy-done.3
  41.6 0.8 %restore.1 = bf16[4,16,1024]{2,1,0:T(8,128)(2,1)} custom-call(bf16[256,256]{1,0:T(8,128)(2,1)S(1)} %bitcast.12, bf16[128,256]{1,0:T(8,128)(2,1)S(1)} %copy-done.3, bf16[4,16,1024]{2,1,0:T(8,128)(2,1)S(1)} %bitcast.18), custom_call_target="tpu_custom_call" | custom-call | bytes 458752 | tf_op jit(solution)/shard_map/restore/pallas_call | solution.py:210
Async XLA Ops:
  0.0 7.7 %copy-start.2 = (bf16[4,1,16,1024]{3,2,1,0:T(8,128)(2,1)S(1)}, bf16[4,1,16,1024]{3,2,1,0:T(8,128)(2,1)}, u32[]{:S(2)}) copy-start(bf16[4,1,16,1024]{3,2,1,0:T(8,128)(2,1)} %param.8) | copy-start | bytes 393220
  0.0 7.7 %copy-start.4 = (f32[1024]{0:T(1024)S(1)}, f32[1024]{0:T(1024)}, u32[]{:S(2)}) copy-start(f32[1024]{0:T(1024)} %param.9) | copy-start | bytes 12292
  0.0 7.1 %collective-permute-start = (bf16[64,1024]{1,0:T(8,128)(2,1)}, bf16[64,1024]{1,0:T(8,128)(2,1)S(1)}, u32[]{:S(2)}, u32[]{:S(2)}) collective-permute-start(bf16[64,1024]{1,0:T(8,128)(2,1)} %bitcast.15), channel_id=1, source_target_pairs={{0,2},{1,3},{2,0},{3,1},{4,6},{5,7},{6,4},{7,5},{8,10},{9,11},{10,... | collective-permute-start | bytes 393224 | tf_op jit(solution)/shard_map/ppermute | solution.py:229
  2.9 4.1 %collective-permute-start.1 = (bf16[64,1024]{1,0:T(8,128)(2,1)}, bf16[64,1024]{1,0:T(8,128)(2,1)S(1)}, u32[]{:S(2)}, u32[]{:S(2)}) collective-permute-start(bf16[64,1024]{1,0:T(8,128)(2,1)} %bitcast.16), channel_id=1, source_target_pairs={{0,1},{1,0},{2,3},{3,2},{4,5},{5,4},{6,7},{7,6},{8,9},{9,8},{10,11... | collective-permute-start | bytes 393224 | tf_op jit(solution)/shard_map/ppermute | solution.py:229
  2.9 7.2 %collective-permute-start.3 = (bf16[3,256,1024]{2,1,0:T(8,128)(2,1)}, bf16[3,256,1024]{2,1,0:T(8,128)(2,1)S(1)}, u32[]{:S(2)}, u32[]{:S(2)}) collective-permute-start(bf16[3,256,1024]{2,1,0:T(8,128)(2,1)} %own_ref.1), channel_id=1, source_target_pairs={{0,1},{1,0},{2,3},{3,2},{4,5},{5,4},{6,7},{7,6},{8,9},{9,8},{10,11... | collective-permute-start | bytes 4718600 | tf_op jit(solution)/shard_map/ppermute | solution.py:229
  3.5 6.7 %collective-permute-start.4 = (bf16[256,1024]{1,0:T(8,128)(2,1)}, bf16[256,1024]{1,0:T(8,128)(2,1)S(1)}, u32[]{:S(2)}, u32[]{:S(2)}) collective-permute-start(bf16[256,1024]{1,0:T(8,128)(2,1)} %own_out.1), channel_id=1, source_target_pairs={{0,1},{1,0},{2,3},{3,2},{4,5},{5,4},{6,7},{7,6},{8,9},{9,8},{10,11... | collective-permute-start | bytes 1572872 | tf_op jit(solution)/shard_map/ppermute | solution.py:229
  3.5 2.3 %copy-start.6 = (bf16[3,3,256,1024]{3,2,1,0:T(8,128)(2,1)S(1)}, bf16[3,3,256,1024]{3,2,1,0:T(8,128)(2,1)}, u32[]{:S(2)}) copy-start(bf16[3,3,256,1024]{3,2,1,0:T(8,128)(2,1)} %weight_ref.1) | copy-start | bytes 14155780
  7.1 1.8 %collective-permute-start.2 = (bf16[64,1024]{1,0:T(8,128)(2,1)S(1)}, bf16[64,1024]{1,0:T(8,128)(2,1)S(1)}, u32[]{:S(2)}, u32[]{:S(2)}) collective-permute-start(bf16[64,1024]{1,0:T(8,128)(2,1)S(1)} %collective-permute-done.refs_2_), channel_id=1, source_target_pairs={{0,1},{1,0},{2,3},{3,2},{4,5},{5,4},{6,7},{7,6},{8,9},{9,8},{10,11... | collective-permute-start | bytes 393224 | tf_op jit(solution)/shard_map/ppermute | solution.py:229
  8.9 1.4 %copy-start.7 = (bf16[3,256,1024]{2,1,0:T(8,128)(2,1)S(1)}, bf16[3,256,1024]{2,1,0:T(8,128)(2,1)}, u32[]{:S(2)}) copy-start(bf16[3,256,1024]{2,1,0:T(8,128)(2,1)} %own_ref.2) | copy-start | bytes 4718596
  8.9 15.2 %copy-start = (bf16[3,256,1024]{2,1,0:T(8,128)(2,1)S(1)}, bf16[3,256,1024]{2,1,0:T(8,128)(2,1)}, u32[]{:S(2)}) copy-start(bf16[3,256,1024]{2,1,0:T(8,128)(2,1)} %own_ref.1) | copy-start | bytes 4718596
  10.3 14.5 %collective-permute-start.5 = (bf16[3,256,1024]{2,1,0:T(8,128)(2,1)S(1)}, bf16[3,256,1024]{2,1,0:T(8,128)(2,1)S(1)}, u32[]{:S(2)}, u32[]{:S(2)}) collective-permute-start(bf16[3,256,1024]{2,1,0:T(8,128)(2,1)S(1)} %copy-done.7), channel_id=1, source_target_pairs={{0,1},{1,0},{2,3},{3,2},{4,5},{5,4},{6,7},{7,6},{8,9},{9,8},{10,11... | collective-permute-start | bytes 4718600 | tf_op jit(solution)/shard_map/ppermute | solution.py:229
  24.7 5.1 %copy-start.1 = (bf16[256,1024]{1,0:T(8,128)(2,1)S(1)}, bf16[256,1024]{1,0:T(8,128)(2,1)}, u32[]{:S(2)}) copy-start(bf16[256,1024]{1,0:T(8,128)(2,1)} %own_out.1) | copy-start | bytes 1572868
  24.8 5.1 %copy-start.5 = (f32[1024]{0:T(1024)S(1)}, f32[1024]{0:T(1024)}, u32[]{:S(2)}) copy-start(f32[1024]{0:T(1024)} %param.12) | copy-start | bytes 12292
  24.8 5.0 %collective-permute-start.6 = (bf16[64,1024]{1,0:T(8,128)(2,1)S(1)}, bf16[64,1024]{1,0:T(8,128)(2,1)S(1)}, u32[]{:S(2)}, u32[]{:S(2)}) collective-permute-start(bf16[64,1024]{1,0:T(8,128)(2,1)S(1)} %temporal.1.refs_0_), channel_id=1, source_target_pairs={{0,2},{1,3},{2,0},{3,1},{4,6},{5,7},{6,4},{7,5},{8,10},{9,11},{10,... | collective-permute-start | bytes 393224 | tf_op jit(solution)/shard_map/ppermute | solution.py:229
  29.8 11.8 %copy-start.3 = (bf16[128,256]{1,0:T(8,128)(2,1)S(1)}, bf16[128,256]{1,0:T(8,128)(2,1)}, u32[]{:S(2)}) copy-start(bf16[128,256]{1,0:T(8,128)(2,1)} %constant.2.clone.order_ref) | copy-start | bytes 196612

commit v12 on v9

--- a/solution.py
+++ b/solution.py
@@ -52,6 +52,7 @@
         self.back = self.pairs * self.ncol
         self.lanes = next(n for n in (1, 2, 4, 8) if self.back * n % 8 == 0)
         self.back_rows, self.back_width = self.back * self.lanes, chans // self.lanes
+        self.tiled = self.back_width % 128 == 0
 
     def column(self, o, core, c):
         return (o * CORES + core) * self.ncol + c if self.by_column else o * self.ncol + c
@@ -148,7 +149,7 @@
 
 
 def attend_kernel(plan, gain_ref, qkv_ref, own_out, other_out, *refs):
-    down_refs, out_ref = refs[:-1], refs[-1]
+    down_refs, (out_ref, tiles, leaving) = refs[:-3], refs[-3:]
     rows, depth = plan.down_rows, plan.slice_chans
     heads = depth // HD
     down = down_refs[0][...].astype(F32)
@@ -189,9 +190,20 @@
     mixed = [(dot(w, v) / dot(w, spread)).astype(BF16) for w, v in zip(weights, values)]
     projected = projected + dot(mixed[0], own_out[...]) + dot(mixed[1], other_out[...])
     width = plan.back_width
-    parts = [projected[:, k * width : (k + 1) * width] for k in range(plan.lanes)]
-    parts = [part.reshape(plan.peers, plan.back, width) for part in parts]
-    out_ref[...] = jnp.concatenate(parts, axis=1).reshape(plan.peers * plan.back_rows, width).astype(BF16)
+    if plan.tiled:
+        for lane in range(plan.chans // 128):
+            tiles[lane] = projected[:, lane * 128 : (lane + 1) * 128]
+        wide = width // 128
+        for lane in range(plan.chans // 128):
+            for t in range(plan.back):
+                source = tiles[lane, pl.ds(t, plan.peers, stride=plan.back), :]
+                leaving[lane % wide, pl.ds(lane // wide * plan.back + t, plan.peers, stride=plan.back_rows), :] = source
+        for lane in range(wide):
+            out_ref[:, lane * 128 : (lane + 1) * 128] = leaving[lane].astype(BF16)
+    else:
+        parts = [projected[:, k * width : (k + 1) * width] for k in range(plan.lanes)]
+        parts = [part.reshape(plan.peers, plan.back, width) for part in parts]
+        out_ref[...] = jnp.concatenate(parts, axis=1).reshape(plan.peers * plan.back_rows, width).astype(BF16)
 
 
 def end_kernel(plan, got_ref, order_ref, latents_ref, out_ref):
@@ -286,6 +298,10 @@
         "attend",
         [(peers * plan.back_rows, plan.back_width)],
         (attn_gain, qkv, out_weight, other_out, *downs),
+        [
+            pltpu.VMEM((chans // 128, plan.down_rows, 128), F32),
+            pltpu.VMEM((max(plan.back_width // 128, 1), peers * plan.back_rows, 128), F32),
+        ],
         flops=2 * 8 * plan.down_rows * chans * plan.slice_chans,
     )
     got = exchange(back.reshape(peers, plan.back_rows, plan.back_width), None if plan.by_column else by_x)

time: 42.7 us -> 42.7 us (level)
  no operation moved by 1% of the time
where the time goes in v12:
time: 42.7 us; the launch traced here: 42.5 us
  blocking collectives  24.2 us (57%)
  Pallas kernels  7.39 us (17%)
  starting transfers between devices  5.28 us (12%)
  waiting for transfers between devices  2.98 us (7%)
  local copies, waits for them, and re-layouts  2.47 us (6%)
    all_to_all x2, blocking collectives, exchange(): lax.all_to_all(blocks, ('orbit', 'space'), 0, 0, tiled=True, axis_index_g...  24.2 us
    pallas_call x7, Pallas kernels, call(): pl.pallas_call(kernel, out_shape=outs, in_specs=[pl.BlockSpec(memory_spac...  7.39 us
    ppermute x7, starting transfers between devices, swap(): lax.ppermute(block, 'space', [(s, s ^ distance) for s in range(space)])  5.28 us
    ppermute x7, waiting for transfers between devices, swap(): lax.ppermute(block, 'space', [(s, s ^ distance) for s in range(space)])  2.98 us
    unnamed x16, local copies, waits for them, and re-layouts  2.47 us
  transfers between devices with their start and end apart: 7, of which 1 were waited for; matrix products, arithmetic and copies ran while one was open for 0% of the time, Pallas kernels for 12%

profile of v12, /device:TPU:0, one launch (start us, length us, event | category | flops | bytes accessed | tf_op | source)
XLA Modules:
  0.0 42.5 jit_solution(1374742787322195307)
XLA Ops:
  0.0 0.0 copy-start.2
  0.0 0.0 copy-start.4
  0.0 2.9 %collective-permute-start = (bf16[64,1024]{1,0:T(8,128)(2,1)}, bf16[64,1024]{1,0:T(8,128)(2,1)S(1)}, u32[]{:S(2)}, u32[]{:S(2)}) collective-permute-start(bf16[64,1024]{1,0:T(8,128)(2,1)} %bitcast.15), channel_id=1, source_target_pairs={{0,2},{1,3},{2,0},{3,1},{4,6},{5,7},{6,4},{7,5},{8,10},{9,11},{10,... | collective-permute-start | bytes 393224 | tf_op jit(solution)/shard_map/ppermute | solution.py:241
  2.9 0.0 collective-permute-start.1
  2.9 0.5 %collective-permute-start.3 = (bf16[3,256,1024]{2,1,0:T(8,128)(2,1)}, bf16[3,256,1024]{2,1,0:T(8,128)(2,1)S(1)}, u32[]{:S(2)}, u32[]{:S(2)}) collective-permute-start(bf16[3,256,1024]{2,1,0:T(8,128)(2,1)} %own_ref.1), channel_id=1, source_target_pairs={{0,1},{1,0},{2,3},{3,2},{4,5},{5,4},{6,7},{7,6},{8,9},{9,8},{10,11... | collective-permute-start | bytes 4718600 | tf_op jit(solution)/shard_map/ppermute | solution.py:241
  3.5 0.0 collective-permute-start.4
  3.5 0.0 copy-start.6
  3.5 2.3 %copy-done.6 = bf16[3,3,256,1024]{3,2,1,0:T(8,128)(2,1)S(1)} copy-done((bf16[3,3,256,1024]{3,2,1,0:T(8,128)(2,1)S(1)}, bf16[3,3,256,1024]{3,2,1,0:T(8,128)(2,1)}, u32[]{:S(2)}) %copy-start.6) | copy-done | bytes 4718616
  5.8 1.3 %turn_conv.1.weight_ref = bf16[3,1024,768]{2,1,0:T(8,128)(2,1)S(1)} custom-call(bf16[3,3,256,1024]{3,2,1,0:T(8,128)(2,1)S(1)} %copy-done.6), custom_call_target="tpu_custom_call" | custom-call | flops 60000002048 | bytes 9437184 | tf_op jit(solution)/shard_map/turn_conv/pallas_call | solution.py:222
  7.1 0.0 collective-permute-done.refs_2_
  7.1 0.0 collective-permute-done.1.refs_1_
  7.1 0.6 %collective-permute-start.2 = (bf16[64,1024]{1,0:T(8,128)(2,1)S(1)}, bf16[64,1024]{1,0:T(8,128)(2,1)S(1)}, u32[]{:S(2)}, u32[]{:S(2)}) collective-permute-start(bf16[64,1024]{1,0:T(8,128)(2,1)S(1)} %collective-permute-done.refs_2_), channel_id=1, source_target_pairs={{0,1},{1,0},{2,3},{3,2},{4,5},{5,4},{6,7},{7,6},{8,9},{9,8},{10,11... | collective-permute-start | bytes 393224 | tf_op jit(solution)/shard_map/ppermute | solution.py:241
  7.7 0.0 copy-done.2
  7.7 0.0 copy-done.4
  7.7 1.2 %conv_early.1.early_ref = f32[384,256]{1,0:T(8,128)S(1)} custom-call(f32[1,1024]{1,0:T(1,128)S(1)} %bitcast.19, bf16[3,1024,768]{2,1,0:T(8,128)(2,1)S(1)} %turn_conv.1.weight_ref, bf16[64,1024]{1,0:T(8,128)(2,1)S(1)} %bitcast.17, bf16[64,1024]{1,0:T(8,128)(2,1)S(1)} %collective-permute-done.1.refs_1_, bf16[64,1024]{1,0:T(8,128)(2,1)S(1)} %collective-permute-done.refs_2_), custom_call_target="tpu_custom_call" | custom-call | flops 6000000000 | bytes 5509120 | tf_op jit(solution)/shard_map/conv_early/pallas_call | solution.py:222
  8.9 0.0 copy-start.7
  8.9 0.0 copy-start
  8.9 0.0 collective-permute-done.2.refs_0_
  8.9 1.3 %conv_late.1 = bf16[256,256]{1,0:T(8,128)(2,1)S(1)} custom-call(f32[1,1024]{1,0:T(1,128)S(1)} %bitcast.20, bf16[3,1024,768]{2,1,0:T(8,128)(2,1)S(1)} %turn_conv.1.weight_ref, f32[384,256]{1,0:T(8,128)S(1)} %conv_early.1.early_ref, bf16[64,1024]{1,0:T(8,128)(2,1)S(1)} %collective-permute-done.2.refs_0_), custom_call_target="tpu_custom_call" | custom-call | flops 1207959552 | bytes 5378048 | tf_op jit(solution)/shard_map/conv_late/pallas_call | solution.py:222
  10.2 0.0 collective-permute-done.4.other_out
  10.2 0.0 collective-permute-done.3.other_ref
  10.2 0.1 copy-done.7
  10.3 0.1 collective-permute-start.5
  10.4 13.7 %all_to_all.10 = bf16[16,16,256]{2,1,0:T(8,128)(2,1)S(1)} all-to-all(bf16[16,16,256]{2,1,0:T(8,128)(2,1)S(1)} %bitcast.11), channel_id=1, replica_groups={{0,1,4,5,8,9,12,13,16,17,20,21,24,25,28,29},{2,3,6,7,10,11,14,15,18,19,..., dimensions={0} | all-to-all | bytes 262144 | tf_op jit(solution)/shard_map/all_to_all | solution.py:244
  24.1 0.0 copy-done
  24.1 0.7 %temporal.1.refs_0_ = bf16[64,1024]{1,0:T(8,128)(2,1)S(1)} custom-call(bf16[8,2,16,256]{3,2,1,0:T(8,128)(2,1)S(1)} %bitcast.13, bf16[3,256,1024]{2,1,0:T(8,128)(2,1)S(1)} %copy-done, bf16[3,256,1024]{2,1,0:T(8,128)(2,1)S(1)} %collective-permute-done.3.other_ref), custom_call_target="tpu_custom_call" | custom-call | flops 201326592 | bytes 3407872 | tf_op jit(solution)/shard_map/temporal/pallas_call | solution.py:222
  24.7 0.0 copy-start.1
  24.8 0.0 copy-start.5
  24.8 0.0 collective-permute-done.5.other_ref
  24.8 1.2 %collective-permute-start.6 = (bf16[64,1024]{1,0:T(8,128)(2,1)S(1)}, bf16[64,1024]{1,0:T(8,128)(2,1)S(1)}, u32[]{:S(2)}, u32[]{:S(2)}) collective-permute-start(bf16[64,1024]{1,0:T(8,128)(2,1)S(1)} %temporal.1.refs_0_), channel_id=1, source_target_pairs={{0,2},{1,3},{2,0},{3,1},{4,6},{5,7},{6,4},{7,5},{8,10},{9,11},{10,... | collective-permute-start | bytes 393224 | tf_op jit(solution)/shard_map/ppermute | solution.py:241
  26.0 0.9 %turn.1.qkv_ref = bf16[2,1024,768]{2,1,0:T(8,128)(2,1)S(1)} custom-call(bf16[3,256,1024]{2,1,0:T(8,128)(2,1)S(1)} %copy-done.7, bf16[3,256,1024]{2,1,0:T(8,128)(2,1)S(1)} %collective-permute-done.5.other_ref), custom_call_target="tpu_custom_call" | custom-call | flops 6000000000 | bytes 6291456 | tf_op jit(solution)/shard_map/turn/pallas_call | solution.py:222
  26.8 3.0 %collective-permute-done.6.refs_1_ = bf16[64,1024]{1,0:T(8,128)(2,1)S(1)} collective-permute-done((bf16[64,1024]{1,0:T(8,128)(2,1)S(1)}, bf16[64,1024]{1,0:T(8,128)(2,1)S(1)}, u32[]{:S(2)}, u32[]{:S(2)}) %collective-permute-start.6) | collective-permute-done | bytes 131104 | tf_op jit(solution)/shard_map/ppermute | solution.py:241
  29.8 0.0 copy-done.1
  29.8 0.0 copy-done.5
  29.8 0.0 copy-start.3
  29.8 1.3 %attend.1 = bf16[256,256]{1,0:T(8,128)(2,1)S(1)} custom-call(f32[1,1024]{1,0:T(1,128)S(1)} %bitcast.21, bf16[2,1024,768]{2,1,0:T(8,128)(2,1)S(1)} %turn.1.qkv_ref, bf16[256,1024]{1,0:T(8,128)(2,1)S(1)} %copy-done.1, bf16[256,1024]{1,0:T(8,128)(2,1)S(1)} %collective-permute-done.4.other_out, bf16[64,1024]{1,0:T(8,128)(2,1)S(1)} %temporal.1.refs_0_, ...), custom_call_target="tpu_custom_call" | custom-call | flops 268435456 | bytes 4591616 | tf_op jit(solution)/shard_map/attend/pallas_call | solution.py:222
  31.1 10.5 %all_to_all.11 = bf16[32,8,256]{2,1,0:T(8,128)(2,1)S(1)} all-to-all(bf16[32,8,256]{2,1,0:T(8,128)(2,1)S(1)} %bitcast.14), channel_id=1, replica_groups=mesh['orbit'=8,'space'=4] {'orbit','space'}, dimensions={0} | all-to-all | bytes 262144 | tf_op jit(solution)/shard_map/all_to_all | solution.py:244
  41.6 0.0 copy-done.3
  41.6 0.8 %restore.1 = bf16[4,16,1024]{2,1,0:T(8,128)(2,1)} custom-call(bf16[256,256]{1,0:T(8,128)(2,1)S(1)} %bitcast.12, bf16[128,256]{1,0:T(8,128)(2,1)S(1)} %copy-done.3, bf16[4,16,1024]{2,1,0:T(8,128)(2,1)S(1)} %bitcast.18), custom_call_target="tpu_custom_call" | custom-call | bytes 458752 | tf_op jit(solution)/shard_map/restore/pallas_call | solution.py:222
Async XLA Ops:
  0.0 7.7 %copy-start.2 = (bf16[4,1,16,1024]{3,2,1,0:T(8,128)(2,1)S(1)}, bf16[4,1,16,1024]{3,2,1,0:T(8,128)(2,1)}, u32[]{:S(2)}) copy-start(bf16[4,1,16,1024]{3,2,1,0:T(8,128)(2,1)} %param.8) | copy-start | bytes 393220
  0.0 7.7 %copy-start.4 = (f32[1024]{0:T(1024)S(1)}, f32[1024]{0:T(1024)}, u32[]{:S(2)}) copy-start(f32[1024]{0:T(1024)} %param.9) | copy-start | bytes 12292
  0.0 7.1 %collective-permute-start = (bf16[64,1024]{1,0:T(8,128)(2,1)}, bf16[64,1024]{1,0:T(8,128)(2,1)S(1)}, u32[]{:S(2)}, u32[]{:S(2)}) collective-permute-start(bf16[64,1024]{1,0:T(8,128)(2,1)} %bitcast.15), channel_id=1, source_target_pairs={{0,2},{1,3},{2,0},{3,1},{4,6},{5,7},{6,4},{7,5},{8,10},{9,11},{10,... | collective-permute-start | bytes 393224 | tf_op jit(solution)/shard_map/ppermute | solution.py:241
  2.9 4.1 %collective-permute-start.1 = (bf16[64,1024]{1,0:T(8,128)(2,1)}, bf16[64,1024]{1,0:T(8,128)(2,1)S(1)}, u32[]{:S(2)}, u32[]{:S(2)}) collective-permute-start(bf16[64,1024]{1,0:T(8,128)(2,1)} %bitcast.16), channel_id=1, source_target_pairs={{0,1},{1,0},{2,3},{3,2},{4,5},{5,4},{6,7},{7,6},{8,9},{9,8},{10,11... | collective-permute-start | bytes 393224 | tf_op jit(solution)/shard_map/ppermute | solution.py:241
  2.9 7.2 %collective-permute-start.3 = (bf16[3,256,1024]{2,1,0:T(8,128)(2,1)}, bf16[3,256,1024]{2,1,0:T(8,128)(2,1)S(1)}, u32[]{:S(2)}, u32[]{:S(2)}) collective-permute-start(bf16[3,256,1024]{2,1,0:T(8,128)(2,1)} %own_ref.1), channel_id=1, source_target_pairs={{0,1},{1,0},{2,3},{3,2},{4,5},{5,4},{6,7},{7,6},{8,9},{9,8},{10,11... | collective-permute-start | bytes 4718600 | tf_op jit(solution)/shard_map/ppermute | solution.py:241
  3.5 6.7 %collective-permute-start.4 = (bf16[256,1024]{1,0:T(8,128)(2,1)}, bf16[256,1024]{1,0:T(8,128)(2,1)S(1)}, u32[]{:S(2)}, u32[]{:S(2)}) collective-permute-start(bf16[256,1024]{1,0:T(8,128)(2,1)} %own_out.1), channel_id=1, source_target_pairs={{0,1},{1,0},{2,3},{3,2},{4,5},{5,4},{6,7},{7,6},{8,9},{9,8},{10,11... | collective-permute-start | bytes 1572872 | tf_op jit(solution)/shard_map/ppermute | solution.py:241
  3.5 2.3 %copy-start.6 = (bf16[3,3,256,1024]{3,2,1,0:T(8,128)(2,1)S(1)}, bf16[3,3,256,1024]{3,2,1,0:T(8,128)(2,1)}, u32[]{:S(2)}) copy-start(bf16[3,3,256,1024]{3,2,1,0:T(8,128)(2,1)} %weight_ref.1) | copy-start | bytes 14155780
  7.1 1.8 %collective-permute-start.2 = (bf16[64,1024]{1,0:T(8,128)(2,1)S(1)}, bf16[64,1024]{1,0:T(8,128)(2,1)S(1)}, u32[]{:S(2)}, u32[]{:S(2)}) collective-permute-start(bf16[64,1024]{1,0:T(8,128)(2,1)S(1)} %collective-permute-done.refs_2_), channel_id=1, source_target_pairs={{0,1},{1,0},{2,3},{3,2},{4,5},{5,4},{6,7},{7,6},{8,9},{9,8},{10,11... | collective-permute-start | bytes 393224 | tf_op jit(solution)/shard_map/ppermute | solution.py:241
  8.9 1.4 %copy-start.7 = (bf16[3,256,1024]{2,1,0:T(8,128)(2,1)S(1)}, bf16[3,256,1024]{2,1,0:T(8,128)(2,1)}, u32[]{:S(2)}) copy-start(bf16[3,256,1024]{2,1,0:T(8,128)(2,1)} %own_ref.2) | copy-start | bytes 4718596
  8.9 15.2 %copy-start = (bf16[3,256,1024]{2,1,0:T(8,128)(2,1)S(1)}, bf16[3,256,1024]{2,1,0:T(8,128)(2,1)}, u32[]{:S(2)}) copy-start(bf16[3,256,1024]{2,1,0:T(8,128)(2,1)} %own_ref.1) | copy-start | bytes 4718596
  10.3 14.5 %collective-permute-start.5 = (bf16[3,256,1024]{2,1,0:T(8,128)(2,1)S(1)}, bf16[3,256,1024]{2,1,0:T(8,128)(2,1)S(1)}, u32[]{:S(2)}, u32[]{:S(2)}) collective-permute-start(bf16[3,256,1024]{2,1,0:T(8,128)(2,1)S(1)} %copy-done.7), channel_id=1, source_target_pairs={{0,1},{1,0},{2,3},{3,2},{4,5},{5,4},{6,7},{7,6},{8,9},{9,8},{10,11... | collective-permute-start | bytes 4718600 | tf_op jit(solution)/shard_map/ppermute | solution.py:241
  24.7 5.1 %copy-start.1 = (bf16[256,1024]{1,0:T(8,128)(2,1)S(1)}, bf16[256,1024]{1,0:T(8,128)(2,1)}, u32[]{:S(2)}) copy-start(bf16[256,1024]{1,0:T(8,128)(2,1)} %own_out.1) | copy-start | bytes 1572868
  24.8 5.1 %copy-start.5 = (f32[1024]{0:T(1024)S(1)}, f32[1024]{0:T(1024)}, u32[]{:S(2)}) copy-start(f32[1024]{0:T(1024)} %param.12) | copy-start | bytes 12292
  24.8 5.0 %collective-permute-start.6 = (bf16[64,1024]{1,0:T(8,128)(2,1)S(1)}, bf16[64,1024]{1,0:T(8,128)(2,1)S(1)}, u32[]{:S(2)}, u32[]{:S(2)}) collective-permute-start(bf16[64,1024]{1,0:T(8,128)(2,1)S(1)} %temporal.1.refs_0_), channel_id=1, source_target_pairs={{0,2},{1,3},{2,0},{3,1},{4,6},{5,7},{6,4},{7,5},{8,10},{9,11},{10,... | collective-permute-start | bytes 393224 | tf_op jit(solution)/shard_map/ppermute | solution.py:241
  29.8 11.8 %copy-start.3 = (bf16[128,256]{1,0:T(8,128)(2,1)S(1)}, bf16[128,256]{1,0:T(8,128)(2,1)}, u32[]{:S(2)}) copy-start(bf16[128,256]{1,0:T(8,128)(2,1)} %constant.2.clone.order_ref) | copy-start | bytes 196612
